TPU v7x, 512 devices: a whole 4x4x16 slice. The times are simulated.
512 devices in a mesh: grp: 16 (over x, z_hi), pose: 32 (over y, z_lo, core).
Axes of the slice: x: 4, y: 4, z: 16 (z_hi: 4, z_lo: 4; z = z_hi * 4 + z_lo), core: 2. Of those that a mesh axis runs over, the one named last changes fastest.
Arguments:
- images: bfloat16 [2, 4096, 4096], P(None, 'grp')
- projections: bfloat16 [2, 4096, 4096], P(None, 'pose', 'grp')
- defocus: float32 [4096], P('grp')
- inv_sigma2: float32 [4096], replicated, may hold values from 0.005 to 0.05
- log_prior: float32 [64], replicated, may hold values from -4 to 4
- row_class: int32 [4096], P('pose'), may hold values from 0 to 63
- pose_block: int32 [4096], P('pose'), may hold values from 0 to 255, as said below
- significant: int32 [4096, 256], P('grp'), may hold values from 0 to 1, as said below
Outputs:
- posteriors: float32 [4096, 4096], P('grp', 'pose')
- back_proj: float32 [3, 4096, 4096], P(None, 'pose', 'grp')
Inputs may be any that keep to these rules, and one draw needn't show every extreme that they name: `pose_block`: every block in 0 to 255 is the block of at least one row. Every particle has at least one significant block.
All inputs are finite; a program needn't handle non-finite values.
Results may differ from a plain program's by a relative error of at most 0.012.
Values may be sent and summed in bfloat16 or wider, within the bound.
No kernel may reach another device: no remote copies, remote signals or barrier semaphores. Data moves between devices by JAX's collectives and lax.ppermute only.
A program may use at most 128 MiB of HBM per device.

v0:
```python
import jax
import jax.numpy as jnp
from jax import lax
from jax.sharding import PartitionSpec as P

NEG_FILL = -1e30


def on_device(
    images, projections, defocus, inv_sigma2, log_prior, row_class, pose_block, significant
):
    width = images.shape[2]
    freq2 = (jnp.arange(width, dtype=jnp.float32) + 0.5) / width
    contrast = -jnp.sin(defocus[:, None] * freq2[None, :] + 0.1)
    weighted = (images.astype(jnp.float32) * (contrast * inv_sigma2[None, :])[None]).astype(
        jnp.bfloat16
    )
    contrast_noise = (contrast * contrast * inv_sigma2[None, :]).astype(jnp.bfloat16)
    piece = lax.all_gather(projections, "grp", axis=2, tiled=True)
    piece_f = piece.astype(jnp.float32)
    piece_power = (piece_f[0] * piece_f[0] + piece_f[1] * piece_f[1]).astype(jnp.bfloat16)
    cross = jnp.einsum("cik,crk->ir", weighted, piece, preferred_element_type=jnp.float32)
    power = jnp.einsum("ik,rk->ir", contrast_noise, piece_power, preferred_element_type=jnp.float32)
    raw_scores = cross - 0.5 * power
    class_match = row_class[:, None] == jnp.arange(log_prior.shape[0])[None, :]
    prior_rows = jnp.sum(jnp.where(class_match, log_prior[None, :], 0.0), axis=1)
    block_table = (pose_block[:, None] == jnp.arange(significant.shape[1])[None, :]).astype(
        jnp.bfloat16
    )
    hits = jnp.einsum(
        "ib,rb->ir",
        significant.astype(jnp.bfloat16),
        block_table,
        preferred_element_type=jnp.float32,
    )
    scores = jnp.where(hits > 0.5, raw_scores + prior_rows[None, :], jnp.float32(NEG_FILL))
    local_peak = jnp.max(scores, axis=1)
    peak = lax.pmax(local_peak, "pose")
    shifted = jnp.exp(scores - peak[:, None])
    total = lax.psum(jnp.sum(shifted, axis=1), "pose")
    posteriors = shifted / total[:, None]
    post_bf = posteriors.astype(jnp.bfloat16)
    contrast_images = images.astype(jnp.float32) * contrast[None]
    stacked = jnp.concatenate([contrast_images, (contrast * contrast)[None]], axis=0).astype(
        jnp.bfloat16
    )
    terms = jnp.einsum("ir,cik->crk", post_bf, stacked, preferred_element_type=jnp.float32)
    back_proj = lax.psum_scatter(
        terms.astype(jnp.bfloat16), "grp", scatter_dimension=2, tiled=True
    ).astype(jnp.float32)
    return (posteriors, back_proj)


def solution(mesh):
    placed = (
        P(None, "grp", None),
        P(None, "pose", "grp"),
        P("grp"),
        P(),
        P(),
        P("pose"),
        P("pose"),
        P("grp", None),
    )
    return jax.shard_map(
        on_device,
        mesh=mesh,
        in_specs=placed,
        out_specs=(P("grp", "pose"), P(None, "pose", "grp")),
        check_vma=False,
    )
```

profile of v0, /device:TPU:6, one launch (start us, length us, event | category | flops | bytes accessed | tf_op | source)
XLA Modules:
  0.0 423.9 jit_solution(4262544559158987689)
XLA Ops:
  7.2 0.0 all-gather.2.cloned.1.call-start
  7.2 0.7 all-gather.2.cloned.1.call-update
  8.0 0.0 reduce-scatter.2.cloned.1.call-start
  8.0 6.4 %copy.15 = bf16[2,256,4096]{1,2,0:T(8,128)(2,1)} copy(bf16[2,256,4096]{2,1,0:T(8,128)(2,1)} %param.8) | data formatting | bytes 8388608 | tf_op args[0]
  14.4 0.0 copy-done.6
  14.4 0.0 copy-done.7
  14.4 0.1 select_reduce_fusion
  14.5 0.2 fusion.26
  14.7 15.8 %multiply_convert_fusion = bf16[1,256,4096]{1,2,0:T(8,128)(2,1)S(1)} fusion(f32[4096]{0:T(1024)S(1)} %add_multiply_fusion, f32[256]{0:T(256)S(1)} %copy-done.4), kind=kLoop, calls=%fused_computation.11 | loop fusion | flops 4194304 | bytes 2114560 | tf_op jit(solution)/shard_map/convert.1
  30.5 16.4 %fusion.15 = (f32[256,4096]{0,1:T(8,128)S(1)}, f32[256,4096]{0,1:T(8,128)}) fusion(f32[4096]{0:T(1024)S(1)} %add_multiply_fusion, f32[256]{0:T(256)S(1)} %copy-done.4, f32[4096]{0:T(1024)S(1)} %copy-done.3), kind=kLoop, calls=%fused_computation.15 | loop fusion | flops 4194304 | bytes 8422400 | tf_op jit(solution)/shard_map/neg | solution.py:14
  46.9 2.9 fusion.1
  49.8 67.8 %all-gather.2.cloned.1.call-done = bf16[2,128,4096]{2,1,0:T(8,128)(2,1)} async-done(((bf16[2,128,256]{2,1,0:T(8,128)(2,1)}), bf16[2,128,4096]{2,1,0:T(8,128)(2,1)}) %all-gather.2.cloned.1.call-update) | async-done | bytes 2097168 | tf_op jit(solution)/shard_map/all_gather | solution.py:19
  117.6 2.2 convert_element_type.40
  119.8 0.6 copy-done.1
  120.4 0.7 copy-done.2
  121.1 3.2 fusion.19
  124.3 15.5 %fusion.37 = (f32[256]{0:T(256)S(1)}, f32[256,128]{0,1:T(8,128)S(1)}) fusion(pred[256,128]{0,1:T(32,128)(4,1)S(1)} %fusion.26, f32[128]{0:T(128)S(1)} %select_reduce_fusion, f32[256,128]{0,1:T(8,128)S(1)} %fusion.19, f32[4096]{0:T(1024)S(1)} %copy-done.3, f32[4096]{0:T(1024)S(1)} %add_multiply_fusion, f32[256]{0:T(256)S(1)} %copy-done.4, ...), kind=kOutput, calls=%fused_computation.43 | convolution fusion | flops 275939072 | bytes 4524544 | tf_op jit(solution)/shard_map/ik,rk->ir/dot_general | solution.py:23
  139.8 67.4 %pmax.7 = f32[256]{0:T(256)S(1)} all-reduce(f32[256]{0:T(256)S(1)} %get-tuple-element.8), channel_id=1, replica_groups=mesh['grp'=16,'pose'=32] {'pose'}, use_global_device_ids=true, to_apply=%region_2.3 | all-reduce | flops 256 | bytes 2048 | tf_op jit(solution)/shard_map/pmax | solution.py:38
  207.3 67.4 %psum.7 = f32[256]{0:T(256)S(1)} all-reduce(f32[256]{0:T(256)S(1)} %fusion.31), channel_id=1, replica_groups=mesh['grp'=16,'pose'=32] {'pose'}, use_global_device_ids=true, to_apply=%region_4.5 | all-reduce | flops 256 | bytes 2048 | tf_op jit(solution)/shard_map/psum | solution.py:40
  274.7 5.7 %fusion.9 = bf16[3,128,4096]{1,2,0:T(8,128)(2,1)} fusion(bf16[1,256,4096]{1,2,0:T(8,128)(2,1)S(1)} %multiply_convert_fusion, bf16[2,256,4096]{1,2,0:T(8,128)(2,1)} %fusion.1, f32[256,128]{0,1:T(8,128)S(1)} %fusion.30), kind=kOutput, calls=%fused_computation.9 | convolution fusion | flops 810057728 | bytes 9568256 | tf_op jit(solution)/shard_map/ir,cik->crk/dot_general | solution.py:47
  280.3 0.0 reduce-scatter.2.cloned.1.call-update
  280.3 0.8 copy.18
  281.1 134.2 %reduce-scatter.2.cloned.1.call-done = bf16[3,128,256]{1,2,0:T(8,128)(2,1)} async-done(((bf16[3,128,4096]{1,2,0:T(8,128)(2,1)}), bf16[3,128,256]{1,2,0:T(8,128)(2,1)}) %reduce-scatter.2.cloned.1.call-update) | async-done | bytes 196624 | tf_op jit(solution)/shard_map/reduce_scatter | solution.py:48
  415.3 1.8 copy.19
  (17 shorter events, 0.1 us)
Async XLA Ops:
  7.2 110.4 %all-gather.2.cloned.1.call-start = ((), (), s32[]{:S(2)}) async-start(), calls=%async_computation.1 | async-start | bytes 2228224 | tf_op jit(solution)/shard_map/all_gather | solution.py:19
  7.9 6.5 %copy-start.6 = (f32[64]{0:T(128)S(1)}, f32[64]{0:T(128)}, u32[]{:S(2)}) copy-start(f32[64]{0:T(128)} %param.12) | copy-start | bytes 772
  7.9 6.5 %copy-start.7 = (s32[128]{0:T(128)S(1)}, s32[128]{0:T(128)}, u32[]{:S(2)}) copy-start(s32[128]{0:T(128)} %param.13) | copy-start | bytes 1540
  7.9 6.6 %copy-start.5 = (s32[256,256]{1,0:T(8,128)S(1)}, s32[256,256]{1,0:T(8,128)}, u32[]{:S(2)}) copy-start(s32[256,256]{1,0:T(8,128)} %param.15) | copy-start | bytes 786436
  7.9 6.6 %copy-start.8 = (s32[128]{0:T(128)S(1)}, s32[128]{0:T(128)}, u32[]{:S(2)}) copy-start(s32[128]{0:T(128)} %param.14) | copy-start | bytes 1540
  7.9 6.8 %copy-start.4 = (f32[256]{0:T(256)S(1)}, f32[256]{0:T(256)}, u32[]{:S(2)}) copy-start(f32[256]{0:T(256)} %param.10) | copy-start | bytes 3076
  8.0 22.6 %copy-start.3 = (f32[4096]{0:T(1024)S(1)}, f32[4096]{0:T(1024)}, u32[]{:S(2)}) copy-start(f32[4096]{0:T(1024)} %param.11) | copy-start | bytes 49156
  8.0 407.3 %reduce-scatter.2.cloned.1.call-start = ((), (), s32[]{:S(2)}) async-start(), calls=%async_computation.2 | async-start | bytes 3342336 | tf_op jit(solution)/shard_map/reduce_scatter | solution.py:48
  30.5 16.4 %copy-start = (bf16[2,256,4096]{1,2,0:T(8,128)(2,1)S(1)}, bf16[2,256,4096]{1,2,0:T(8,128)(2,1)}, u32[]{:S(2)}) copy-start(bf16[2,256,4096]{1,2,0:T(8,128)(2,1)} %copy.15) | copy-start | bytes 12582916
  117.6 2.8 copy-start.1
  117.6 3.5 copy-start.2
Sparse Core Ops, SparseCore 0:
  11.0 106.5 all-gather.1
  280.5 134.7 reduce-scatter.1
where the time goes:
time: 425 us; the launch traced here: 424 us
  waiting for transfers between devices  203 us (48%)
  blocking collectives  135 us (32%)
  other arithmetic  37.4 us (9%)
  matrix products  24.6 us (6%)
  between operations  14.2 us (3%)
  local copies, waits for them, and re-layouts  10.2 us (2%)
    reduce_scatter x1, waiting for transfers between devices, on_device(): lax.psum_scatter(terms.astype(jnp.bfloat16), 'grp', scatter_dimension=2,...  134 us
    all_gather x1, waiting for transfers between devices, on_device(): piece = lax.all_gather(projections, 'grp', axis=2, tiled=True)  67.8 us
    pmax x1, blocking collectives, on_device(): peak = lax.pmax(local_peak, 'pose')  67.4 us
    psum x1, blocking collectives, on_device(): total = lax.psum(jnp.sum(shifted, axis=1), 'pose')  67.4 us
    another operation x2, other arithmetic  18.7 us
    neg x1, other arithmetic, on_device(): contrast = -jnp.sin(defocus[:, None] * freq2[None, :] + 0.1)  16.4 us
    dot_general x1, matrix products, on_device(): jnp.einsum('ik,rk->ir', contrast_noise, piece_power, preferred_element_ty...  15.5 us
    unnamed x21, local copies, waits for them, and re-layouts  10.2 us
  transfers between devices with their start and end apart: 2, of which 2 were waited for; matrix products, arithmetic and copies ran while one was open for 10% of the time, Pallas kernels for 0%

commit v1 on v0

v1 whole, which is shorter than its diff:
```python
import functools
import math

import jax
import jax.numpy as jnp
from jax import lax
from jax.experimental import pallas as pl
from jax.experimental.pallas import tpu as pltpu
from jax.sharding import PartitionSpec as P

NEG_FILL = -1e30
NX, NZH = 4, 4
NY, NZL, NC = 4, 4, 2
LANES = 128
TERM_ROWS = 16
VMEM_LIMIT = 20 << 20
MOST_VMEM = 63 << 20
SMALL_COST = pl.CostEstimate(flops=1, bytes_accessed=1, transcendentals=0)
INTERPRET = False


def grp_shift(dx):
    return [(x * NZH + z, ((x + dx) % NX) * NZH + z) for x in range(NX) for z in range(NZH)]


def pose_shift(dy, dz, dc):
    return [
        (
            (y * NZL + z) * NC + c,
            (((y + dy) % NY) * NZL + (z + dz) % NZL) * NC + (c + dc) % NC,
        )
        for y in range(NY)
        for z in range(NZL)
        for c in range(NC)
    ]


def share_pairs():
    n_pose = NY * NZL * NC
    pairs = []
    for x in range(NX):
        for zh in range(NZH):
            for y in range(NY):
                for zl in range(NZL):
                    for c in range(NC):
                        pose = (y * NZL + zl) * NC + c
                        src = x * NZH + zh
                        dst = ((x + y) % NX) * NZH + (zh + zl) % NZH
                        pairs.append((src * n_pose + pose, dst * n_pose + pose))
    return pairs


WEIGHT_ROWS = 32


def weight_kernel(images_ref, sin_ref, cos_ref, inv_ref, weighted_ref, noise_ref, token_ref):
    width = images_ref.shape[2]

    def body(i, _):
        rows = pl.ds(pl.multiple_of(i * WEIGHT_ROWS, WEIGHT_ROWS), WEIGHT_ROWS)
        sin_lo, cos_lo = sin_ref[rows, :LANES], cos_ref[rows, :LANES]
        sin_all, cos_all = sin_ref[rows, LANES:], cos_ref[rows, LANES:]
        for j in range(width // LANES):
            cols = slice(j * LANES, (j + 1) * LANES)
            contrast = -(sin_all[:, j : j + 1] * cos_lo + cos_all[:, j : j + 1] * sin_lo)
            scaled = contrast * inv_ref[:, cols]
            for c in range(2):
                image = images_ref[c, rows, cols].astype(jnp.float32)
                weighted_ref[c, rows, cols] = (image * scaled).astype(jnp.bfloat16)
            noise_ref[rows, cols] = (contrast * scaled).astype(jnp.bfloat16)
        return 0

    lax.fori_loop(0, images_ref.shape[1] // WEIGHT_ROWS, body, 0)
    token_ref[...] = jnp.zeros_like(token_ref)


def weight_images(images, defocus, inv_sigma2):
    _, n, width = images.shape
    low = jnp.arange(LANES, dtype=jnp.float32) / width
    high = (jnp.arange(LANES, dtype=jnp.float32) * LANES + 0.5) / width
    phase = jnp.concatenate(
        [defocus[:, None] * low[None, :], defocus[:, None] * high[None, :] + 0.1], axis=1
    )
    assert width <= LANES * LANES
    in_vmem = pl.BlockSpec(memory_space=pltpu.VMEM)
    return pl.pallas_call(
        weight_kernel,
        in_specs=[in_vmem] * 4,
        out_specs=[in_vmem] * 3,
        out_shape=[
            jax.ShapeDtypeStruct((2, n, width), jnp.bfloat16),
            jax.ShapeDtypeStruct((n, width), jnp.bfloat16),
            jax.ShapeDtypeStruct((8, LANES), jnp.float32),
        ],
        cost_estimate=SMALL_COST,
        compiler_params=pltpu.CompilerParams(vmem_limit_bytes=VMEM_LIMIT),
        interpret=INTERPRET,
        name="weight_images",
    )(images, jnp.sin(phase), jnp.cos(phase), inv_sigma2[None, :])


def dot_nt(a, b):
    return lax.dot_general(a, b, (((1,), (1,)), ((), ())), preferred_element_type=jnp.float32)


def score_kernel(
    proj_hbm, weighted_hbm, noise_hbm, bias_ref, _, scores_ref, log_sum_ref,
    proj_ref, weighted_ref, noise_ref, sems,
):
    n_x, n_z, _, _, slab = proj_ref.shape
    block = n_z * slab

    def copies(i):
        cols = slice(i * block, (i + 1) * block)
        return (
            pltpu.make_async_copy(proj_hbm.at[i], proj_ref.at[i], sems.at[0, i]),
            pltpu.make_async_copy(
                weighted_hbm.at[:, :, cols], weighted_ref.at[:, :, cols], sems.at[1, i]
            ),
            pltpu.make_async_copy(noise_hbm.at[:, cols], noise_ref.at[:, cols], sems.at[2, i]),
        )

    for i in range(n_x):
        for copy in copies(i):
            copy.start()
    total = jnp.zeros(scores_ref.shape, jnp.float32)
    half_power = jnp.zeros(scores_ref.shape, jnp.float32)
    for i in range(n_x):
        for copy in copies(i):
            copy.wait()
        for z in range(n_z):
            cols = slice(i * block + z * slab, i * block + (z + 1) * slab)
            real, imag = proj_ref[i, z, 0], proj_ref[i, z, 1]
            real_f, imag_f = real.astype(jnp.float32), imag.astype(jnp.float32)
            power = (real_f * real_f + imag_f * imag_f).astype(jnp.bfloat16)
            total += dot_nt(real, weighted_ref[0, :, cols])
            total += dot_nt(imag, weighted_ref[1, :, cols])
            half_power += dot_nt(power, noise_ref[:, cols])
    bias = bias_ref[...]
    scores = jnp.where(bias == NEG_FILL, bias, total - 0.5 * half_power + bias)
    scores_ref[...] = scores
    peak = jnp.max(scores, axis=0, keepdims=True)
    log_sum = peak + jnp.log(jnp.sum(jnp.exp(scores - peak), axis=0, keepdims=True))
    log_sum_ref[...] = jnp.broadcast_to(log_sum[None], log_sum_ref.shape)


def score(proj, weighted, noise, bias, token, copies):
    n_x, rows = proj.shape[0], proj.shape[3]
    n = weighted.shape[1]
    in_hbm, in_vmem = pl.BlockSpec(memory_space=pl.ANY), pl.BlockSpec(memory_space=pltpu.VMEM)
    return pl.pallas_call(
        score_kernel,
        in_specs=[in_hbm] * 3 + [in_vmem] * 2,
        out_specs=[pl.BlockSpec(), in_vmem],
        out_shape=[
            jax.ShapeDtypeStruct((rows, n), jnp.float32),
            jax.ShapeDtypeStruct((copies, 1, n), jnp.float32),
        ],
        scratch_shapes=[
            pltpu.VMEM(proj.shape, jnp.bfloat16),
            pltpu.VMEM(weighted.shape, jnp.bfloat16),
            pltpu.VMEM(noise.shape, jnp.bfloat16),
            pltpu.SemaphoreType.DMA((3, n_x)),
        ],
        cost_estimate=SMALL_COST,
        compiler_params=pltpu.CompilerParams(vmem_limit_bytes=MOST_VMEM),
        interpret=INTERPRET,
        name="score",
    )(proj, weighted, noise, bias, token)


def posterior_kernel(core_ref, scores_ref, log_sums_ref, post_ref, post_bf_ref):
    parts = log_sums_ref[...]
    peak = jnp.max(parts, axis=0)
    log_sum = peak + jnp.log(jnp.sum(jnp.exp(parts - peak[None]), axis=0))
    posteriors = jnp.exp(scores_ref[...] - log_sum)
    half = posteriors.shape[1] // NC
    swapped = jnp.concatenate([posteriors[:, half:], posteriors[:, :half]], axis=1)
    own_first = jnp.where(core_ref[0] == 0, posteriors, swapped).astype(jnp.bfloat16)
    post_bf_ref[...] = own_first
    post_ref[...] = posteriors.T


def posterior(core, scores, log_sums):
    rows, n = scores.shape
    return pl.pallas_call(
        posterior_kernel,
        in_specs=[
            pl.BlockSpec(memory_space=pltpu.SMEM),
            pl.BlockSpec(),
            pl.BlockSpec(memory_space=pltpu.VMEM),
        ],
        out_shape=[
            jax.ShapeDtypeStruct((n, rows), jnp.float32),
            jax.ShapeDtypeStruct((rows, n), jnp.bfloat16),
        ],
        cost_estimate=SMALL_COST,
        compiler_params=pltpu.CompilerParams(vmem_limit_bytes=VMEM_LIMIT),
        interpret=INTERPRET,
        name="posterior",
    )(core[None], scores, log_sums)


SIN_TERMS = tuple(
    (-1) ** n * (2 * math.pi) ** (2 * n + 1) / math.factorial(2 * n + 1) for n in range(7)
)


def squared_contrast(defocus, start, pixels, width):
    pixel = start + lax.broadcasted_iota(jnp.int32, (pixels, defocus.shape[1]), 0)
    freq2 = (pixel.astype(jnp.float32) + 0.5) * (1.0 / width)
    turns = (freq2 * defocus + 0.1) * (1.0 / math.pi)
    turns = 0.25 - jnp.abs(turns - jnp.round(turns))
    square = turns * turns
    value = jnp.full_like(square, SIN_TERMS[-1])
    for term in SIN_TERMS[-2::-1]:
        value = value * square + term
    return 0.5 - 0.5 * (value * turns)


def defocus_terms(defocus):
    scaled = defocus * (1.0 / 256.0)
    first = lax.reduce_precision(scaled, 8, 7)
    second = lax.reduce_precision(scaled - first, 8, 7)
    third = scaled - first - second
    return jnp.stack([first, second, third]).astype(jnp.bfloat16)


def back_kernel(sources, added, width, start_ref, *refs):
    n_s = len(sources)
    hbm, before_ref = refs[: n_s + 2], refs[n_s + 2] if added else None
    out_ref, post_ref, own_ref, other_ref, sems = refs[n_s + 2 + added :]
    slab = out_ref.shape[2]
    half = post_ref.shape[3] // NC

    def copies(i):
        pairs = [(src.at[sources[i]], dst.at[i]) for src, dst in zip(hbm[n_s:], (own_ref, other_ref))]
        pairs.append((hbm[i], post_ref.at[i]))
        return [
            pltpu.make_async_copy(src, dst, sems.at[i, j]) for j, (src, dst) in enumerate(pairs)
        ]

    for i in range(n_s):
        for copy in copies(i):
            copy.start()
    if added:
        sums = [before_ref[c] for c in range(3)]
    else:
        sums = [jnp.zeros(out_ref.shape[1:], jnp.float32) for _ in range(3)]
    for i in range(n_s):
        for copy in copies(i):
            copy.wait()
        for t in range(post_ref.shape[1]):
            for stack, at in ((own_ref, 0), (other_ref, half)):
                post = post_ref[i, t, :, at : at + half]
                for c in range(2):
                    image = stack[i, t, c * half : (c + 1) * half]
                    sums[c] += jnp.dot(post, image, preferred_element_type=jnp.float32)
                terms = stack[i, t, NC * half : NC * half + TERM_ROWS].astype(jnp.float32)
                defocus = (terms[0:1, :half] + terms[1:2, :half] + terms[2:3, :half]) * 256.0
                square = squared_contrast(defocus, start_ref[0], slab, width)
                sums[2] += dot_nt(post, square.astype(jnp.bfloat16))
    for c in range(3):
        out_ref[c] = sums[c]


def back_project(start, width, sources, posts, stacks, before=None):
    n_s, (n_z, rows, n) = len(sources), posts[0].shape
    slab = stacks[0].shape[3]
    in_hbm, in_vmem = pl.BlockSpec(memory_space=pl.ANY), pl.BlockSpec(memory_space=pltpu.VMEM)
    added = before is not None
    scratch = [pltpu.VMEM((n_s, n_z, rows, n), jnp.bfloat16)]
    scratch += [pltpu.VMEM((n_s,) + stack.shape[1:], jnp.bfloat16) for stack in stacks]
    return pl.pallas_call(
        functools.partial(back_kernel, sources, added, width),
        in_specs=[pl.BlockSpec(memory_space=pltpu.SMEM)]
        + [in_hbm] * (n_s + 2)
        + [in_vmem] * added,
        out_specs=in_vmem,
        out_shape=jax.ShapeDtypeStruct((3, rows, slab), jnp.float32),
        scratch_shapes=scratch + [pltpu.SemaphoreType.DMA((n_s, 3))],
        cost_estimate=SMALL_COST,
        compiler_params=pltpu.CompilerParams(vmem_limit_bytes=MOST_VMEM),
        interpret=INTERPRET,
        name="back_project",
    )(start[None], *posts, *stacks, *([before] if added else []))


def exchange(copies, axis, groups=None):
    return lax.all_to_all(copies, axis, 0, 0, axis_index_groups=groups)


def copies_of(value, size):
    return jnp.broadcast_to(value[None], (size,) + value.shape)


def on_device(
    images, projections, defocus, inv_sigma2, log_prior, row_class, pose_block, significant
):
    _, n, width = images.shape
    _, rows, slab = projections.shape
    half = n // NC
    group, pose = lax.axis_index("grp"), lax.axis_index("pose")
    x, zh = group >> 2, group & 3
    y, zl, core = pose >> 3, (pose >> 1) & 3, pose & 1

    z_groups = [[a * NZH + b for b in range(NZH)] for a in range(NX)]
    x_groups = [[a * NZH + b for a in range(NX)] for b in range(NZH)]
    y_groups = [
        [(a * NZL + b) * NC + c for a in range(NY)] for b in range(NZL) for c in range(NC)
    ]
    with jax.named_scope("gather_projections"):
        proj_z = lax.all_gather(projections, "grp", axis=0, axis_index_groups=z_groups)
        proj_z, defocus = lax.optimization_barrier((proj_z, defocus))
        proj = lax.all_gather(proj_z, "grp", axis=0, axis_index_groups=x_groups)

    with jax.named_scope("exchange_images"):
        target = (((x + y) & 3) << 2) + ((zh + zl) & 3)
        part = lax.dynamic_slice(images, (0, core * half, target * slab), (2, half, slab))
        part_defocus = lax.dynamic_slice(defocus, (core * half,), (half,))
        pixel = (target * slab + jnp.arange(slab)).astype(jnp.float32)
        contrast = -jnp.sin(part_defocus[:, None] * ((pixel + 0.5) / width)[None, :] + 0.1)
        part = (part.astype(jnp.float32) * contrast[None]).astype(jnp.bfloat16)
        terms = jnp.pad(defocus_terms(part_defocus), ((0, TERM_ROWS - 3), (0, slab - half)))
        share = jnp.concatenate([part.reshape(2 * half, slab), terms], axis=0)
        share = lax.ppermute(share, ("grp", "pose"), share_pairs())

    with jax.named_scope("weights"):
        weighted, noise, token = weight_images(images, defocus, inv_sigma2)
        class_match = row_class[:, None] == jnp.arange(log_prior.shape[0])[None, :]
        prior_rows = jnp.sum(jnp.where(class_match, log_prior[None, :], 0.0), axis=1)
        block_table = pose_block[:, None] == jnp.arange(significant.shape[1])[None, :]
        hits = jnp.einsum(
            "rb,ib->ri",
            block_table.astype(jnp.bfloat16),
            significant.astype(jnp.bfloat16),
            preferred_element_type=jnp.float32,
        )
        bias = jnp.where(hits > 0.5, prior_rows[:, None], jnp.float32(NEG_FILL))

    with jax.named_scope("gather_images"):
        share, token, bias = lax.optimization_barrier((share, token, bias))
        turned = copies_of(share, NZL)
        for d in (1, 2, 3):
            block = lax.ppermute(share, "pose", pose_shift(0, d, 0))
            turned = lax.dynamic_update_slice_in_dim(turned, block[None], (zh - zl + d) & 3, 0)
        turned, proj = lax.optimization_barrier((turned, proj))
        own = lax.all_gather(turned, "pose", axis=0, axis_index_groups=y_groups)

    with jax.named_scope("scores"):
        scores, log_sum = score(proj, weighted, noise, bias, token, NY * NZL * NC)

    with jax.named_scope("softmax"):
        posteriors, post_bf = posterior(core, scores, exchange(log_sum, "pose"))

    with jax.named_scope("gather_posteriors"):
        post = [lax.all_gather(post_bf, "grp", axis=0, axis_index_groups=z_groups)] + [None] * 3
        for d in (2, 1, 3):
            post[d] = lax.ppermute(post[0], "grp", grp_shift(d))
        post[0], own = lax.optimization_barrier((post[0], own))
        other = lax.ppermute(own, "pose", pose_shift(0, 0, 1))

    with jax.named_scope("back_project"):
        start, stacks = group * slab, (own, other)
        back_proj = back_project(start, width, (0, 1), post[:2], stacks)
        back_proj = back_project(start, width, (3, 2), (post[3], post[2]), stacks, back_proj)
    return (posteriors, back_proj)


def solution(mesh):
    placed = (
        P(None, "grp", None),
        P(None, "pose", "grp"),
        P("grp"),
        P(),
        P(),
        P("pose"),
        P("pose"),
        P("grp", None),
    )
    return jax.shard_map(
        on_device,
        mesh=mesh,
        in_specs=placed,
        out_specs=(P("grp", "pose"), P(None, "pose", "grp")),
        check_vma=False,
    )
```

time: 425 us -> 159 us (0.37)
  waiting for transfers between devices: 203 us -> 9.36 us
  blocking collectives: 135 us -> 72.8 us
  other arithmetic: 37.4 us -> 4.11 us
  starting transfers between devices: 0.08 us -> 28.2 us
  matrix products: 24.6 us -> 0.87 us
  Pallas kernels: 0 us -> 19.3 us
    reduce_scatter x1 -> x0, waiting for transfers between devices: 134 us -> none  [on_device(): lax.psum_scatter(terms.astype(jnp.bfloat16), 'grp', scatter_dimension=2,...]
    all_gather x1 -> x2, waiting for transfers between devices: 67.8 us -> 0.32 us  [the longest x1 0.32 us: on_device(): proj = lax.all_gather(proj_z, 'grp', axis=0, axis_index_groups=x_groups)]
    pmax x1 -> x0, blocking collectives: 67.4 us -> none  [on_device(): peak = lax.pmax(local_peak, 'pose')]
    psum x1 -> x0, blocking collectives: 67.4 us -> none  [on_device(): total = lax.psum(jnp.sum(shifted, axis=1), 'pose')]
    all_gather x0 -> x2, blocking collectives: none -> 55.6 us  [the longest x1 35.2 us: on_device(): lax.all_gather(projections, 'grp', axis=0, axis_index_groups=z_groups)]
    ppermute x0 -> x8, starting transfers between devices: none -> 28.1 us  [the longest x3 15.4 us: on_device(): block = lax.ppermute(share, 'pose', pose_shift(0, d, 0))]
    dot_general x4 -> x1, matrix products: 24.6 us -> 0.87 us  [on_device(): jnp.einsum('rb,ib->ri', block_table.astype(jnp.bfloat16), significant.ast...]
    pallas_call x0 -> x5, Pallas kernels: none -> 19.3 us  [the longest x2 9.23 us: back_project(): pl.pallas_call(functools.partial(back_kernel, sources, added, width), in_...]
  transfers between devices with their start and end apart: 2 -> 10, of which waited for: 2 -> 5; matrix products, arithmetic and copies ran while one was open for 10% -> 3% of each run, Pallas kernels for 0% -> 9%
where the time goes in v1:
time: 159 us
  blocking collectives  72.8 us (46%)
  starting transfers between devices  28.2 us (18%)
  Pallas kernels  19.3 us (12%)
  between operations  14.3 us (9%)
  local copies, waits for them, and re-layouts  9.67 us (6%)
  waiting for transfers between devices  9.36 us (6%)
  other arithmetic  4.11 us (3%)
    all_gather x1, blocking collectives, on_device(): lax.all_gather(projections, 'grp', axis=0, axis_index_groups=z_groups)  35.2 us
    all_gather x1, blocking collectives, on_device(): lax.all_gather(post_bf, 'grp', axis=0, axis_index_groups=z_groups)  20.4 us
    all_to_all x1, blocking collectives, exchange(): return lax.all_to_all(copies, axis, 0, 0, axis_index_groups=groups)  17.2 us
    ppermute x3, starting transfers between devices, on_device(): block = lax.ppermute(share, 'pose', pose_shift(0, d, 0))  15.4 us
    ppermute x3, starting transfers between devices, on_device(): post[d] = lax.ppermute(post[0], 'grp', grp_shift(d))  10.1 us
    unnamed x30, local copies, waits for them, and re-layouts  9.59 us
    pallas_call x2, Pallas kernels, back_project(): pl.pallas_call(functools.partial(back_kernel, sources, added, width), in_...  9.23 us
    ppermute x3, waiting for transfers between devices, on_device(): post[d] = lax.ppermute(post[0], 'grp', grp_shift(d))  6.52 us
  transfers between devices with their start and end apart: 10, of which 5 were waited for; matrix products, arithmetic and copies ran while one was open for 3% of the time, Pallas kernels for 9%

profile of v1, /device:TPU:6, one launch (start us, length us, event | category | flops | bytes accessed | tf_op | source)
XLA Modules:
  0.0 158.5 jit_solution(12607909808459129531)
XLA Ops:
  7.2 35.2 %all-gather = bf16[8,128,256]{2,1,0:T(8,128)(2,1)} all-gather(bf16[2,128,256]{2,1,0:T(8,128)(2,1)} %param.9), channel_id=2, replica_groups={{0,32,64,96},{128,160,192,224},{256,288,320,352},{384,416,448,480},{1,3..., dimensions={0}, use_global_device_ids=true | all-gather | bytes 655360 | tf_op jit(solution)/shard_map/gather_projections/all_gather | solution.py:313
  43.8 0.9 multiply_convert_fusion
  46.3 1.0 fusion.1
  47.3 2.2 %copy-done = bf16[2,256,4096]{2,1,0:T(8,128)(2,1)S(1)} copy-done((bf16[2,256,4096]{2,1,0:T(8,128)(2,1)S(1)}, bf16[2,256,4096]{2,1,0:T(8,128)(2,1)}, u32[]{:S(2)}) %copy-start) | copy-done | bytes 4194328
  49.5 3.2 %weight_images.1 = (bf16[2,256,4096]{2,1,0:T(8,128)(2,1)S(1)}, bf16[256,4096]{1,0:T(8,128)(2,1)S(1)}, f32[8,128]{1,0:T(8,128)S(1)}) custom-call(bf16[2,256,4096]{2,1,0:T(8,128)(2,1)S(1)} %copy-done, f32[256,256]{1,0:T(8,128)S(1)} %get-tuple-element.37.sin_ref, f32[256,256]{1,0:T(8,128)S(1)} %get-tuple-element.36.cos_ref, f32[1,4096]{1,0:T(1,128)S(1)} %bitcast.20), custom_call_target="tpu_custom_call" | custom-call | flops 1 | bytes 1 | tf_op jit(solution)/shard_map/weights/weight_images/pallas_call | solution.py:86
  52.7 1.9 %copy-done.1 = bf16[2,256,4096]{2,1,0:T(8,128)(2,1)} copy-done((bf16[2,256,4096]{2,1,0:T(8,128)(2,1)}, bf16[2,256,4096]{2,1,0:T(8,128)(2,1)S(1)}, u32[]{:S(2)}) %copy-start.1) | copy-done | bytes 4194328
  54.6 1.4 copy-done.2
  56.7 0.9 fusion.bias_ref
  57.5 6.1 %collective-permute-start.1 = (bf16[272,256]{1,0:T(8,128)(2,1)S(1)}, bf16[272,256]{1,0:T(8,128)(2,1)S(1)}, u32[]{:S(2)}, u32[]{:S(2)}) collective-permute-start(bf16[272,256]{1,0:T(8,128)(2,1)S(1)} %collective-permute-done), channel_id=1, source_target_pairs={{0,2},{1,3},{2,4},{3,5},{4,6},{5,7},{6,0},{7,1},{8,10},{9,11},{10,... | collective-permute-start | bytes 417800 | tf_op jit(solution)/shard_map/gather_images/ppermute | solution.py:345
  63.6 4.5 %collective-permute-start.2 = (bf16[272,256]{1,0:T(8,128)(2,1)S(1)}, bf16[272,256]{1,0:T(8,128)(2,1)S(1)}, u32[]{:S(2)}, u32[]{:S(2)}) collective-permute-start(bf16[272,256]{1,0:T(8,128)(2,1)S(1)} %collective-permute-done), channel_id=1, source_target_pairs={{0,4},{1,5},{2,6},{3,7},{4,0},{5,1},{6,2},{7,3},{8,12},{9,13},{10,... | collective-permute-start | bytes 417800 | tf_op jit(solution)/shard_map/gather_images/ppermute | solution.py:345
  68.2 4.8 %collective-permute-start.3 = (bf16[272,256]{1,0:T(8,128)(2,1)S(1)}, bf16[272,256]{1,0:T(8,128)(2,1)S(1)}, u32[]{:S(2)}, u32[]{:S(2)}) collective-permute-start(bf16[272,256]{1,0:T(8,128)(2,1)S(1)} %collective-permute-done), channel_id=1, source_target_pairs={{0,6},{1,7},{2,0},{3,1},{4,2},{5,3},{6,4},{7,5},{8,14},{9,15},{10,... | collective-permute-start | bytes 417800 | tf_op jit(solution)/shard_map/gather_images/ppermute | solution.py:345
  73.1 1.5 collective-permute-done.2
  74.6 1.0 collective-permute-done.3
  76.4 6.0 %score.1 = (f32[128,256]{1,0:T(8,128)}, f32[32,1,256]{2,1,0:T(1,128)}) custom-call(bf16[4,4,2,128,256]{4,3,2,1,0:T(8,128)(2,1)} %bitcast.25, bf16[2,256,4096]{2,1,0:T(8,128)(2,1)} %copy-done.1, bf16[256,4096]{1,0:T(8,128)(2,1)} %copy-done.2, f32[128,256]{1,0:T(8,128)} %fusion.bias_ref, f32[8,128]{1,0:T(8,128)} %copy-done.5), custom_call_target="tpu_custom_call" | custom-call | flops 1 | bytes 1 | tf_op jit(solution)/shard_map/scores/score/pallas_call | solution.py:151
  82.4 17.2 %all_to_all.5.log_sums_ref = f32[32,1,256]{2,1,0:T(1,128)S(1)} all-to-all(f32[32,1,256]{2,1,0:T(1,128)} %get-tuple-element.28), channel_id=1, replica_groups=mesh['grp'=16,'pose'=32] {'pose'}, dimensions={0} | all-to-all | bytes 65536 | tf_op jit(solution)/shard_map/softmax/all_to_all | solution.py:290
  99.7 0.9 copy-done.3
  101.4 20.4 %all-gather.2 = bf16[512,256]{1,0:T(8,128)(2,1)S(1)} all-gather(bf16[128,256]{1,0:T(8,128)(2,1)S(1)} %get-tuple-element.30), channel_id=4, replica_groups={{0,32,64,96},{128,160,192,224},{256,288,320,352},{384,416,448,480},{1,3..., dimensions={0}, use_global_device_ids=true | all-gather | bytes 327680 | tf_op jit(solution)/shard_map/gather_posteriors/all_gather | solution.py:357
  121.8 1.9 %collective-permute-start.6 = (bf16[4,4,272,256]{3,2,1,0:T(8,128)(2,1)}, bf16[4,4,272,256]{3,2,1,0:T(8,128)(2,1)}, u32[]{:S(2)}, u32[]{:S(2)}) collective-permute-start(bf16[4,4,272,256]{3,2,1,0:T(8,128)(2,1)} %bitcast.21), channel_id=1, source_target_pairs={{0,1},{1,0},{2,3},{3,2},{4,5},{5,4},{6,7},{7,6},{8,9},{9,8},{10,11... | collective-permute-start | bytes 6684680 | tf_op jit(solution)/shard_map/gather_posteriors/ppermute | solution.py:361
  123.7 4.3 %collective-permute-start.7 = (bf16[4,128,256]{2,1,0:T(8,128)(2,1)S(1)}, bf16[4,128,256]{2,1,0:T(8,128)(2,1)S(1)}, u32[]{:S(2)}, u32[]{:S(2)}) collective-permute-start(bf16[4,128,256]{2,1,0:T(8,128)(2,1)S(1)} %bitcast.26), channel_id=1, source_target_pairs={{0,128},{32,160},{64,192},{96,224},{128,256},{160,288},{192,320},{... | collective-permute-start | bytes 786440 | tf_op jit(solution)/shard_map/gather_posteriors/ppermute | solution.py:359
  128.0 1.9 %collective-permute-start.4 = (bf16[4,128,256]{2,1,0:T(8,128)(2,1)S(1)}, bf16[4,128,256]{2,1,0:T(8,128)(2,1)S(1)}, u32[]{:S(2)}, u32[]{:S(2)}) collective-permute-start(bf16[4,128,256]{2,1,0:T(8,128)(2,1)S(1)} %bitcast.27), channel_id=1, source_target_pairs={{0,384},{32,416},{64,448},{96,480},{128,0},{160,32},{192,64},{224,... | collective-permute-start | bytes 786440 | tf_op jit(solution)/shard_map/gather_posteriors/ppermute | solution.py:359
  129.9 3.9 %collective-permute-start.5 = (bf16[4,128,256]{2,1,0:T(8,128)(2,1)S(1)}, bf16[4,128,256]{2,1,0:T(8,128)(2,1)S(1)}, u32[]{:S(2)}, u32[]{:S(2)}) collective-permute-start(bf16[4,128,256]{2,1,0:T(8,128)(2,1)S(1)} %bitcast.28), channel_id=1, source_target_pairs={{0,256},{32,288},{64,320},{96,352},{128,384},{160,416},{192,448},{... | collective-permute-start | bytes 786440 | tf_op jit(solution)/shard_map/gather_posteriors/ppermute | solution.py:359
  135.0 4.1 %back_project.2.refs_4_ = f32[3,128,256]{2,1,0:T(8,128)} custom-call(s32[1]{0:T(128)} %bitcast.11.start_ref, bf16[4,128,256]{2,1,0:T(8,128)(2,1)} %bitcast.29, bf16[4,128,256]{2,1,0:T(8,128)(2,1)} %copy-done.10, bf16[4,4,272,256]{3,2,1,0:T(8,128)(2,1)} %bitcast.22, bf16[4,4,272,256]{3,2,1,0:T(8,128)(2,1)} %collective-permute-done.6.refs_3_), custom_call_target="tpu_custom_call" | custom-call | flops 1 | bytes 1 | tf_op jit(solution)/shard_map/back_project/back_project/pallas_call | solution.py:274
  139.1 6.0 %collective-permute-done.4.refs_0_ = bf16[4,128,256]{2,1,0:T(8,128)(2,1)S(1)} collective-permute-done((bf16[4,128,256]{2,1,0:T(8,128)(2,1)S(1)}, bf16[4,128,256]{2,1,0:T(8,128)(2,1)S(1)}, u32[]{:S(2)}, u32[]{:S(2)}) %collective-permute-start.4) | collective-permute-done | bytes 262176 | tf_op jit(solution)/shard_map/gather_posteriors/ppermute | solution.py:359
  146.6 5.1 %back_project.3 = f32[3,128,256]{2,1,0:T(8,128)} custom-call(s32[1]{0:T(128)} %bitcast.11.start_ref, bf16[4,128,256]{2,1,0:T(8,128)(2,1)} %copy-done.8, bf16[4,128,256]{2,1,0:T(8,128)(2,1)} %copy-done.9, bf16[4,4,272,256]{3,2,1,0:T(8,128)(2,1)} %bitcast.23, bf16[4,4,272,256]{3,2,1,0:T(8,128)(2,1)} %collective-permute-done.6.refs_3_, ...), custom_call_target="tpu_custom_call" | custom-call | flops 1 | bytes 1 | tf_op jit(solution)/shard_map/back_project/back_project/pallas_call | solution.py:274
  (52 shorter events, 7.9 us)
Async XLA Ops:
  7.2 40.1 %copy-start.4 = (f32[4096]{0:T(1024)S(1)}, f32[4096]{0:T(1024)}, u32[]{:S(2)}) copy-start(f32[4096]{0:T(1024)} %param.11) | copy-start | bytes 49156
  7.2 68.7 %all-gather.7.cloned.1.call-start = ((), (), s32[]{:S(2)}) async-start(), calls=%async_computation.1 | async-start | bytes 2621440 | tf_op jit(solution)/shard_map/gather_projections/all_gather | solution.py:315
  42.5 79.3 %all-gather.9.cloned.1.call-start = ((), (), s32[]{:S(2)}) async-start(), calls=%async_computation.2 | async-start | bytes 2785280 | tf_op jit(solution)/shard_map/gather_images/all_gather | solution.py:348
  44.8 12.7 %collective-permute-start = (bf16[272,256]{1,0:T(8,128)(2,1)S(1)}, bf16[272,256]{1,0:T(8,128)(2,1)S(1)}, u32[]{:S(2)}, u32[]{:S(2)}) collective-permute-start(bf16[272,256]{1,0:T(8,128)(2,1)S(1)} %pad_maximum_fusion.1), channel_id=1, source_target_pairs={{0,0},{1,1},{2,34},{3,35},{4,68},{5,69},{6,102},{7,103},{8,136},{9... | collective-permute-start | bytes 417800 | tf_op jit(solution)/shard_map/exchange_images/ppermute | solution.py:326
  47.3 2.2 %copy-start = (bf16[2,256,4096]{2,1,0:T(8,128)(2,1)S(1)}, bf16[2,256,4096]{2,1,0:T(8,128)(2,1)}, u32[]{:S(2)}) copy-start(bf16[2,256,4096]{2,1,0:T(8,128)(2,1)} %images_ref.1) | copy-start | bytes 12582916
  49.5 7.1 %copy-start.13 = (f32[64]{0:T(128)S(1)}, f32[64]{0:T(128)}, u32[]{:S(2)}) copy-start(f32[64]{0:T(128)} %param.12) | copy-start | bytes 772
  49.5 7.1 %copy-start.14 = (s32[128]{0:T(128)S(1)}, s32[128]{0:T(128)}, u32[]{:S(2)}) copy-start(s32[128]{0:T(128)} %param.13) | copy-start | bytes 1540
  49.5 7.2 %copy-start.11 = (s32[256,256]{1,0:T(8,128)S(1)}, s32[256,256]{1,0:T(8,128)}, u32[]{:S(2)}) copy-start(s32[256,256]{1,0:T(8,128)} %param.15) | copy-start | bytes 786436
  49.5 7.2 %copy-start.12 = (s32[128]{0:T(128)S(1)}, s32[128]{0:T(128)}, u32[]{:S(2)}) copy-start(s32[128]{0:T(128)} %param.14) | copy-start | bytes 1540
  52.6 2.0 %copy-start.1 = (bf16[2,256,4096]{2,1,0:T(8,128)(2,1)}, bf16[2,256,4096]{2,1,0:T(8,128)(2,1)S(1)}, u32[]{:S(2)}) copy-start(bf16[2,256,4096]{2,1,0:T(8,128)(2,1)S(1)} %get-tuple-element.23.weighted_hbm) | copy-start | bytes 12582916
  54.6 1.4 copy-start.2
  57.5 15.5 %collective-permute-start.1 = (bf16[272,256]{1,0:T(8,128)(2,1)S(1)}, bf16[272,256]{1,0:T(8,128)(2,1)S(1)}, u32[]{:S(2)}, u32[]{:S(2)}) collective-permute-start(bf16[272,256]{1,0:T(8,128)(2,1)S(1)} %collective-permute-done), channel_id=1, source_target_pairs={{0,2},{1,3},{2,4},{3,5},{4,6},{5,7},{6,0},{7,1},{8,10},{9,11},{10,... | collective-permute-start | bytes 417800 | tf_op jit(solution)/shard_map/gather_images/ppermute | solution.py:345
  63.6 11.0 %collective-permute-start.2 = (bf16[272,256]{1,0:T(8,128)(2,1)S(1)}, bf16[272,256]{1,0:T(8,128)(2,1)S(1)}, u32[]{:S(2)}, u32[]{:S(2)}) collective-permute-start(bf16[272,256]{1,0:T(8,128)(2,1)S(1)} %collective-permute-done), channel_id=1, source_target_pairs={{0,4},{1,5},{2,6},{3,7},{4,0},{5,1},{6,2},{7,3},{8,12},{9,13},{10,... | collective-permute-start | bytes 417800 | tf_op jit(solution)/shard_map/gather_images/ppermute | solution.py:345
  68.2 7.4 %collective-permute-start.3 = (bf16[272,256]{1,0:T(8,128)(2,1)S(1)}, bf16[272,256]{1,0:T(8,128)(2,1)S(1)}, u32[]{:S(2)}, u32[]{:S(2)}) collective-permute-start(bf16[272,256]{1,0:T(8,128)(2,1)S(1)} %collective-permute-done), channel_id=1, source_target_pairs={{0,6},{1,7},{2,0},{3,1},{4,2},{5,3},{6,4},{7,5},{8,14},{9,15},{10,... | collective-permute-start | bytes 417800 | tf_op jit(solution)/shard_map/gather_images/ppermute | solution.py:345
  75.6 0.8 copy-start.6
  99.7 0.9 copy-start.3
  121.8 13.2 %copy-start.7 = (bf16[512,256]{1,0:T(8,128)(2,1)}, bf16[512,256]{1,0:T(8,128)(2,1)S(1)}, u32[]{:S(2)}) copy-start(bf16[512,256]{1,0:T(8,128)(2,1)S(1)} %all-gather.2) | copy-start | bytes 786436
  121.8 13.2 %collective-permute-start.6 = (bf16[4,4,272,256]{3,2,1,0:T(8,128)(2,1)}, bf16[4,4,272,256]{3,2,1,0:T(8,128)(2,1)}, u32[]{:S(2)}, u32[]{:S(2)}) collective-permute-start(bf16[4,4,272,256]{3,2,1,0:T(8,128)(2,1)} %bitcast.21), channel_id=1, source_target_pairs={{0,1},{1,0},{2,3},{3,2},{4,5},{5,4},{6,7},{7,6},{8,9},{9,8},{10,11... | collective-permute-start | bytes 6684680 | tf_op jit(solution)/shard_map/gather_posteriors/ppermute | solution.py:361
  123.7 10.6 %collective-permute-start.7 = (bf16[4,128,256]{2,1,0:T(8,128)(2,1)S(1)}, bf16[4,128,256]{2,1,0:T(8,128)(2,1)S(1)}, u32[]{:S(2)}, u32[]{:S(2)}) collective-permute-start(bf16[4,128,256]{2,1,0:T(8,128)(2,1)S(1)} %bitcast.26), channel_id=1, source_target_pairs={{0,128},{32,160},{64,192},{96,224},{128,256},{160,288},{192,320},{... | collective-permute-start | bytes 786440 | tf_op jit(solution)/shard_map/gather_posteriors/ppermute | solution.py:359
  128.0 17.2 %collective-permute-start.4 = (bf16[4,128,256]{2,1,0:T(8,128)(2,1)S(1)}, bf16[4,128,256]{2,1,0:T(8,128)(2,1)S(1)}, u32[]{:S(2)}, u32[]{:S(2)}) collective-permute-start(bf16[4,128,256]{2,1,0:T(8,128)(2,1)S(1)} %bitcast.27), channel_id=1, source_target_pairs={{0,384},{32,416},{64,448},{96,480},{128,0},{160,32},{192,64},{224,... | collective-permute-start | bytes 786440 | tf_op jit(solution)/shard_map/gather_posteriors/ppermute | solution.py:359
  129.9 15.2 %collective-permute-start.5 = (bf16[4,128,256]{2,1,0:T(8,128)(2,1)S(1)}, bf16[4,128,256]{2,1,0:T(8,128)(2,1)S(1)}, u32[]{:S(2)}, u32[]{:S(2)}) collective-permute-start(bf16[4,128,256]{2,1,0:T(8,128)(2,1)S(1)} %bitcast.28), channel_id=1, source_target_pairs={{0,256},{32,288},{64,320},{96,352},{128,384},{160,416},{192,448},{... | collective-permute-start | bytes 786440 | tf_op jit(solution)/shard_map/gather_posteriors/ppermute | solution.py:359
  134.3 0.7 copy-start.10
  145.2 0.7 copy-start.8
  145.9 0.7 copy-start.9
  (1 other events, 0.6 us)
Sparse Core Ops, SparseCore 0:
  42.6 33.2 all-gather.6
  78.0 41.5 all-gather.8

commit v2 on v1

v2 whole, which is shorter than its diff:
```python
import functools
import math

import jax
import jax.numpy as jnp
from jax import lax
from jax.experimental import pallas as pl
from jax.experimental.pallas import tpu as pltpu
from jax.sharding import PartitionSpec as P

NEG_FILL = -1e30
NX, NZH = 4, 4
NY, NZL, NC = 4, 4, 2
LANES = 128
TERM_ROWS = 16
VMEM_LIMIT = 20 << 20
MOST_VMEM = 63 << 20
BACK_VMEM = 52 << 20
SMALL_COST = pl.CostEstimate(flops=1, bytes_accessed=1, transcendentals=0)
INTERPRET = False


def grp_shift(dx):
    return [(x * NZH + z, ((x + dx) % NX) * NZH + z) for x in range(NX) for z in range(NZH)]


def pose_shift(dy, dz, dc):
    return [
        (
            (y * NZL + z) * NC + c,
            (((y + dy) % NY) * NZL + (z + dz) % NZL) * NC + (c + dc) % NC,
        )
        for y in range(NY)
        for z in range(NZL)
        for c in range(NC)
    ]


def share_pairs():
    n_pose = NY * NZL * NC
    pairs = []
    for x in range(NX):
        for zh in range(NZH):
            for y in range(NY):
                for zl in range(NZL):
                    for c in range(NC):
                        pose = (y * NZL + zl) * NC + c
                        src = x * NZH + zh
                        dst = ((x + y) % NX) * NZH + (zh + zl) % NZH
                        pairs.append((src * n_pose + pose, dst * n_pose + pose))
    return pairs


SIN_TERMS = tuple(
    (-1) ** n * (2 * math.pi) ** (2 * n + 1) / math.factorial(2 * n + 1) for n in range(7)
)


def sin_quarter(t, scale=1.0):
    square = t * t
    value = square * (scale * SIN_TERMS[-1]) + scale * SIN_TERMS[-2]
    for term in SIN_TERMS[-3::-1]:
        value = value * square + scale * term
    return value * t


WEIGHT_ROWS = 32


def dot_nt(a, b):
    return lax.dot_general(a, b, (((1,), (1,)), ((), ())), preferred_element_type=jnp.float32)


def score_terms(proj, weighted_real, weighted_imag, noise):
    n_z = proj.shape[0]
    real = jnp.concatenate([proj[z, 0] for z in range(n_z)], axis=1)
    imag = jnp.concatenate([proj[z, 1] for z in range(n_z)], axis=1)
    real_f, imag_f = real.astype(jnp.float32), imag.astype(jnp.float32)
    power = (real_f * real_f + imag_f * imag_f).astype(jnp.bfloat16)
    return dot_nt(real, weighted_real) + dot_nt(imag, weighted_imag) - 0.5 * dot_nt(power, noise)


def weight_kernel(
    x_ref, images_ref, sin_ref, cos_ref, inv_ref, proj_ref, weighted_ref, noise_ref, part_ref
):
    width = images_ref.shape[2]

    def body(i, _):
        rows = pl.ds(pl.multiple_of(i * WEIGHT_ROWS, WEIGHT_ROWS), WEIGHT_ROWS)
        sin_lo, cos_lo = sin_ref[rows, :LANES], cos_ref[rows, :LANES]
        sin_all, cos_all = sin_ref[rows, LANES:], cos_ref[rows, LANES:]
        for j in range(width // LANES):
            cols = slice(j * LANES, (j + 1) * LANES)
            contrast = -(sin_all[:, j : j + 1] * cos_lo + cos_all[:, j : j + 1] * sin_lo)
            scaled = contrast * inv_ref[:, cols]
            for c in range(2):
                image = images_ref[c, rows, cols].astype(jnp.float32)
                weighted_ref[c, rows, cols] = (image * scaled).astype(jnp.bfloat16)
            noise_ref[rows, cols] = (contrast * scaled).astype(jnp.bfloat16)
        return 0

    lax.fori_loop(0, images_ref.shape[1] // WEIGHT_ROWS, body, 0)
    block = proj_ref.shape[0] * proj_ref.shape[3]
    cols = pl.ds(pl.multiple_of(x_ref[0] * block, block), block)
    part_ref[...] = score_terms(
        proj_ref, weighted_ref[0, :, cols], weighted_ref[1, :, cols], noise_ref[:, cols]
    )


def weight_images(x, images, defocus, inv_sigma2, proj):
    _, n, width = images.shape
    low = jnp.arange(LANES, dtype=jnp.float32) / width
    high = (jnp.arange(LANES, dtype=jnp.float32) * LANES + 0.5) / width
    phase = jnp.concatenate(
        [defocus[:, None] * low[None, :], defocus[:, None] * high[None, :] + 0.1], axis=1
    )
    assert width <= LANES * LANES
    in_vmem = pl.BlockSpec(memory_space=pltpu.VMEM)
    return pl.pallas_call(
        weight_kernel,
        in_specs=[pl.BlockSpec(memory_space=pltpu.SMEM)] + [in_vmem] * 5,
        out_specs=[in_vmem] * 3,
        out_shape=[
            jax.ShapeDtypeStruct((2, n, width), jnp.bfloat16),
            jax.ShapeDtypeStruct((n, width), jnp.bfloat16),
            jax.ShapeDtypeStruct((proj.shape[2], n), jnp.float32),
        ],
        cost_estimate=SMALL_COST,
        compiler_params=pltpu.CompilerParams(vmem_limit_bytes=VMEM_LIMIT),
        interpret=INTERPRET,
        name="weight_images",
    )(x[None], images, jnp.sin(phase), jnp.cos(phase), inv_sigma2[None, :], proj)


def score_kernel(
    x_ref, proj_hbm, weighted_hbm, noise_hbm, part_ref, bias_ref, scores_ref, log_sum_ref,
    proj_ref, weighted_ref, noise_ref, sems,
):
    n_s, n_z, _, _, slab = proj_ref.shape
    block = n_z * slab

    def copies(i):
        source = (x_ref[0] + i + 1) & (NX - 1)
        cols = pl.ds(pl.multiple_of(source * block, block), block)
        return (
            pltpu.make_async_copy(proj_hbm.at[source], proj_ref.at[i], sems.at[0, i]),
            pltpu.make_async_copy(weighted_hbm.at[:, :, cols], weighted_ref.at[i], sems.at[1, i]),
            pltpu.make_async_copy(noise_hbm.at[:, cols], noise_ref.at[i], sems.at[2, i]),
        )

    for i in range(n_s):
        for copy in copies(i):
            copy.start()
    total = part_ref[...]
    for i in range(n_s):
        for copy in copies(i):
            copy.wait()
        total += score_terms(proj_ref.at[i], weighted_ref[i, 0], weighted_ref[i, 1], noise_ref[i])
    bias = bias_ref[...]
    scores = jnp.where(bias == NEG_FILL, bias, total + bias)
    scores_ref[...] = scores
    peak = jnp.max(scores, axis=0, keepdims=True)
    log_sum = peak + jnp.log(jnp.sum(jnp.exp(scores - peak), axis=0, keepdims=True))
    log_sum_ref[...] = jnp.broadcast_to(log_sum[None], log_sum_ref.shape)


def score(x, proj, weighted, noise, part, bias, copies):
    n_x, n_z, _, rows, slab = proj.shape
    n = weighted.shape[1]
    in_hbm, in_vmem = pl.BlockSpec(memory_space=pl.ANY), pl.BlockSpec(memory_space=pltpu.VMEM)
    return pl.pallas_call(
        score_kernel,
        in_specs=[pl.BlockSpec(memory_space=pltpu.SMEM)] + [in_hbm] * 3 + [in_vmem] * 2,
        out_specs=[in_vmem] * 2,
        out_shape=[
            jax.ShapeDtypeStruct((rows, n), jnp.float32),
            jax.ShapeDtypeStruct((copies, 1, n), jnp.float32),
        ],
        scratch_shapes=[
            pltpu.VMEM((n_x - 1,) + proj.shape[1:], jnp.bfloat16),
            pltpu.VMEM((n_x - 1, 2, n, n_z * slab), jnp.bfloat16),
            pltpu.VMEM((n_x - 1, n, n_z * slab), jnp.bfloat16),
            pltpu.SemaphoreType.DMA((3, n_x - 1)),
        ],
        cost_estimate=SMALL_COST,
        compiler_params=pltpu.CompilerParams(vmem_limit_bytes=MOST_VMEM),
        interpret=INTERPRET,
        name="score",
    )(x[None], proj, weighted, noise, part, bias)


def posterior_kernel(core_ref, scores_ref, log_sums_ref, post_ref, post_bf_ref):
    parts = log_sums_ref[...]
    peak = jnp.max(parts, axis=0)
    log_sum = peak + jnp.log(jnp.sum(jnp.exp(parts - peak[None]), axis=0))
    posteriors = jnp.exp(scores_ref[...] - log_sum)
    half = posteriors.shape[1] // NC
    swapped = jnp.concatenate([posteriors[:, half:], posteriors[:, :half]], axis=1)
    own_first = jnp.where(core_ref[0] == 0, posteriors, swapped).astype(jnp.bfloat16)
    post_bf_ref[...] = own_first
    post_ref[...] = posteriors.T


def posterior(core, scores, log_sums):
    rows, n = scores.shape
    return pl.pallas_call(
        posterior_kernel,
        in_specs=[
            pl.BlockSpec(memory_space=pltpu.SMEM),
            pl.BlockSpec(),
            pl.BlockSpec(memory_space=pltpu.VMEM),
        ],
        out_shape=[
            jax.ShapeDtypeStruct((n, rows), jnp.float32),
            jax.ShapeDtypeStruct((rows, n), jnp.bfloat16),
        ],
        cost_estimate=SMALL_COST,
        compiler_params=pltpu.CompilerParams(vmem_limit_bytes=VMEM_LIMIT),
        interpret=INTERPRET,
        name="posterior",
    )(core[None], scores, log_sums)


def squared_contrast(defocus, freq2):
    turns = freq2 * (defocus * (1.0 / math.pi)) + 0.1 / math.pi
    return 0.5 - sin_quarter(0.25 - jnp.abs(turns - jnp.round(turns)), 0.5)


def defocus_terms(defocus):
    scaled = defocus * (1.0 / 256.0)
    first = lax.reduce_precision(scaled, 8, 7)
    second = lax.reduce_precision(scaled - first, 8, 7)
    third = scaled - first - second
    return jnp.stack([first, second, third]).astype(jnp.bfloat16)


def back_kernel(sources, added, width, start_ref, *refs):
    n_s = len(sources)
    posts, hbm = refs[:n_s], refs[n_s : n_s + 2]
    before_ref = refs[n_s + 2] if added else None
    out_ref, own_ref, other_ref, sems = refs[n_s + 2 + added :]
    n_z, _, n = posts[0].shape
    slab, half = out_ref.shape[2], n // NC

    def copies(i):
        pairs = zip(hbm, (own_ref, other_ref))
        return [
            pltpu.make_async_copy(src.at[sources[i]], dst.at[i], sems.at[i, j])
            for j, (src, dst) in enumerate(pairs)
        ]

    for i in range(n_s):
        for copy in copies(i):
            copy.start()
    pixel = start_ref[0] + lax.broadcasted_iota(jnp.int32, (slab, half), 0)
    freq2 = (pixel.astype(jnp.float32) + 0.5) * (1.0 / width)
    for i in range(n_s):
        for copy in copies(i):
            copy.wait()
        stacks = [stack[i, t] for t in range(n_z) for stack in (own_ref, other_ref)]
        post = jnp.concatenate([posts[i][t] for t in range(n_z)], axis=1)
        first = added or i > 0
        for c in range(2):
            images = jnp.concatenate([stack[c * half : (c + 1) * half] for stack in stacks], axis=0)
            total = jnp.dot(post, images, preferred_element_type=jnp.float32)
            before = (out_ref if i > 0 else before_ref)[c] if first else None
            out_ref[c] = total + before if first else total
        squares = []
        for stack in stacks:
            terms = stack[NC * half : NC * half + TERM_ROWS].astype(jnp.float32)
            defocus = (terms[0:1, :half] + terms[1:2, :half] + terms[2:3, :half]) * 256.0
            squares.append(squared_contrast(defocus, freq2).astype(jnp.bfloat16))
        total = dot_nt(post, jnp.concatenate(squares, axis=1))
        before = (out_ref if i > 0 else before_ref)[2] if first else None
        out_ref[2] = total + before if first else total


def back_project(start, width, sources, posts, stacks, before=None):
    n_s, rows = len(sources), posts[0].shape[1]
    slab = stacks[0].shape[3]
    in_hbm, in_vmem = pl.BlockSpec(memory_space=pl.ANY), pl.BlockSpec(memory_space=pltpu.VMEM)
    added = before is not None
    scratch = [pltpu.VMEM((n_s,) + stack.shape[1:], jnp.bfloat16) for stack in stacks]
    return pl.pallas_call(
        functools.partial(back_kernel, sources, added, width),
        in_specs=[pl.BlockSpec(memory_space=pltpu.SMEM)]
        + [in_vmem] * n_s
        + [in_hbm] * 2
        + [in_vmem] * added,
        out_specs=in_vmem,
        out_shape=jax.ShapeDtypeStruct((3, rows, slab), jnp.float32),
        scratch_shapes=scratch + [pltpu.SemaphoreType.DMA((n_s, 2))],
        cost_estimate=SMALL_COST,
        compiler_params=pltpu.CompilerParams(vmem_limit_bytes=BACK_VMEM),
        interpret=INTERPRET,
        name="back_project",
    )(start[None], *posts, *stacks, *([before] if added else []))


def exchange(copies, axis, groups=None):
    return lax.all_to_all(copies, axis, 0, 0, axis_index_groups=groups)


def copies_of(value, size):
    return jnp.broadcast_to(value[None], (size,) + value.shape)


def on_device(
    images, projections, defocus, inv_sigma2, log_prior, row_class, pose_block, significant
):
    _, n, width = images.shape
    _, rows, slab = projections.shape
    half = n // NC
    group, pose = lax.axis_index("grp"), lax.axis_index("pose")
    x, zh = group >> 2, group & 3
    y, zl, core = pose >> 3, (pose >> 1) & 3, pose & 1

    z_groups = [[a * NZH + b for b in range(NZH)] for a in range(NX)]
    x_groups = [[a * NZH + b for a in range(NX)] for b in range(NZH)]
    y_groups = [
        [(a * NZL + b) * NC + c for a in range(NY)] for b in range(NZL) for c in range(NC)
    ]
    with jax.named_scope("gather_projections"):
        proj_z = lax.all_gather(projections, "grp", axis=0, axis_index_groups=z_groups)
        proj_z, defocus = lax.optimization_barrier((proj_z, defocus))
        proj = lax.all_gather(proj_z, "grp", axis=0, axis_index_groups=x_groups)

    with jax.named_scope("exchange_images"):
        target = (((x + y) & 3) << 2) + ((zh + zl) & 3)
        cut = lax.dynamic_slice(images, (0, core * half, target * slab), (2, half, slab))
        part_defocus = lax.dynamic_slice(defocus, (core * half,), (half,))
        pixel = (target * slab + jnp.arange(slab)).astype(jnp.float32)
        contrast = -jnp.sin(part_defocus[:, None] * ((pixel + 0.5) / width)[None, :] + 0.1)
        cut = (cut.astype(jnp.float32) * contrast[None]).astype(jnp.bfloat16)
        terms = jnp.pad(defocus_terms(part_defocus), ((0, TERM_ROWS - 3), (0, slab - half)))
        share = jnp.concatenate([cut.reshape(2 * half, slab), terms], axis=0)
        share = lax.ppermute(share, ("grp", "pose"), share_pairs())

    with jax.named_scope("weights"):
        weighted, noise, part = weight_images(x, images, defocus, inv_sigma2, proj_z)
        class_match = row_class[:, None] == jnp.arange(log_prior.shape[0])[None, :]
        prior_rows = jnp.sum(jnp.where(class_match, log_prior[None, :], 0.0), axis=1)
        block_table = pose_block[:, None] == jnp.arange(significant.shape[1])[None, :]
        hits = jnp.einsum(
            "rb,ib->ri",
            block_table.astype(jnp.bfloat16),
            significant.astype(jnp.bfloat16),
            preferred_element_type=jnp.float32,
        )
        bias = jnp.where(hits > 0.5, prior_rows[:, None], jnp.float32(NEG_FILL))

    with jax.named_scope("gather_images"):
        share, part, bias = lax.optimization_barrier((share, part, bias))
        turned = copies_of(share, NZL)
        for d in (1, 2, 3):
            block = lax.ppermute(share, "pose", pose_shift(0, d, 0))
            turned = lax.dynamic_update_slice_in_dim(turned, block[None], (zh - zl + d) & 3, 0)
        turned, proj = lax.optimization_barrier((turned, proj))
        own = lax.all_gather(turned, "pose", axis=0, axis_index_groups=y_groups)

    with jax.named_scope("scores"):
        scores, log_sum = score(x, proj, weighted, noise, part, bias, NY * NZL * NC)

    with jax.named_scope("softmax"):
        posteriors, post_bf = posterior(core, scores, exchange(log_sum, "pose"))

    with jax.named_scope("gather_posteriors"):
        post = [lax.all_gather(post_bf, "grp", axis=0, axis_index_groups=z_groups)] + [None] * 3
        for d in (1, 3, 2):
            post[d] = lax.ppermute(post[0], "grp", grp_shift(d))
        post[0], own = lax.optimization_barrier((post[0], own))
        other = lax.ppermute(own, "pose", pose_shift(0, 0, 1))

    with jax.named_scope("back_project"):
        start, stacks = group * slab, (own, other)
        back_proj = back_project(start, width, (0, 1), post[:2], stacks)
        back_proj = back_project(start, width, (3, 2), (post[3], post[2]), stacks, back_proj)
    return (posteriors, back_proj)


def solution(mesh):
    placed = (
        P(None, "grp", None),
        P(None, "pose", "grp"),
        P("grp"),
        P(),
        P(),
        P("pose"),
        P("pose"),
        P("grp", None),
    )
    return jax.shard_map(
        on_device,
        mesh=mesh,
        in_specs=placed,
        out_specs=(P("grp", "pose"), P(None, "pose", "grp")),
        check_vma=False,
    )
```

time: 159 us -> 156 us (0.981)
  Pallas kernels: 19.3 us -> 17.4 us
    pallas_call x2, Pallas kernels: 9.23 us -> 7.35 us  [back_project(): pl.pallas_call(functools.partial(back_kernel, sources, added, width), in_...]
    unnamed x30 -> x26, local copies, waits for them, and re-layouts: 9.59 us -> 9.27 us
  transfers between devices with their start and end apart: 10 -> 10, of which waited for: 5 -> 4; matrix products, arithmetic and copies ran while one was open for 3% -> 3% of each run, Pallas kernels for 9% -> 9%
where the time goes in v2:
time: 156 us
  blocking collectives  72.2 us (46%)
  starting transfers between devices  27.9 us (18%)
  Pallas kernels  17.4 us (11%)
  between operations  14.3 us (9%)
  waiting for transfers between devices  9.48 us (6%)
  local copies, waits for them, and re-layouts  9.35 us (6%)
  other arithmetic  4.16 us (3%)
    all_gather x1, blocking collectives, on_device(): lax.all_gather(projections, 'grp', axis=0, axis_index_groups=z_groups)  35.2 us
    all_gather x1, blocking collectives, on_device(): lax.all_gather(post_bf, 'grp', axis=0, axis_index_groups=z_groups)  19.7 us
    all_to_all x1, blocking collectives, exchange(): return lax.all_to_all(copies, axis, 0, 0, axis_index_groups=groups)  17.2 us
    ppermute x3, starting transfers between devices, on_device(): block = lax.ppermute(share, 'pose', pose_shift(0, d, 0))  15.4 us
    ppermute x3, starting transfers between devices, on_device(): post[d] = lax.ppermute(post[0], 'grp', grp_shift(d))  9.82 us
    unnamed x26, local copies, waits for them, and re-layouts  9.27 us
    pallas_call x2, Pallas kernels, back_project(): pl.pallas_call(functools.partial(back_kernel, sources, added, width), in_...  7.35 us
    ppermute x3, waiting for transfers between devices, on_device(): post[d] = lax.ppermute(post[0], 'grp', grp_shift(d))  6.93 us
  transfers between devices with their start and end apart: 10, of which 4 were waited for; matrix products, arithmetic and copies ran while one was open for 3% of the time, Pallas kernels for 9%

profile of v2, /device:TPU:6, one launch (start us, length us, event | category | flops | bytes accessed | tf_op | source)
XLA Modules:
  0.0 155.6 jit_solution(1200858012922222566)
XLA Ops:
  7.2 35.2 %all-gather = bf16[8,128,256]{2,1,0:T(8,128)(2,1)} all-gather(bf16[2,128,256]{2,1,0:T(8,128)(2,1)} %param.9), channel_id=2, replica_groups={{0,32,64,96},{128,160,192,224},{256,288,320,352},{384,416,448,480},{1,3..., dimensions={0}, use_global_device_ids=true | all-gather | bytes 655360 | tf_op jit(solution)/shard_map/gather_projections/all_gather | solution.py:324
  43.9 0.9 multiply_convert_fusion
  46.3 1.0 fusion.1
  47.3 2.2 %copy-done.1 = bf16[2,256,4096]{2,1,0:T(8,128)(2,1)S(1)} copy-done((bf16[2,256,4096]{2,1,0:T(8,128)(2,1)S(1)}, bf16[2,256,4096]{2,1,0:T(8,128)(2,1)}, u32[]{:S(2)}) %copy-start.1) | copy-done | bytes 4194328
  49.5 3.8 %weight_images.1 = (bf16[2,256,4096]{2,1,0:T(8,128)(2,1)S(1)}, bf16[256,4096]{1,0:T(8,128)(2,1)S(1)}, f32[128,256]{1,0:T(8,128)S(1)}) custom-call(s32[1]{0:T(128)} %bitcast.1.x_ref, bf16[2,256,4096]{2,1,0:T(8,128)(2,1)S(1)} %copy-done.1, f32[256,256]{1,0:T(8,128)S(1)} %get-tuple-element.37.sin_ref, f32[256,256]{1,0:T(8,128)S(1)} %get-tuple-element.36.cos_ref, ...), custom_call_target="tpu_custom_call" | custom-call | flops 1 | bytes 1 | tf_op jit(solution)/shard_map/weights/weight_images/pallas_call | solution.py:119
  53.4 2.0 %copy-done.2 = bf16[2,256,4096]{2,1,0:T(8,128)(2,1)} copy-done((bf16[2,256,4096]{2,1,0:T(8,128)(2,1)}, bf16[2,256,4096]{2,1,0:T(8,128)(2,1)S(1)}, u32[]{:S(2)}) %copy-start.2) | copy-done | bytes 4194328
  55.3 1.4 copy-done.3
  58.4 6.1 %collective-permute-start.1 = (bf16[272,256]{1,0:T(8,128)(2,1)S(1)}, bf16[272,256]{1,0:T(8,128)(2,1)S(1)}, u32[]{:S(2)}, u32[]{:S(2)}) collective-permute-start(bf16[272,256]{1,0:T(8,128)(2,1)S(1)} %collective-permute-done), channel_id=1, source_target_pairs={{0,2},{1,3},{2,4},{3,5},{4,6},{5,7},{6,0},{7,1},{8,10},{9,11},{10,... | collective-permute-start | bytes 417800 | tf_op jit(solution)/shard_map/gather_images/ppermute | solution.py:356
  64.4 4.5 %collective-permute-start.2 = (bf16[272,256]{1,0:T(8,128)(2,1)S(1)}, bf16[272,256]{1,0:T(8,128)(2,1)S(1)}, u32[]{:S(2)}, u32[]{:S(2)}) collective-permute-start(bf16[272,256]{1,0:T(8,128)(2,1)S(1)} %collective-permute-done), channel_id=1, source_target_pairs={{0,4},{1,5},{2,6},{3,7},{4,0},{5,1},{6,2},{7,3},{8,12},{9,13},{10,... | collective-permute-start | bytes 417800 | tf_op jit(solution)/shard_map/gather_images/ppermute | solution.py:356
  69.0 4.8 %collective-permute-start.3 = (bf16[272,256]{1,0:T(8,128)(2,1)S(1)}, bf16[272,256]{1,0:T(8,128)(2,1)S(1)}, u32[]{:S(2)}, u32[]{:S(2)}) collective-permute-start(bf16[272,256]{1,0:T(8,128)(2,1)S(1)} %collective-permute-done), channel_id=1, source_target_pairs={{0,6},{1,7},{2,0},{3,1},{4,2},{5,3},{6,4},{7,5},{8,14},{9,15},{10,... | collective-permute-start | bytes 417800 | tf_op jit(solution)/shard_map/gather_images/ppermute | solution.py:356
  73.9 1.5 collective-permute-done.2
  75.4 1.0 collective-permute-done.3
  77.3 5.3 %score.1 = (f32[128,256]{1,0:T(8,128)}, f32[32,1,256]{2,1,0:T(1,128)}) custom-call(s32[1]{0:T(128)} %bitcast.1.x_ref, bf16[4,4,2,128,256]{4,3,2,1,0:T(8,128)(2,1)} %bitcast.31, bf16[2,256,4096]{2,1,0:T(8,128)(2,1)} %copy-done.2, bf16[256,4096]{1,0:T(8,128)(2,1)} %copy-done.3, f32[128,256]{1,0:T(8,128)} %copy-done.4, f32[128,256]{1,0:T(8,128)} %fusion.bias_ref), custom_call_target="tpu_custom_call" | custom-call | flops 1 | bytes 1 | tf_op jit(solution)/shard_map/scores/score/pallas_call | solution.py:171
  82.6 17.2 %all_to_all.5.log_sums_ref = f32[32,1,256]{2,1,0:T(1,128)S(1)} all-to-all(f32[32,1,256]{2,1,0:T(1,128)} %get-tuple-element.28), channel_id=1, replica_groups=mesh['grp'=16,'pose'=32] {'pose'}, dimensions={0} | all-to-all | bytes 65536 | tf_op jit(solution)/shard_map/softmax/all_to_all | solution.py:301
  99.8 0.9 copy-done.5
  101.6 19.7 %all-gather.2 = bf16[512,256]{1,0:T(8,128)(2,1)S(1)} all-gather(bf16[128,256]{1,0:T(8,128)(2,1)S(1)} %get-tuple-element.30), channel_id=4, replica_groups={{0,32,64,96},{128,160,192,224},{256,288,320,352},{384,416,448,480},{1,3..., dimensions={0}, use_global_device_ids=true | all-gather | bytes 327680 | tf_op jit(solution)/shard_map/gather_posteriors/all_gather | solution.py:368
  121.3 1.9 %collective-permute-start.6 = (bf16[4,4,272,256]{3,2,1,0:T(8,128)(2,1)}, bf16[4,4,272,256]{3,2,1,0:T(8,128)(2,1)S(1)}, u32[]{:S(2)}, u32[]{:S(2)}) collective-permute-start(bf16[4,4,272,256]{3,2,1,0:T(8,128)(2,1)} %bitcast.28), channel_id=1, source_target_pairs={{0,1},{1,0},{2,3},{3,2},{4,5},{5,4},{6,7},{7,6},{8,9},{9,8},{10,11... | collective-permute-start | bytes 6684680 | tf_op jit(solution)/shard_map/gather_posteriors/ppermute | solution.py:372
  123.2 4.3 %collective-permute-start.7 = (bf16[4,128,256]{2,1,0:T(8,128)(2,1)S(1)}, bf16[4,128,256]{2,1,0:T(8,128)(2,1)S(1)}, u32[]{:S(2)}, u32[]{:S(2)}) collective-permute-start(bf16[4,128,256]{2,1,0:T(8,128)(2,1)S(1)} %bitcast.23), channel_id=1, source_target_pairs={{0,128},{32,160},{64,192},{96,224},{128,256},{160,288},{192,320},{... | collective-permute-start | bytes 786440 | tf_op jit(solution)/shard_map/gather_posteriors/ppermute | solution.py:370
  127.5 1.9 %collective-permute-start.4 = (bf16[4,128,256]{2,1,0:T(8,128)(2,1)S(1)}, bf16[4,128,256]{2,1,0:T(8,128)(2,1)S(1)}, u32[]{:S(2)}, u32[]{:S(2)}) collective-permute-start(bf16[4,128,256]{2,1,0:T(8,128)(2,1)S(1)} %bitcast.24), channel_id=1, source_target_pairs={{0,384},{32,416},{64,448},{96,480},{128,0},{160,32},{192,64},{224,... | collective-permute-start | bytes 786440 | tf_op jit(solution)/shard_map/gather_posteriors/ppermute | solution.py:370
  129.4 3.6 %collective-permute-start.5 = (bf16[4,128,256]{2,1,0:T(8,128)(2,1)S(1)}, bf16[4,128,256]{2,1,0:T(8,128)(2,1)S(1)}, u32[]{:S(2)}, u32[]{:S(2)}) collective-permute-start(bf16[4,128,256]{2,1,0:T(8,128)(2,1)S(1)} %bitcast.25), channel_id=1, source_target_pairs={{0,256},{32,288},{64,320},{96,352},{128,384},{160,416},{192,448},{... | collective-permute-start | bytes 786440 | tf_op jit(solution)/shard_map/gather_posteriors/ppermute | solution.py:370
  133.8 1.4 copy-done.7
  135.2 3.3 %back_project.2.refs_4_ = f32[3,128,256]{2,1,0:T(8,128)S(1)} custom-call(s32[1]{0:T(128)} %bitcast.12.start_ref, bf16[4,128,256]{2,1,0:T(8,128)(2,1)S(1)} %bitcast.26, bf16[4,128,256]{2,1,0:T(8,128)(2,1)S(1)} %collective-permute-done.7.refs_1_, bf16[4,4,272,256]{3,2,1,0:T(8,128)(2,1)} %bitcast.29, bf16[4,4,272,256]{3,2,1,0:T(8,128)(2,1)} %copy-done.7), custom_call_target="tpu_custom_call" | custom-call | flops 1 | bytes 1 | tf_op jit(solution)/shard_map/back_project/back_project/pallas_call | solution.py:284
  138.5 6.2 %collective-permute-done.4.refs_0_ = bf16[4,128,256]{2,1,0:T(8,128)(2,1)S(1)} collective-permute-done((bf16[4,128,256]{2,1,0:T(8,128)(2,1)S(1)}, bf16[4,128,256]{2,1,0:T(8,128)(2,1)S(1)}, u32[]{:S(2)}, u32[]{:S(2)}) %collective-permute-start.4) | collective-permute-done | bytes 262176 | tf_op jit(solution)/shard_map/gather_posteriors/ppermute | solution.py:370
  144.7 4.1 %back_project.3 = f32[3,128,256]{2,1,0:T(8,128)} custom-call(s32[1]{0:T(128)} %bitcast.12.start_ref, bf16[4,128,256]{2,1,0:T(8,128)(2,1)S(1)} %collective-permute-done.4.refs_0_, bf16[4,128,256]{2,1,0:T(8,128)(2,1)S(1)} %collective-permute-done.5.refs_1_, bf16[4,4,272,256]{3,2,1,0:T(8,128)(2,1)} %bitcast.30, bf16[4,4,272,256]{3,2,1,0:T(8,128)(2,1)} %copy-done.7, ...), custom_call_target="tpu_custom_call" | custom-call | flops 1 | bytes 1 | tf_op jit(solution)/shard_map/back_project/back_project/pallas_call | solution.py:284
  (48 shorter events, 7.1 us)
Async XLA Ops:
  7.2 40.2 %copy-start.6 = (f32[4096]{0:T(1024)S(1)}, f32[4096]{0:T(1024)}, u32[]{:S(2)}) copy-start(f32[4096]{0:T(1024)} %param.11) | copy-start | bytes 49156
  7.2 69.3 %all-gather.7.cloned.1.call-start = ((), (), s32[]{:S(2)}) async-start(), calls=%async_computation.1 | async-start | bytes 2621440 | tf_op jit(solution)/shard_map/gather_projections/all_gather | solution.py:326
  42.4 4.9 %copy-start = (bf16[8,128,256]{2,1,0:T(8,128)(2,1)S(1)}, bf16[8,128,256]{2,1,0:T(8,128)(2,1)}, u32[]{:S(2)}) copy-start(bf16[8,128,256]{2,1,0:T(8,128)(2,1)} %all-gather) | copy-start | bytes 1572868
  42.5 78.8 %all-gather.9.cloned.1.call-start = ((), (), s32[]{:S(2)}) async-start(), calls=%async_computation.2 | async-start | bytes 2785280 | tf_op jit(solution)/shard_map/gather_images/all_gather | solution.py:359
  44.9 13.5 %collective-permute-start = (bf16[272,256]{1,0:T(8,128)(2,1)S(1)}, bf16[272,256]{1,0:T(8,128)(2,1)S(1)}, u32[]{:S(2)}, u32[]{:S(2)}) collective-permute-start(bf16[272,256]{1,0:T(8,128)(2,1)S(1)} %pad_maximum_fusion.1), channel_id=1, source_target_pairs={{0,0},{1,1},{2,34},{3,35},{4,68},{5,69},{6,102},{7,103},{8,136},{9... | collective-permute-start | bytes 417800 | tf_op jit(solution)/shard_map/exchange_images/ppermute | solution.py:337
  47.3 2.2 %copy-start.1 = (bf16[2,256,4096]{2,1,0:T(8,128)(2,1)S(1)}, bf16[2,256,4096]{2,1,0:T(8,128)(2,1)}, u32[]{:S(2)}) copy-start(bf16[2,256,4096]{2,1,0:T(8,128)(2,1)} %images_ref.1) | copy-start | bytes 12582916
  49.5 7.9 %copy-start.11 = (f32[64]{0:T(128)S(1)}, f32[64]{0:T(128)}, u32[]{:S(2)}) copy-start(f32[64]{0:T(128)} %param.12) | copy-start | bytes 772
  49.5 7.9 %copy-start.12 = (s32[128]{0:T(128)S(1)}, s32[128]{0:T(128)}, u32[]{:S(2)}) copy-start(s32[128]{0:T(128)} %param.13) | copy-start | bytes 1540
  49.5 7.9 %copy-start.9 = (s32[256,256]{1,0:T(8,128)S(1)}, s32[256,256]{1,0:T(8,128)}, u32[]{:S(2)}) copy-start(s32[256,256]{1,0:T(8,128)} %param.15) | copy-start | bytes 786436
  49.5 7.9 %copy-start.10 = (s32[128]{0:T(128)S(1)}, s32[128]{0:T(128)}, u32[]{:S(2)}) copy-start(s32[128]{0:T(128)} %param.14) | copy-start | bytes 1540
  53.4 2.0 %copy-start.2 = (bf16[2,256,4096]{2,1,0:T(8,128)(2,1)}, bf16[2,256,4096]{2,1,0:T(8,128)(2,1)S(1)}, u32[]{:S(2)}) copy-start(bf16[2,256,4096]{2,1,0:T(8,128)(2,1)S(1)} %get-tuple-element.23.weighted_hbm) | copy-start | bytes 12582916
  55.3 1.4 copy-start.3
  56.7 0.7 copy-start.4
  58.4 15.5 %collective-permute-start.1 = (bf16[272,256]{1,0:T(8,128)(2,1)S(1)}, bf16[272,256]{1,0:T(8,128)(2,1)S(1)}, u32[]{:S(2)}, u32[]{:S(2)}) collective-permute-start(bf16[272,256]{1,0:T(8,128)(2,1)S(1)} %collective-permute-done), channel_id=1, source_target_pairs={{0,2},{1,3},{2,4},{3,5},{4,6},{5,7},{6,0},{7,1},{8,10},{9,11},{10,... | collective-permute-start | bytes 417800 | tf_op jit(solution)/shard_map/gather_images/ppermute | solution.py:356
  64.4 11.0 %collective-permute-start.2 = (bf16[272,256]{1,0:T(8,128)(2,1)S(1)}, bf16[272,256]{1,0:T(8,128)(2,1)S(1)}, u32[]{:S(2)}, u32[]{:S(2)}) collective-permute-start(bf16[272,256]{1,0:T(8,128)(2,1)S(1)} %collective-permute-done), channel_id=1, source_target_pairs={{0,4},{1,5},{2,6},{3,7},{4,0},{5,1},{6,2},{7,3},{8,12},{9,13},{10,... | collective-permute-start | bytes 417800 | tf_op jit(solution)/shard_map/gather_images/ppermute | solution.py:356
  69.0 7.4 %collective-permute-start.3 = (bf16[272,256]{1,0:T(8,128)(2,1)S(1)}, bf16[272,256]{1,0:T(8,128)(2,1)S(1)}, u32[]{:S(2)}, u32[]{:S(2)}) collective-permute-start(bf16[272,256]{1,0:T(8,128)(2,1)S(1)} %collective-permute-done), channel_id=1, source_target_pairs={{0,6},{1,7},{2,0},{3,1},{4,2},{5,3},{6,4},{7,5},{8,14},{9,15},{10,... | collective-permute-start | bytes 417800 | tf_op jit(solution)/shard_map/gather_images/ppermute | solution.py:356
  76.4 0.8 copy-start.8
  99.8 0.9 copy-start.5
  121.3 12.5 %collective-permute-start.6 = (bf16[4,4,272,256]{3,2,1,0:T(8,128)(2,1)}, bf16[4,4,272,256]{3,2,1,0:T(8,128)(2,1)S(1)}, u32[]{:S(2)}, u32[]{:S(2)}) collective-permute-start(bf16[4,4,272,256]{3,2,1,0:T(8,128)(2,1)} %bitcast.28), channel_id=1, source_target_pairs={{0,1},{1,0},{2,3},{3,2},{4,5},{5,4},{6,7},{7,6},{8,9},{9,8},{10,11... | collective-permute-start | bytes 6684680 | tf_op jit(solution)/shard_map/gather_posteriors/ppermute | solution.py:372
  123.2 10.6 %collective-permute-start.7 = (bf16[4,128,256]{2,1,0:T(8,128)(2,1)S(1)}, bf16[4,128,256]{2,1,0:T(8,128)(2,1)S(1)}, u32[]{:S(2)}, u32[]{:S(2)}) collective-permute-start(bf16[4,128,256]{2,1,0:T(8,128)(2,1)S(1)} %bitcast.23), channel_id=1, source_target_pairs={{0,128},{32,160},{64,192},{96,224},{128,256},{160,288},{192,320},{... | collective-permute-start | bytes 786440 | tf_op jit(solution)/shard_map/gather_posteriors/ppermute | solution.py:370
  127.5 17.2 %collective-permute-start.4 = (bf16[4,128,256]{2,1,0:T(8,128)(2,1)S(1)}, bf16[4,128,256]{2,1,0:T(8,128)(2,1)S(1)}, u32[]{:S(2)}, u32[]{:S(2)}) collective-permute-start(bf16[4,128,256]{2,1,0:T(8,128)(2,1)S(1)} %bitcast.24), channel_id=1, source_target_pairs={{0,384},{32,416},{64,448},{96,480},{128,0},{160,32},{192,64},{224,... | collective-permute-start | bytes 786440 | tf_op jit(solution)/shard_map/gather_posteriors/ppermute | solution.py:370
  129.4 15.2 %collective-permute-start.5 = (bf16[4,128,256]{2,1,0:T(8,128)(2,1)S(1)}, bf16[4,128,256]{2,1,0:T(8,128)(2,1)S(1)}, u32[]{:S(2)}, u32[]{:S(2)}) collective-permute-start(bf16[4,128,256]{2,1,0:T(8,128)(2,1)S(1)} %bitcast.25), channel_id=1, source_target_pairs={{0,256},{32,288},{64,320},{96,352},{128,384},{160,416},{192,448},{... | collective-permute-start | bytes 786440 | tf_op jit(solution)/shard_map/gather_posteriors/ppermute | solution.py:370
  133.8 1.4 copy-start.7
Sparse Core Ops, SparseCore 0:
  42.6 33.3 all-gather.6
  78.1 41.5 all-gather.8

commit v3 on v2

--- a/solution.py
+++ b/solution.py
@@ -16,6 +16,7 @@
 VMEM_LIMIT = 20 << 20
 MOST_VMEM = 63 << 20
 BACK_VMEM = 52 << 20
+WEIGHT_VMEM = 60 << 20
 SMALL_COST = pl.CostEstimate(flops=1, bytes_accessed=1, transcendentals=0)
 INTERPRET = False
 
@@ -81,12 +82,37 @@
 
 
 def weight_kernel(
-    x_ref, images_ref, sin_ref, cos_ref, inv_ref, proj_ref, weighted_ref, noise_ref, part_ref
+    x_ref, images_hbm, sin_ref, cos_ref, inv_ref, proj_ref, weighted_hbm, noise_hbm, part_ref,
+    images_ref, weighted_ref, noise_ref, sems,
 ):
-    width = images_ref.shape[2]
+    n, width = images_ref.shape[1:]
+    steps = n // WEIGHT_ROWS
+
+    def rows_of(i):
+        return pl.ds(pl.multiple_of(i * WEIGHT_ROWS, WEIGHT_ROWS), WEIGHT_ROWS)
+
+    def copy_in(i):
+        rows = rows_of(i)
+        return pltpu.make_async_copy(
+            images_hbm.at[:, rows, :], images_ref.at[:, rows, :], sems.at[0, i]
+        )
+
+    def copies_out(i):
+        rows = rows_of(i)
+        return (
+            pltpu.make_async_copy(
+                weighted_ref.at[:, rows, :], weighted_hbm.at[:, rows, :], sems.at[1, i]
+            ),
+            pltpu.make_async_copy(noise_ref.at[rows, :], noise_hbm.at[rows, :], sems.at[2, i]),
+        )
+
+    def start(i, _):
+        copy_in(i).start()
+        return 0
 
     def body(i, _):
-        rows = pl.ds(pl.multiple_of(i * WEIGHT_ROWS, WEIGHT_ROWS), WEIGHT_ROWS)
+        copy_in(i).wait()
+        rows = rows_of(i)
         sin_lo, cos_lo = sin_ref[rows, :LANES], cos_ref[rows, :LANES]
         sin_all, cos_all = sin_ref[rows, LANES:], cos_ref[rows, LANES:]
         for j in range(width // LANES):
@@ -97,14 +123,23 @@
                 image = images_ref[c, rows, cols].astype(jnp.float32)
                 weighted_ref[c, rows, cols] = (image * scaled).astype(jnp.bfloat16)
             noise_ref[rows, cols] = (contrast * scaled).astype(jnp.bfloat16)
+        for copy in copies_out(i):
+            copy.start()
         return 0
 
-    lax.fori_loop(0, images_ref.shape[1] // WEIGHT_ROWS, body, 0)
+    def finish(i, _):
+        for copy in copies_out(i):
+            copy.wait()
+        return 0
+
+    lax.fori_loop(0, steps, start, 0)
+    lax.fori_loop(0, steps, body, 0)
     block = proj_ref.shape[0] * proj_ref.shape[3]
     cols = pl.ds(pl.multiple_of(x_ref[0] * block, block), block)
     part_ref[...] = score_terms(
         proj_ref, weighted_ref[0, :, cols], weighted_ref[1, :, cols], noise_ref[:, cols]
     )
+    lax.fori_loop(0, steps, finish, 0)
 
 
 def weight_images(x, images, defocus, inv_sigma2, proj):
@@ -115,18 +150,24 @@
         [defocus[:, None] * low[None, :], defocus[:, None] * high[None, :] + 0.1], axis=1
     )
     assert width <= LANES * LANES
-    in_vmem = pl.BlockSpec(memory_space=pltpu.VMEM)
+    in_hbm, in_vmem = pl.BlockSpec(memory_space=pl.ANY), pl.BlockSpec(memory_space=pltpu.VMEM)
     return pl.pallas_call(
         weight_kernel,
-        in_specs=[pl.BlockSpec(memory_space=pltpu.SMEM)] + [in_vmem] * 5,
-        out_specs=[in_vmem] * 3,
+        in_specs=[pl.BlockSpec(memory_space=pltpu.SMEM), in_hbm] + [in_vmem] * 4,
+        out_specs=[in_hbm, in_hbm, in_vmem],
         out_shape=[
             jax.ShapeDtypeStruct((2, n, width), jnp.bfloat16),
             jax.ShapeDtypeStruct((n, width), jnp.bfloat16),
             jax.ShapeDtypeStruct((proj.shape[2], n), jnp.float32),
         ],
+        scratch_shapes=[
+            pltpu.VMEM((2, n, width), jnp.bfloat16),
+            pltpu.VMEM((2, n, width), jnp.bfloat16),
+            pltpu.VMEM((n, width), jnp.bfloat16),
+            pltpu.SemaphoreType.DMA((3, n // WEIGHT_ROWS)),
+        ],
         cost_estimate=SMALL_COST,
-        compiler_params=pltpu.CompilerParams(vmem_limit_bytes=VMEM_LIMIT),
+        compiler_params=pltpu.CompilerParams(vmem_limit_bytes=WEIGHT_VMEM),
         interpret=INTERPRET,
         name="weight_images",
     )(x[None], images, jnp.sin(phase), jnp.cos(phase), inv_sigma2[None, :], proj)
@@ -189,10 +230,13 @@
     )(x[None], proj, weighted, noise, part, bias)
 
 
-def posterior_kernel(core_ref, scores_ref, log_sums_ref, post_ref, post_bf_ref):
+def posterior_kernel(core_ref, scores_hbm, log_sums_ref, post_ref, post_bf_ref, scores_ref, sem):
+    copy = pltpu.make_async_copy(scores_hbm, scores_ref, sem)
+    copy.start()
     parts = log_sums_ref[...]
     peak = jnp.max(parts, axis=0)
     log_sum = peak + jnp.log(jnp.sum(jnp.exp(parts - peak[None]), axis=0))
+    copy.wait()
     posteriors = jnp.exp(scores_ref[...] - log_sum)
     half = posteriors.shape[1] // NC
     swapped = jnp.concatenate([posteriors[:, half:], posteriors[:, :half]], axis=1)
@@ -207,15 +251,16 @@
         posterior_kernel,
         in_specs=[
             pl.BlockSpec(memory_space=pltpu.SMEM),
-            pl.BlockSpec(),
+            pl.BlockSpec(memory_space=pl.ANY),
             pl.BlockSpec(memory_space=pltpu.VMEM),
         ],
         out_shape=[
             jax.ShapeDtypeStruct((n, rows), jnp.float32),
             jax.ShapeDtypeStruct((rows, n), jnp.bfloat16),
         ],
+        scratch_shapes=[pltpu.VMEM(scores.shape, jnp.float32), pltpu.SemaphoreType.DMA],
         cost_estimate=SMALL_COST,
-        compiler_params=pltpu.CompilerParams(vmem_limit_bytes=VMEM_LIMIT),
+        compiler_params=pltpu.CompilerParams(vmem_limit_bytes=MOST_VMEM),
         interpret=INTERPRET,
         name="posterior",
     )(core[None], scores, log_sums)
@@ -234,67 +279,102 @@
     return jnp.stack([first, second, third]).astype(jnp.bfloat16)
 
 
-def back_kernel(sources, added, width, start_ref, *refs):
-    n_s = len(sources)
+def squares_of(stacks, freq2):
+    parts = []
+    half = freq2.shape[1]
+    for stack in stacks:
+        terms = stack.astype(jnp.float32)
+        defocus = (terms[0:1, :half] + terms[1:2, :half] + terms[2:3, :half]) * 256.0
+        parts.append(squared_contrast(defocus, freq2).astype(jnp.bfloat16))
+    return jnp.concatenate(parts, axis=1)
+
+
+def back_kernel(sources, ahead, width, start_ref, *refs):
+    n_s, last = len(sources), not ahead
     posts, hbm = refs[:n_s], refs[n_s : n_s + 2]
-    before_ref = refs[n_s + 2] if added else None
-    out_ref, own_ref, other_ref, sems = refs[n_s + 2 + added :]
+    if last:
+        before_ref, squares_ref, out_ref, own_ref, other_ref, sems = refs[n_s + 2 :]
+    else:
+        out_ref, squares_ref, own_ref, other_ref, terms_ref, sems = refs[n_s + 2 :]
     n_z, _, n = posts[0].shape
     slab, half = out_ref.shape[2], n // NC
 
     def copies(i):
-        pairs = zip(hbm, (own_ref, other_ref))
         return [
             pltpu.make_async_copy(src.at[sources[i]], dst.at[i], sems.at[i, j])
-            for j, (src, dst) in enumerate(pairs)
+            for j, (src, dst) in enumerate(zip(hbm, (own_ref, other_ref)))
+        ]
+
+    def term_copies(i):
+        return [
+            pltpu.make_async_copy(
+                src.at[ahead[i], :, pl.ds(n, TERM_ROWS), :], terms_ref.at[i, j], sems.at[n_s + i, j]
+            )
+            for j, src in enumerate(hbm)
         ]
 
     for i in range(n_s):
         for copy in copies(i):
             copy.start()
-    pixel = start_ref[0] + lax.broadcasted_iota(jnp.int32, (slab, half), 0)
-    freq2 = (pixel.astype(jnp.float32) + 0.5) * (1.0 / width)
+    for i in range(len(ahead)):
+        for copy in term_copies(i):
+            copy.start()
+    if not last:
+        pixel = start_ref[0] + lax.broadcasted_iota(jnp.int32, (slab, half), 0)
+        freq2 = (pixel.astype(jnp.float32) + 0.5) * (1.0 / width)
     for i in range(n_s):
         for copy in copies(i):
             copy.wait()
         stacks = [stack[i, t] for t in range(n_z) for stack in (own_ref, other_ref)]
         post = jnp.concatenate([posts[i][t] for t in range(n_z)], axis=1)
-        first = added or i > 0
-        for c in range(2):
-            images = jnp.concatenate([stack[c * half : (c + 1) * half] for stack in stacks], axis=0)
-            total = jnp.dot(post, images, preferred_element_type=jnp.float32)
-            before = (out_ref if i > 0 else before_ref)[c] if first else None
-            out_ref[c] = total + before if first else total
-        squares = []
-        for stack in stacks:
-            terms = stack[NC * half : NC * half + TERM_ROWS].astype(jnp.float32)
-            defocus = (terms[0:1, :half] + terms[1:2, :half] + terms[2:3, :half]) * 256.0
-            squares.append(squared_contrast(defocus, freq2).astype(jnp.bfloat16))
-        total = dot_nt(post, jnp.concatenate(squares, axis=1))
-        before = (out_ref if i > 0 else before_ref)[2] if first else None
-        out_ref[2] = total + before if first else total
-
-
-def back_project(start, width, sources, posts, stacks, before=None):
-    n_s, rows = len(sources), posts[0].shape[1]
+        if last:
+            square = squares_ref[i]
+        else:
+            square = squares_of([stack[n : n + TERM_ROWS] for stack in stacks], freq2)
+        for c in range(3):
+            if c < 2:
+                images = [stack[c * half : (c + 1) * half] for stack in stacks]
+                total = jnp.dot(
+                    post, jnp.concatenate(images, axis=0), preferred_element_type=jnp.float32
+                )
+            else:
+                total = dot_nt(post, square)
+            if i > 0:
+                total += out_ref[c]
+            elif last:
+                total += before_ref[c]
+            out_ref[c] = total
+    for i in range(len(ahead)):
+        for copy in term_copies(i):
+            copy.wait()
+        stacks = [terms_ref[i, j, t] for t in range(n_z) for j in range(2)]
+        squares_ref[i] = squares_of(stacks, freq2)
+
+
+def back_project(start, width, sources, posts, stacks, ahead=(), before=()):
+    n_s, (n_z, rows, n) = len(sources), posts[0].shape
     slab = stacks[0].shape[3]
     in_hbm, in_vmem = pl.BlockSpec(memory_space=pl.ANY), pl.BlockSpec(memory_space=pltpu.VMEM)
-    added = before is not None
+    out_shape = [jax.ShapeDtypeStruct((3, rows, slab), jnp.float32)]
     scratch = [pltpu.VMEM((n_s,) + stack.shape[1:], jnp.bfloat16) for stack in stacks]
+    if ahead:
+        n_a = len(ahead)
+        out_shape.append(jax.ShapeDtypeStruct((n_a, slab, n_z * n), jnp.bfloat16))
+        scratch.append(pltpu.VMEM((n_a, NC, n_z, TERM_ROWS, slab), jnp.bfloat16))
     return pl.pallas_call(
-        functools.partial(back_kernel, sources, added, width),
+        functools.partial(back_kernel, sources, ahead, width),
         in_specs=[pl.BlockSpec(memory_space=pltpu.SMEM)]
         + [in_vmem] * n_s
         + [in_hbm] * 2
-        + [in_vmem] * added,
-        out_specs=in_vmem,
-        out_shape=jax.ShapeDtypeStruct((3, rows, slab), jnp.float32),
-        scratch_shapes=scratch + [pltpu.SemaphoreType.DMA((n_s, 2))],
+        + [in_vmem] * len(before),
+        out_specs=[in_vmem] * len(out_shape),
+        out_shape=out_shape,
+        scratch_shapes=scratch + [pltpu.SemaphoreType.DMA((n_s + len(ahead), 2))],
         cost_estimate=SMALL_COST,
         compiler_params=pltpu.CompilerParams(vmem_limit_bytes=BACK_VMEM),
         interpret=INTERPRET,
         name="back_project",
-    )(start[None], *posts, *stacks, *([before] if added else []))
+    )(start[None], *posts, *stacks, *before)
 
 
 def exchange(copies, axis, groups=None):
@@ -373,8 +453,9 @@
 
     with jax.named_scope("back_project"):
         start, stacks = group * slab, (own, other)
-        back_proj = back_project(start, width, (0, 1), post[:2], stacks)
-        back_proj = back_project(start, width, (3, 2), (post[3], post[2]), stacks, back_proj)
+        near, far = (0, 1), (3, 2)
+        before = back_project(start, width, near, [post[d] for d in near], stacks, ahead=far)
+        (back_proj,) = back_project(start, width, far, [post[d] for d in far], stacks, before=before)
     return (posteriors, back_proj)
 
 

time: 156 us -> 156 us (level)
  local copies, waits for them, and re-layouts: 9.35 us -> 1.49 us
  Pallas kernels: 17.4 us -> 23.1 us
    unnamed x26 -> x12, local copies, waits for them, and re-layouts: 9.27 us -> 1.41 us
    pallas_call x1, Pallas kernels: 3.84 us -> 7.25 us  [weight_images(): pl.pallas_call(weight_kernel, in_specs=[pl.BlockSpec(memory_space=pltpu.S...]
    all_gather x1, blocking collectives: 19.7 us -> 21.9 us  [on_device(): lax.all_gather(post_bf, 'grp', axis=0, axis_index_groups=z_groups)]
    ppermute x3, waiting for transfers between devices: 6.93 us -> 5.02 us  [on_device(): post[d] = lax.ppermute(post[0], 'grp', grp_shift(d))]
    pallas_call x1, Pallas kernels: 0.84 us -> 2.46 us  [posterior(): pl.pallas_call(posterior_kernel, in_specs=[pl.BlockSpec(memory_space=pltp...]
    all_gather x1, waiting for transfers between devices: 0.02 us -> 1.64 us  [on_device(): proj = lax.all_gather(proj_z, 'grp', axis=0, axis_index_groups=x_groups)]
  transfers between devices with their start and end apart: 10 -> 10, of which waited for: 4 -> 5; matrix products, arithmetic and copies ran while one was open for 3% -> 4% of each run, Pallas kernels for 9% -> 13%
where the time goes in v3:
time: 156 us
  blocking collectives  73.6 us (47%)
  starting transfers between devices  28.2 us (18%)
  Pallas kernels  23.1 us (15%)
  between operations  14.3 us (9%)
  waiting for transfers between devices  9.18 us (6%)
  other arithmetic  4.8 us (3%)
    all_gather x1, blocking collectives, on_device(): lax.all_gather(projections, 'grp', axis=0, axis_index_groups=z_groups)  35.2 us
    all_gather x1, blocking collectives, on_device(): lax.all_gather(post_bf, 'grp', axis=0, axis_index_groups=z_groups)  21.9 us
    all_to_all x1, blocking collectives, exchange(): return lax.all_to_all(copies, axis, 0, 0, axis_index_groups=groups)  16.5 us
    ppermute x3, starting transfers between devices, on_device(): block = lax.ppermute(share, 'pose', pose_shift(0, d, 0))  15.4 us
    ppermute x3, starting transfers between devices, on_device(): post[d] = lax.ppermute(post[0], 'grp', grp_shift(d))  10.1 us
    pallas_call x2, Pallas kernels, back_project(): pl.pallas_call(functools.partial(back_kernel, sources, ahead, width), in_...  8.08 us
    pallas_call x1, Pallas kernels, weight_images(): pl.pallas_call(weight_kernel, in_specs=[pl.BlockSpec(memory_space=pltpu.S...  7.25 us
    pallas_call x1, Pallas kernels, score(): pl.pallas_call(score_kernel, in_specs=[pl.BlockSpec(memory_space=pltpu.SM...  5.31 us
  transfers between devices with their start and end apart: 10, of which 5 were waited for; matrix products, arithmetic and copies ran while one was open for 4% of the time, Pallas kernels for 13%

profile of v3, /device:TPU:6, one launch (start us, length us, event | category | flops | bytes accessed | tf_op | source)
XLA Modules:
  0.0 155.5 jit_solution(5257256006378895628)
XLA Ops:
  7.2 35.2 %all-gather = bf16[8,128,256]{2,1,0:T(8,128)(2,1)} all-gather(bf16[2,128,256]{2,1,0:T(8,128)(2,1)} %param.9), channel_id=2, replica_groups={{0,32,64,96},{128,160,192,224},{256,288,320,352},{384,416,448,480},{1,3..., dimensions={0}, use_global_device_ids=true | all-gather | bytes 655360 | tf_op jit(solution)/shard_map/gather_projections/all_gather | solution.py:404
  43.8 0.9 multiply_convert_fusion
  45.5 0.8 broadcast_multiply_fusion
  46.3 1.7 %fusion.1 = (f32[256,256]{1,0:T(8,128)}, f32[256,256]{1,0:T(8,128)}) fusion(f32[256,128]{1,0:T(8,128)S(1)} %get-tuple-element.43, f32[256,128]{1,0:T(8,128)S(1)} %get-tuple-element.42), kind=kLoop, calls=%fused_computation.4 | loop fusion | flops 65536 | bytes 786432 | tf_op jit(solution)/shard_map/weights/cos | solution.py:173
  47.9 7.3 %weight_images.1 = (bf16[2,256,4096]{2,1,0:T(8,128)(2,1)}, bf16[256,4096]{1,0:T(8,128)(2,1)}, f32[128,256]{1,0:T(8,128)}) custom-call(s32[1]{0:T(128)} %bitcast.1.x_ref, bf16[2,256,4096]{2,1,0:T(8,128)(2,1)} %images_hbm.1, f32[256,256]{1,0:T(8,128)} %get-tuple-element.41.sin_ref, f32[256,256]{1,0:T(8,128)} %get-tuple-element.40.cos_ref, f32[1,4096]{1,0:T(1,128)} %bitcast.32, ...), custom_call_target="tpu_custom_call" | custom-call | flops 1 | bytes 1 | tf_op jit(solution)/shard_map/weights/weight_images/pallas_call | solution.py:154
  55.3 0.9 fusion.bias_ref
  56.2 6.1 %collective-permute-start.1 = (bf16[272,256]{1,0:T(8,128)(2,1)S(1)}, bf16[272,256]{1,0:T(8,128)(2,1)S(1)}, u32[]{:S(2)}, u32[]{:S(2)}) collective-permute-start(bf16[272,256]{1,0:T(8,128)(2,1)S(1)} %collective-permute-done), channel_id=1, source_target_pairs={{0,2},{1,3},{2,4},{3,5},{4,6},{5,7},{6,0},{7,1},{8,10},{9,11},{10,... | collective-permute-start | bytes 417800 | tf_op jit(solution)/shard_map/gather_images/ppermute | solution.py:436
  62.3 4.5 %collective-permute-start.2 = (bf16[272,256]{1,0:T(8,128)(2,1)S(1)}, bf16[272,256]{1,0:T(8,128)(2,1)S(1)}, u32[]{:S(2)}, u32[]{:S(2)}) collective-permute-start(bf16[272,256]{1,0:T(8,128)(2,1)S(1)} %collective-permute-done), channel_id=1, source_target_pairs={{0,4},{1,5},{2,6},{3,7},{4,0},{5,1},{6,2},{7,3},{8,12},{9,13},{10,... | collective-permute-start | bytes 417800 | tf_op jit(solution)/shard_map/gather_images/ppermute | solution.py:436
  66.8 4.8 %collective-permute-start.3 = (bf16[272,256]{1,0:T(8,128)(2,1)S(1)}, bf16[272,256]{1,0:T(8,128)(2,1)S(1)}, u32[]{:S(2)}, u32[]{:S(2)}) collective-permute-start(bf16[272,256]{1,0:T(8,128)(2,1)S(1)} %collective-permute-done), channel_id=1, source_target_pairs={{0,6},{1,7},{2,0},{3,1},{4,2},{5,3},{6,4},{7,5},{8,14},{9,15},{10,... | collective-permute-start | bytes 417800 | tf_op jit(solution)/shard_map/gather_images/ppermute | solution.py:436
  71.8 1.5 collective-permute-done.2
  73.3 1.0 collective-permute-done.3
  74.3 1.6 %all-gather.7.cloned.1.call-done = bf16[16,2,128,256]{3,2,1,0:T(8,128)(2,1)} async-done(((bf16[4,2,128,256]{3,2,1,0:T(8,128)(2,1)}), bf16[16,2,128,256]{3,2,1,0:T(8,128)(2,1)}) %all-gather.7.cloned.1.call-update) | async-done | bytes 2097168 | tf_op jit(solution)/shard_map/gather_projections/all_gather | solution.py:406
  75.9 5.3 %score.1 = (f32[128,256]{1,0:T(8,128)}, f32[32,1,256]{2,1,0:T(1,128)}) custom-call(s32[1]{0:T(128)} %bitcast.1.x_ref, bf16[4,4,2,128,256]{4,3,2,1,0:T(8,128)(2,1)} %bitcast.30, bf16[2,256,4096]{2,1,0:T(8,128)(2,1)} %get-tuple-element.25.weighted_hbm, bf16[256,4096]{1,0:T(8,128)(2,1)} %get-tuple-element.26.noise_hbm, f32[128,256]{1,0:T(8,128)} %get-tuple-element.27.part_ref, ...), custom_call_target="tpu_custom_call" | custom-call | flops 1 | bytes 1 | tf_op jit(solution)/shard_map/scores/score/pallas_call | solution.py:212
  81.3 16.5 %all_to_all.5.log_sums_ref = f32[32,1,256]{2,1,0:T(1,128)} all-to-all(f32[32,1,256]{2,1,0:T(1,128)} %get-tuple-element.30), channel_id=1, replica_groups=mesh['grp'=16,'pose'=32] {'pose'}, dimensions={0} | all-to-all | bytes 65536 | tf_op jit(solution)/shard_map/softmax/all_to_all | solution.py:381
  97.8 2.5 %posterior.1 = (f32[256,128]{1,0:T(8,128)}, bf16[128,256]{1,0:T(8,128)(2,1)}) custom-call(s32[1]{0:T(128)} %bitcast.core_ref, f32[128,256]{1,0:T(8,128)} %get-tuple-element.29.scores_hbm, f32[32,1,256]{2,1,0:T(1,128)} %all_to_all.5.log_sums_ref), custom_call_target="tpu_custom_call" | custom-call | flops 1 | bytes 1 | tf_op jit(solution)/shard_map/softmax/posterior/pallas_call | solution.py:250
  100.2 21.9 %all-gather.2 = bf16[512,256]{1,0:T(8,128)(2,1)S(1)} all-gather(bf16[128,256]{1,0:T(8,128)(2,1)} %get-tuple-element.32), channel_id=4, replica_groups={{0,32,64,96},{128,160,192,224},{256,288,320,352},{384,416,448,480},{1,3..., dimensions={0}, use_global_device_ids=true | all-gather | bytes 327680 | tf_op jit(solution)/shard_map/gather_posteriors/all_gather | solution.py:448
  122.1 1.9 %collective-permute-start.6 = (bf16[4,4,272,256]{3,2,1,0:T(8,128)(2,1)}, bf16[4,4,272,256]{3,2,1,0:T(8,128)(2,1)S(1)}, u32[]{:S(2)}, u32[]{:S(2)}) collective-permute-start(bf16[4,4,272,256]{3,2,1,0:T(8,128)(2,1)} %bitcast.25), channel_id=1, source_target_pairs={{0,1},{1,0},{2,3},{3,2},{4,5},{5,4},{6,7},{7,6},{8,9},{9,8},{10,11... | collective-permute-start | bytes 6684680 | tf_op jit(solution)/shard_map/gather_posteriors/ppermute | solution.py:452
  124.0 4.3 %collective-permute-start.7 = (bf16[4,128,256]{2,1,0:T(8,128)(2,1)S(1)}, bf16[4,128,256]{2,1,0:T(8,128)(2,1)S(1)}, u32[]{:S(2)}, u32[]{:S(2)}) collective-permute-start(bf16[4,128,256]{2,1,0:T(8,128)(2,1)S(1)} %bitcast.21), channel_id=1, source_target_pairs={{0,128},{32,160},{64,192},{96,224},{128,256},{160,288},{192,320},{... | collective-permute-start | bytes 786440 | tf_op jit(solution)/shard_map/gather_posteriors/ppermute | solution.py:450
  128.3 1.9 %collective-permute-start.4 = (bf16[4,128,256]{2,1,0:T(8,128)(2,1)S(1)}, bf16[4,128,256]{2,1,0:T(8,128)(2,1)S(1)}, u32[]{:S(2)}, u32[]{:S(2)}) collective-permute-start(bf16[4,128,256]{2,1,0:T(8,128)(2,1)S(1)} %bitcast.22), channel_id=1, source_target_pairs={{0,384},{32,416},{64,448},{96,480},{128,0},{160,32},{192,64},{224,... | collective-permute-start | bytes 786440 | tf_op jit(solution)/shard_map/gather_posteriors/ppermute | solution.py:450
  130.3 3.9 %collective-permute-start.5 = (bf16[4,128,256]{2,1,0:T(8,128)(2,1)S(1)}, bf16[4,128,256]{2,1,0:T(8,128)(2,1)S(1)}, u32[]{:S(2)}, u32[]{:S(2)}) collective-permute-start(bf16[4,128,256]{2,1,0:T(8,128)(2,1)S(1)} %bitcast.23), channel_id=1, source_target_pairs={{0,256},{32,288},{64,320},{96,352},{128,384},{160,416},{192,448},{... | collective-permute-start | bytes 786440 | tf_op jit(solution)/shard_map/gather_posteriors/ppermute | solution.py:450
  134.6 1.4 copy-done
  136.0 4.9 %back_project.2 = (f32[3,128,256]{2,1,0:T(8,128)S(1)}, bf16[2,256,1024]{2,1,0:T(8,128)(2,1)S(1)}) custom-call(s32[1]{0:T(128)} %bitcast.12.start_ref, bf16[4,128,256]{2,1,0:T(8,128)(2,1)S(1)} %bitcast.24, bf16[4,128,256]{2,1,0:T(8,128)(2,1)S(1)} %collective-permute-done.7.refs_1_, bf16[4,4,272,256]{3,2,1,0:T(8,128)(2,1)} %bitcast.26, ...), custom_call_target="tpu_custom_call" | custom-call | flops 1 | bytes 1 | tf_op jit(solution)/shard_map/back_project/back_project/pallas_call | solution.py:364
  140.9 4.5 %collective-permute-done.4.refs_0_ = bf16[4,128,256]{2,1,0:T(8,128)(2,1)S(1)} collective-permute-done((bf16[4,128,256]{2,1,0:T(8,128)(2,1)S(1)}, bf16[4,128,256]{2,1,0:T(8,128)(2,1)S(1)}, u32[]{:S(2)}, u32[]{:S(2)}) %collective-permute-start.4) | collective-permute-done | bytes 262176 | tf_op jit(solution)/shard_map/gather_posteriors/ppermute | solution.py:450
  145.5 3.2 %back_project.3 = f32[3,128,256]{2,1,0:T(8,128)} custom-call(s32[1]{0:T(128)} %bitcast.12.start_ref, bf16[4,128,256]{2,1,0:T(8,128)(2,1)S(1)} %collective-permute-done.4.refs_0_, bf16[4,128,256]{2,1,0:T(8,128)(2,1)S(1)} %collective-permute-done.5.refs_1_, bf16[4,4,272,256]{3,2,1,0:T(8,128)(2,1)} %bitcast.27, bf16[4,4,272,256]{3,2,1,0:T(8,128)(2,1)} %copy-done, ...), custom_call_target="tpu_custom_call" | custom-call | flops 1 | bytes 1 | tf_op jit(solution)/shard_map/back_project/back_project/pallas_call | solution.py:364
  (34 shorter events, 2.8 us)
Async XLA Ops:
  7.2 68.7 %all-gather.7.cloned.1.call-start = ((), (), s32[]{:S(2)}) async-start(), calls=%async_computation.1 | async-start | bytes 2621440 | tf_op jit(solution)/shard_map/gather_projections/all_gather | solution.py:406
  42.4 79.7 %all-gather.9.cloned.1.call-start = ((), (), s32[]{:S(2)}) async-start(), calls=%async_computation.2 | async-start | bytes 2785280 | tf_op jit(solution)/shard_map/gather_images/all_gather | solution.py:439
  44.8 11.4 %collective-permute-start = (bf16[272,256]{1,0:T(8,128)(2,1)S(1)}, bf16[272,256]{1,0:T(8,128)(2,1)S(1)}, u32[]{:S(2)}, u32[]{:S(2)}) collective-permute-start(bf16[272,256]{1,0:T(8,128)(2,1)S(1)} %pad_maximum_fusion.1), channel_id=1, source_target_pairs={{0,0},{1,1},{2,34},{3,35},{4,68},{5,69},{6,102},{7,103},{8,136},{9... | collective-permute-start | bytes 417800 | tf_op jit(solution)/shard_map/exchange_images/ppermute | solution.py:417
  47.9 7.3 %copy-start.4 = (f32[64]{0:T(128)S(1)}, f32[64]{0:T(128)}, u32[]{:S(2)}) copy-start(f32[64]{0:T(128)} %param.12) | copy-start | bytes 772
  47.9 7.3 %copy-start.5 = (s32[128]{0:T(128)S(1)}, s32[128]{0:T(128)}, u32[]{:S(2)}) copy-start(s32[128]{0:T(128)} %param.13) | copy-start | bytes 1540
  47.9 7.4 %copy-start.2 = (s32[256,256]{1,0:T(8,128)S(1)}, s32[256,256]{1,0:T(8,128)}, u32[]{:S(2)}) copy-start(s32[256,256]{1,0:T(8,128)} %param.15) | copy-start | bytes 786436
  47.9 7.4 %copy-start.3 = (s32[128]{0:T(128)S(1)}, s32[128]{0:T(128)}, u32[]{:S(2)}) copy-start(s32[128]{0:T(128)} %param.14) | copy-start | bytes 1540
  56.2 15.5 %collective-permute-start.1 = (bf16[272,256]{1,0:T(8,128)(2,1)S(1)}, bf16[272,256]{1,0:T(8,128)(2,1)S(1)}, u32[]{:S(2)}, u32[]{:S(2)}) collective-permute-start(bf16[272,256]{1,0:T(8,128)(2,1)S(1)} %collective-permute-done), channel_id=1, source_target_pairs={{0,2},{1,3},{2,4},{3,5},{4,6},{5,7},{6,0},{7,1},{8,10},{9,11},{10,... | collective-permute-start | bytes 417800 | tf_op jit(solution)/shard_map/gather_images/ppermute | solution.py:436
  62.3 11.0 %collective-permute-start.2 = (bf16[272,256]{1,0:T(8,128)(2,1)S(1)}, bf16[272,256]{1,0:T(8,128)(2,1)S(1)}, u32[]{:S(2)}, u32[]{:S(2)}) collective-permute-start(bf16[272,256]{1,0:T(8,128)(2,1)S(1)} %collective-permute-done), channel_id=1, source_target_pairs={{0,4},{1,5},{2,6},{3,7},{4,0},{5,1},{6,2},{7,3},{8,12},{9,13},{10,... | collective-permute-start | bytes 417800 | tf_op jit(solution)/shard_map/gather_images/ppermute | solution.py:436
  66.8 7.4 %collective-permute-start.3 = (bf16[272,256]{1,0:T(8,128)(2,1)S(1)}, bf16[272,256]{1,0:T(8,128)(2,1)S(1)}, u32[]{:S(2)}, u32[]{:S(2)}) collective-permute-start(bf16[272,256]{1,0:T(8,128)(2,1)S(1)} %collective-permute-done), channel_id=1, source_target_pairs={{0,6},{1,7},{2,0},{3,1},{4,2},{5,3},{6,4},{7,5},{8,14},{9,15},{10,... | collective-permute-start | bytes 417800 | tf_op jit(solution)/shard_map/gather_images/ppermute | solution.py:436
  74.3 1.6 %copy-start.1 = (bf16[4,272,256]{2,1,0:T(8,128)(2,1)}, bf16[4,272,256]{2,1,0:T(8,128)(2,1)S(1)}, u32[]{:S(2)}) copy-start(bf16[4,272,256]{2,1,0:T(8,128)(2,1)S(1)} %bitcast_dynamic-update-slice_fusion) | copy-start | bytes 1671172
  122.1 12.5 %collective-permute-start.6 = (bf16[4,4,272,256]{3,2,1,0:T(8,128)(2,1)}, bf16[4,4,272,256]{3,2,1,0:T(8,128)(2,1)S(1)}, u32[]{:S(2)}, u32[]{:S(2)}) collective-permute-start(bf16[4,4,272,256]{3,2,1,0:T(8,128)(2,1)} %bitcast.25), channel_id=1, source_target_pairs={{0,1},{1,0},{2,3},{3,2},{4,5},{5,4},{6,7},{7,6},{8,9},{9,8},{10,11... | collective-permute-start | bytes 6684680 | tf_op jit(solution)/shard_map/gather_posteriors/ppermute | solution.py:452
  124.0 10.6 %collective-permute-start.7 = (bf16[4,128,256]{2,1,0:T(8,128)(2,1)S(1)}, bf16[4,128,256]{2,1,0:T(8,128)(2,1)S(1)}, u32[]{:S(2)}, u32[]{:S(2)}) collective-permute-start(bf16[4,128,256]{2,1,0:T(8,128)(2,1)S(1)} %bitcast.21), channel_id=1, source_target_pairs={{0,128},{32,160},{64,192},{96,224},{128,256},{160,288},{192,320},{... | collective-permute-start | bytes 786440 | tf_op jit(solution)/shard_map/gather_posteriors/ppermute | solution.py:450
  128.3 17.2 %collective-permute-start.4 = (bf16[4,128,256]{2,1,0:T(8,128)(2,1)S(1)}, bf16[4,128,256]{2,1,0:T(8,128)(2,1)S(1)}, u32[]{:S(2)}, u32[]{:S(2)}) collective-permute-start(bf16[4,128,256]{2,1,0:T(8,128)(2,1)S(1)} %bitcast.22), channel_id=1, source_target_pairs={{0,384},{32,416},{64,448},{96,480},{128,0},{160,32},{192,64},{224,... | collective-permute-start | bytes 786440 | tf_op jit(solution)/shard_map/gather_posteriors/ppermute | solution.py:450
  130.3 15.2 %collective-permute-start.5 = (bf16[4,128,256]{2,1,0:T(8,128)(2,1)S(1)}, bf16[4,128,256]{2,1,0:T(8,128)(2,1)S(1)}, u32[]{:S(2)}, u32[]{:S(2)}) collective-permute-start(bf16[4,128,256]{2,1,0:T(8,128)(2,1)S(1)} %bitcast.23), channel_id=1, source_target_pairs={{0,256},{32,288},{64,320},{96,352},{128,384},{160,416},{192,448},{... | collective-permute-start | bytes 786440 | tf_op jit(solution)/shard_map/gather_posteriors/ppermute | solution.py:450
  134.6 1.4 copy-start
Sparse Core Ops, SparseCore 0:
  42.6 33.2 all-gather.6
  78.0 41.5 all-gather.8

commit v4 on v3

--- a/solution.py
+++ b/solution.py
@@ -13,9 +13,8 @@
 NY, NZL, NC = 4, 4, 2
 LANES = 128
 TERM_ROWS = 16
-VMEM_LIMIT = 20 << 20
 MOST_VMEM = 63 << 20
-BACK_VMEM = 52 << 20
+BACK_VMEM = 20 << 20
 WEIGHT_VMEM = 60 << 20
 SMALL_COST = pl.CostEstimate(flops=1, bytes_accessed=1, transcendentals=0)
 INTERPRET = False
@@ -290,91 +289,60 @@
 
 
 def back_kernel(sources, ahead, width, start_ref, *refs):
-    n_s, last = len(sources), not ahead
-    posts, hbm = refs[:n_s], refs[n_s : n_s + 2]
+    last = not ahead
+    n_s = len(sources)
+    posts, images = refs[:n_s], refs[n_s : n_s + 2]
     if last:
-        before_ref, squares_ref, out_ref, own_ref, other_ref, sems = refs[n_s + 2 :]
+        before_ref, squares_ref, out_ref = refs[n_s + 2 :]
     else:
-        out_ref, squares_ref, own_ref, other_ref, terms_ref, sems = refs[n_s + 2 :]
+        out_ref, squares_ref = refs[n_s + 2 :]
     n_z, _, n = posts[0].shape
     slab, half = out_ref.shape[2], n // NC
 
-    def copies(i):
-        return [
-            pltpu.make_async_copy(src.at[sources[i]], dst.at[i], sems.at[i, j])
-            for j, (src, dst) in enumerate(zip(hbm, (own_ref, other_ref)))
-        ]
-
-    def term_copies(i):
-        return [
-            pltpu.make_async_copy(
-                src.at[ahead[i], :, pl.ds(n, TERM_ROWS), :], terms_ref.at[i, j], sems.at[n_s + i, j]
-            )
-            for j, src in enumerate(hbm)
-        ]
-
-    for i in range(n_s):
-        for copy in copies(i):
-            copy.start()
-    for i in range(len(ahead)):
-        for copy in term_copies(i):
-            copy.start()
+    def stacked(source, first, size):
+        rows = slice(first, first + size)
+        return [ref[source, t, rows] for t in range(n_z) for ref in images]
+
     if not last:
         pixel = start_ref[0] + lax.broadcasted_iota(jnp.int32, (slab, half), 0)
         freq2 = (pixel.astype(jnp.float32) + 0.5) * (1.0 / width)
-    for i in range(n_s):
-        for copy in copies(i):
-            copy.wait()
-        stacks = [stack[i, t] for t in range(n_z) for stack in (own_ref, other_ref)]
+    for i, source in enumerate(sources):
         post = jnp.concatenate([posts[i][t] for t in range(n_z)], axis=1)
-        if last:
-            square = squares_ref[i]
-        else:
-            square = squares_of([stack[n : n + TERM_ROWS] for stack in stacks], freq2)
         for c in range(3):
             if c < 2:
-                images = [stack[c * half : (c + 1) * half] for stack in stacks]
-                total = jnp.dot(
-                    post, jnp.concatenate(images, axis=0), preferred_element_type=jnp.float32
-                )
+                image = jnp.concatenate(stacked(source, c * half, half), axis=0)
+                total = jnp.dot(post, image, preferred_element_type=jnp.float32)
+            elif last:
+                total = dot_nt(post, squares_ref[i])
             else:
-                total = dot_nt(post, square)
+                total = dot_nt(post, squares_of(stacked(source, n, TERM_ROWS), freq2))
             if i > 0:
                 total += out_ref[c]
             elif last:
                 total += before_ref[c]
             out_ref[c] = total
-    for i in range(len(ahead)):
-        for copy in term_copies(i):
-            copy.wait()
-        stacks = [terms_ref[i, j, t] for t in range(n_z) for j in range(2)]
-        squares_ref[i] = squares_of(stacks, freq2)
-
-
-def back_project(start, width, sources, posts, stacks, ahead=(), before=()):
-    n_s, (n_z, rows, n) = len(sources), posts[0].shape
-    slab = stacks[0].shape[3]
-    in_hbm, in_vmem = pl.BlockSpec(memory_space=pl.ANY), pl.BlockSpec(memory_space=pltpu.VMEM)
+    for i, source in enumerate(ahead):
+        squares_ref[i] = squares_of(stacked(source, n, TERM_ROWS), freq2)
+
+
+def back_project(start, width, sources, posts, images, ahead=(), before=()):
+    n_z, rows, n = posts[0].shape
+    slab = images[0].shape[3]
+    in_vmem = pl.BlockSpec(memory_space=pltpu.VMEM)
     out_shape = [jax.ShapeDtypeStruct((3, rows, slab), jnp.float32)]
-    scratch = [pltpu.VMEM((n_s,) + stack.shape[1:], jnp.bfloat16) for stack in stacks]
     if ahead:
-        n_a = len(ahead)
-        out_shape.append(jax.ShapeDtypeStruct((n_a, slab, n_z * n), jnp.bfloat16))
-        scratch.append(pltpu.VMEM((n_a, NC, n_z, TERM_ROWS, slab), jnp.bfloat16))
+        out_shape.append(jax.ShapeDtypeStruct((len(ahead), slab, n_z * n), jnp.bfloat16))
     return pl.pallas_call(
         functools.partial(back_kernel, sources, ahead, width),
         in_specs=[pl.BlockSpec(memory_space=pltpu.SMEM)]
-        + [in_vmem] * n_s
-        + [in_hbm] * 2
-        + [in_vmem] * len(before),
+        + [in_vmem] * (len(sources) + 2 + len(before)),
         out_specs=[in_vmem] * len(out_shape),
         out_shape=out_shape,
-        scratch_shapes=scratch + [pltpu.SemaphoreType.DMA((n_s + len(ahead), 2))],
         cost_estimate=SMALL_COST,
         compiler_params=pltpu.CompilerParams(vmem_limit_bytes=BACK_VMEM),
         interpret=INTERPRET,
         name="back_project",
-    )(start[None], *posts, *stacks, *before)
+    )(start[None], *posts, *images, *before)
 
 
 def exchange(copies, axis, groups=None):
@@ -452,8 +420,8 @@
         other = lax.ppermute(own, "pose", pose_shift(0, 0, 1))
 
     with jax.named_scope("back_project"):
-        start, stacks = group * slab, (own, other)
-        near, far = (0, 1), (3, 2)
+        start = group * slab
+        near, far, stacks = (0,), (1, 3, 2), (own, other)
         before = back_project(start, width, near, [post[d] for d in near], stacks, ahead=far)
         (back_proj,) = back_project(start, width, far, [post[d] for d in far], stacks, before=before)
     return (posteriors, back_proj)

time: 156 us -> 155 us (level)
  Pallas kernels: 23.1 us -> 20.2 us
    pallas_call x2, Pallas kernels: 8.08 us -> 5.23 us  [back_project(): pl.pallas_call(functools.partial(back_kernel, sources, ahead, width), in_...]
  transfers between devices with their start and end apart: 10 -> 10, of which waited for: 5 -> 4; matrix products, arithmetic and copies ran while one was open for 4% -> 4% of each run, Pallas kernels for 13% -> 12%
where the time goes in v4:
time: 155 us; the launch traced here: 154 us
  blocking collectives  73.6 us (47%)
  starting transfers between devices  28.1 us (18%)
  Pallas kernels  20.2 us (13%)
  between operations  14.3 us (9%)
  waiting for transfers between devices  10.6 us (7%)
  other arithmetic  4.79 us (3%)
  local copies, waits for them, and re-layouts  1.72 us (1%)
    all_gather x1, blocking collectives, on_device(): lax.all_gather(projections, 'grp', axis=0, axis_index_groups=z_groups)  35.2 us
    all_gather x1, blocking collectives, on_device(): lax.all_gather(post_bf, 'grp', axis=0, axis_index_groups=z_groups)  21.9 us
    all_to_all x1, blocking collectives, exchange(): return lax.all_to_all(copies, axis, 0, 0, axis_index_groups=groups)  16.5 us
    ppermute x3, starting transfers between devices, on_device(): block = lax.ppermute(share, 'pose', pose_shift(0, d, 0))  15.4 us
    ppermute x3, starting transfers between devices, on_device(): post[d] = lax.ppermute(post[0], 'grp', grp_shift(d))  10.1 us
    pallas_call x1, Pallas kernels, weight_images(): pl.pallas_call(weight_kernel, in_specs=[pl.BlockSpec(memory_space=pltpu.S...  7.25 us
    ppermute x3, waiting for transfers between devices, on_device(): post[d] = lax.ppermute(post[0], 'grp', grp_shift(d))  6.44 us
    pallas_call x1, Pallas kernels, score(): pl.pallas_call(score_kernel, in_specs=[pl.BlockSpec(memory_space=pltpu.SM...  5.3 us
  transfers between devices with their start and end apart: 10, of which 4 were waited for; matrix products, arithmetic and copies ran while one was open for 4% of the time, Pallas kernels for 12%

profile of v4, /device:TPU:6, one launch (start us, length us, event | category | flops | bytes accessed | tf_op | source)
XLA Modules:
  0.0 154.3 jit_solution(16119453579085737495)
XLA Ops:
  7.2 35.2 %all-gather = bf16[8,128,256]{2,1,0:T(8,128)(2,1)} all-gather(bf16[2,128,256]{2,1,0:T(8,128)(2,1)} %param.9), channel_id=2, replica_groups={{0,32,64,96},{128,160,192,224},{256,288,320,352},{384,416,448,480},{1,3..., dimensions={0}, use_global_device_ids=true | all-gather | bytes 655360 | tf_op jit(solution)/shard_map/gather_projections/all_gather | solution.py:372
  43.8 0.9 multiply_convert_fusion
  45.5 0.8 broadcast_multiply_fusion
  46.3 1.6 %fusion.1 = (f32[256,256]{1,0:T(8,128)}, f32[256,256]{1,0:T(8,128)}) fusion(f32[256,128]{1,0:T(8,128)S(1)} %get-tuple-element.43, f32[256,128]{1,0:T(8,128)S(1)} %get-tuple-element.42), kind=kLoop, calls=%fused_computation.4 | loop fusion | flops 65536 | bytes 786432 | tf_op jit(solution)/shard_map/weights/cos | solution.py:172
  47.9 7.2 %weight_images.1 = (bf16[2,256,4096]{2,1,0:T(8,128)(2,1)}, bf16[256,4096]{1,0:T(8,128)(2,1)}, f32[128,256]{1,0:T(8,128)}) custom-call(s32[1]{0:T(128)} %bitcast.1.x_ref, bf16[2,256,4096]{2,1,0:T(8,128)(2,1)} %images_hbm.1, f32[256,256]{1,0:T(8,128)} %get-tuple-element.41.sin_ref, f32[256,256]{1,0:T(8,128)} %get-tuple-element.40.cos_ref, f32[1,4096]{1,0:T(1,128)} %bitcast.32, ...), custom_call_target="tpu_custom_call" | custom-call | flops 1 | bytes 1 | tf_op jit(solution)/shard_map/weights/weight_images/pallas_call | solution.py:153
  55.3 0.9 fusion.bias_ref
  56.2 6.1 %collective-permute-start.1 = (bf16[272,256]{1,0:T(8,128)(2,1)S(1)}, bf16[272,256]{1,0:T(8,128)(2,1)S(1)}, u32[]{:S(2)}, u32[]{:S(2)}) collective-permute-start(bf16[272,256]{1,0:T(8,128)(2,1)S(1)} %collective-permute-done), channel_id=1, source_target_pairs={{0,2},{1,3},{2,4},{3,5},{4,6},{5,7},{6,0},{7,1},{8,10},{9,11},{10,... | collective-permute-start | bytes 417800 | tf_op jit(solution)/shard_map/gather_images/ppermute | solution.py:404
  62.3 4.5 %collective-permute-start.2 = (bf16[272,256]{1,0:T(8,128)(2,1)S(1)}, bf16[272,256]{1,0:T(8,128)(2,1)S(1)}, u32[]{:S(2)}, u32[]{:S(2)}) collective-permute-start(bf16[272,256]{1,0:T(8,128)(2,1)S(1)} %collective-permute-done), channel_id=1, source_target_pairs={{0,4},{1,5},{2,6},{3,7},{4,0},{5,1},{6,2},{7,3},{8,12},{9,13},{10,... | collective-permute-start | bytes 417800 | tf_op jit(solution)/shard_map/gather_images/ppermute | solution.py:404
  66.8 4.8 %collective-permute-start.3 = (bf16[272,256]{1,0:T(8,128)(2,1)S(1)}, bf16[272,256]{1,0:T(8,128)(2,1)S(1)}, u32[]{:S(2)}, u32[]{:S(2)}) collective-permute-start(bf16[272,256]{1,0:T(8,128)(2,1)S(1)} %collective-permute-done), channel_id=1, source_target_pairs={{0,6},{1,7},{2,0},{3,1},{4,2},{5,3},{6,4},{7,5},{8,14},{9,15},{10,... | collective-permute-start | bytes 417800 | tf_op jit(solution)/shard_map/gather_images/ppermute | solution.py:404
  71.7 1.5 collective-permute-done.2
  73.3 1.0 collective-permute-done.3
  74.3 1.7 %all-gather.7.cloned.1.call-done = bf16[16,2,128,256]{3,2,1,0:T(8,128)(2,1)} async-done(((bf16[4,2,128,256]{3,2,1,0:T(8,128)(2,1)}), bf16[16,2,128,256]{3,2,1,0:T(8,128)(2,1)}) %all-gather.7.cloned.1.call-update) | async-done | bytes 2097168 | tf_op jit(solution)/shard_map/gather_projections/all_gather | solution.py:374
  75.9 5.3 %score.1 = (f32[128,256]{1,0:T(8,128)}, f32[32,1,256]{2,1,0:T(1,128)}) custom-call(s32[1]{0:T(128)} %bitcast.1.x_ref, bf16[4,4,2,128,256]{4,3,2,1,0:T(8,128)(2,1)} %bitcast.30, bf16[2,256,4096]{2,1,0:T(8,128)(2,1)} %get-tuple-element.25.weighted_hbm, bf16[256,4096]{1,0:T(8,128)(2,1)} %get-tuple-element.26.noise_hbm, f32[128,256]{1,0:T(8,128)} %get-tuple-element.27.part_ref, ...), custom_call_target="tpu_custom_call" | custom-call | flops 1 | bytes 1 | tf_op jit(solution)/shard_map/scores/score/pallas_call | solution.py:211
  81.2 16.5 %all_to_all.5.log_sums_ref = f32[32,1,256]{2,1,0:T(1,128)} all-to-all(f32[32,1,256]{2,1,0:T(1,128)} %get-tuple-element.30), channel_id=1, replica_groups=mesh['grp'=16,'pose'=32] {'pose'}, dimensions={0} | all-to-all | bytes 65536 | tf_op jit(solution)/shard_map/softmax/all_to_all | solution.py:349
  97.7 2.5 %posterior.1 = (f32[256,128]{1,0:T(8,128)}, bf16[128,256]{1,0:T(8,128)(2,1)}) custom-call(s32[1]{0:T(128)} %bitcast.core_ref, f32[128,256]{1,0:T(8,128)} %get-tuple-element.29.scores_hbm, f32[32,1,256]{2,1,0:T(1,128)} %all_to_all.5.log_sums_ref), custom_call_target="tpu_custom_call" | custom-call | flops 1 | bytes 1 | tf_op jit(solution)/shard_map/softmax/posterior/pallas_call | solution.py:249
  100.2 21.9 %all-gather.2 = bf16[512,256]{1,0:T(8,128)(2,1)S(1)} all-gather(bf16[128,256]{1,0:T(8,128)(2,1)} %get-tuple-element.32), channel_id=4, replica_groups={{0,32,64,96},{128,160,192,224},{256,288,320,352},{384,416,448,480},{1,3..., dimensions={0}, use_global_device_ids=true | all-gather | bytes 327680 | tf_op jit(solution)/shard_map/gather_posteriors/all_gather | solution.py:416
  122.1 1.9 %collective-permute-start.7 = (bf16[4,4,272,256]{3,2,1,0:T(8,128)(2,1)}, bf16[4,4,272,256]{3,2,1,0:T(8,128)(2,1)S(1)}, u32[]{:S(2)}, u32[]{:S(2)}) collective-permute-start(bf16[4,4,272,256]{3,2,1,0:T(8,128)(2,1)} %bitcast.21), channel_id=1, source_target_pairs={{0,1},{1,0},{2,3},{3,2},{4,5},{5,4},{6,7},{7,6},{8,9},{9,8},{10,11... | collective-permute-start | bytes 6684680 | tf_op jit(solution)/shard_map/gather_posteriors/ppermute | solution.py:420
  124.1 4.4 %collective-permute-start.4 = (bf16[4,128,256]{2,1,0:T(8,128)(2,1)S(1)}, bf16[4,128,256]{2,1,0:T(8,128)(2,1)S(1)}, u32[]{:S(2)}, u32[]{:S(2)}) collective-permute-start(bf16[4,128,256]{2,1,0:T(8,128)(2,1)S(1)} %bitcast.24), channel_id=1, source_target_pairs={{0,128},{32,160},{64,192},{96,224},{128,256},{160,288},{192,320},{... | collective-permute-start | bytes 786440 | tf_op jit(solution)/shard_map/gather_posteriors/ppermute | solution.py:418
  128.5 1.9 %collective-permute-start.5 = (bf16[4,128,256]{2,1,0:T(8,128)(2,1)S(1)}, bf16[4,128,256]{2,1,0:T(8,128)(2,1)S(1)}, u32[]{:S(2)}, u32[]{:S(2)}) collective-permute-start(bf16[4,128,256]{2,1,0:T(8,128)(2,1)S(1)} %bitcast.25), channel_id=1, source_target_pairs={{0,384},{32,416},{64,448},{96,480},{128,0},{160,32},{192,64},{224,... | collective-permute-start | bytes 786440 | tf_op jit(solution)/shard_map/gather_posteriors/ppermute | solution.py:418
  130.4 3.7 %collective-permute-start.6 = (bf16[4,128,256]{2,1,0:T(8,128)(2,1)S(1)}, bf16[4,128,256]{2,1,0:T(8,128)(2,1)S(1)}, u32[]{:S(2)}, u32[]{:S(2)}) collective-permute-start(bf16[4,128,256]{2,1,0:T(8,128)(2,1)S(1)} %bitcast.26), channel_id=1, source_target_pairs={{0,256},{32,288},{64,320},{96,352},{128,384},{160,416},{192,448},{... | collective-permute-start | bytes 786440 | tf_op jit(solution)/shard_map/gather_posteriors/ppermute | solution.py:418
  134.2 1.6 %copy-done = bf16[16,272,256]{2,1,0:T(8,128)(2,1)S(1)} copy-done((bf16[16,272,256]{2,1,0:T(8,128)(2,1)S(1)}, bf16[16,272,256]{2,1,0:T(8,128)(2,1)}, u32[]{:S(2)}) %copy-start) | copy-done | bytes 2228248
  135.8 3.4 %back_project.2 = (f32[3,128,256]{2,1,0:T(8,128)S(1)}, bf16[3,256,1024]{2,1,0:T(8,128)(2,1)S(1)}) custom-call(s32[1]{0:T(128)} %bitcast.12.start_ref, bf16[4,128,256]{2,1,0:T(8,128)(2,1)S(1)} %bitcast.27, bf16[4,4,272,256]{3,2,1,0:T(8,128)(2,1)S(1)} %bitcast.22, bf16[4,4,272,256]{3,2,1,0:T(8,128)(2,1)S(1)} %collective-permute-done.7.refs_2_.refs_4_), custom_call_target="tpu_custom_call" | custom-call | flops 1 | bytes 1 | tf_op jit(solution)/shard_map/back_project/back_project/pallas_call | solution.py:335
  139.2 6.4 %collective-permute-done.5.refs_1_ = bf16[4,128,256]{2,1,0:T(8,128)(2,1)S(1)} collective-permute-done((bf16[4,128,256]{2,1,0:T(8,128)(2,1)S(1)}, bf16[4,128,256]{2,1,0:T(8,128)(2,1)S(1)}, u32[]{:S(2)}, u32[]{:S(2)}) %collective-permute-start.5) | collective-permute-done | bytes 262176 | tf_op jit(solution)/shard_map/gather_posteriors/ppermute | solution.py:418
  145.6 1.8 %back_project.3 = f32[3,128,256]{2,1,0:T(8,128)} custom-call(s32[1]{0:T(128)} %bitcast.12.start_ref, bf16[4,128,256]{2,1,0:T(8,128)(2,1)S(1)} %collective-permute-done.4.refs_0_, bf16[4,128,256]{2,1,0:T(8,128)(2,1)S(1)} %collective-permute-done.5.refs_1_, bf16[4,128,256]{2,1,0:T(8,128)(2,1)S(1)} %collective-permute-done.6.refs_2_, ...), custom_call_target="tpu_custom_call" | custom-call | flops 1 | bytes 1 | tf_op jit(solution)/shard_map/back_project/back_project/pallas_call | solution.py:335
  (36 shorter events, 2.3 us)
Async XLA Ops:
  7.2 68.7 %all-gather.7.cloned.1.call-start = ((), (), s32[]{:S(2)}) async-start(), calls=%async_computation.1 | async-start | bytes 2621440 | tf_op jit(solution)/shard_map/gather_projections/all_gather | solution.py:374
  42.4 79.7 %all-gather.9.cloned.1.call-start = ((), (), s32[]{:S(2)}) async-start(), calls=%async_computation.2 | async-start | bytes 2785280 | tf_op jit(solution)/shard_map/gather_images/all_gather | solution.py:407
  44.8 11.4 %collective-permute-start = (bf16[272,256]{1,0:T(8,128)(2,1)S(1)}, bf16[272,256]{1,0:T(8,128)(2,1)S(1)}, u32[]{:S(2)}, u32[]{:S(2)}) collective-permute-start(bf16[272,256]{1,0:T(8,128)(2,1)S(1)} %pad_maximum_fusion.1), channel_id=1, source_target_pairs={{0,0},{1,1},{2,34},{3,35},{4,68},{5,69},{6,102},{7,103},{8,136},{9... | collective-permute-start | bytes 417800 | tf_op jit(solution)/shard_map/exchange_images/ppermute | solution.py:385
  47.9 7.3 %copy-start.5 = (f32[64]{0:T(128)S(1)}, f32[64]{0:T(128)}, u32[]{:S(2)}) copy-start(f32[64]{0:T(128)} %param.12) | copy-start | bytes 772
  47.9 7.3 %copy-start.6 = (s32[128]{0:T(128)S(1)}, s32[128]{0:T(128)}, u32[]{:S(2)}) copy-start(s32[128]{0:T(128)} %param.13) | copy-start | bytes 1540
  47.9 7.4 %copy-start.3 = (s32[256,256]{1,0:T(8,128)S(1)}, s32[256,256]{1,0:T(8,128)}, u32[]{:S(2)}) copy-start(s32[256,256]{1,0:T(8,128)} %param.15) | copy-start | bytes 786436
  47.9 7.4 %copy-start.4 = (s32[128]{0:T(128)S(1)}, s32[128]{0:T(128)}, u32[]{:S(2)}) copy-start(s32[128]{0:T(128)} %param.14) | copy-start | bytes 1540
  56.2 15.5 %collective-permute-start.1 = (bf16[272,256]{1,0:T(8,128)(2,1)S(1)}, bf16[272,256]{1,0:T(8,128)(2,1)S(1)}, u32[]{:S(2)}, u32[]{:S(2)}) collective-permute-start(bf16[272,256]{1,0:T(8,128)(2,1)S(1)} %collective-permute-done), channel_id=1, source_target_pairs={{0,2},{1,3},{2,4},{3,5},{4,6},{5,7},{6,0},{7,1},{8,10},{9,11},{10,... | collective-permute-start | bytes 417800 | tf_op jit(solution)/shard_map/gather_images/ppermute | solution.py:404
  62.3 11.0 %collective-permute-start.2 = (bf16[272,256]{1,0:T(8,128)(2,1)S(1)}, bf16[272,256]{1,0:T(8,128)(2,1)S(1)}, u32[]{:S(2)}, u32[]{:S(2)}) collective-permute-start(bf16[272,256]{1,0:T(8,128)(2,1)S(1)} %collective-permute-done), channel_id=1, source_target_pairs={{0,4},{1,5},{2,6},{3,7},{4,0},{5,1},{6,2},{7,3},{8,12},{9,13},{10,... | collective-permute-start | bytes 417800 | tf_op jit(solution)/shard_map/gather_images/ppermute | solution.py:404
  66.8 7.4 %collective-permute-start.3 = (bf16[272,256]{1,0:T(8,128)(2,1)S(1)}, bf16[272,256]{1,0:T(8,128)(2,1)S(1)}, u32[]{:S(2)}, u32[]{:S(2)}) collective-permute-start(bf16[272,256]{1,0:T(8,128)(2,1)S(1)} %collective-permute-done), channel_id=1, source_target_pairs={{0,6},{1,7},{2,0},{3,1},{4,2},{5,3},{6,4},{7,5},{8,14},{9,15},{10,... | collective-permute-start | bytes 417800 | tf_op jit(solution)/shard_map/gather_images/ppermute | solution.py:404
  74.2 1.7 %copy-start.2 = (bf16[4,272,256]{2,1,0:T(8,128)(2,1)}, bf16[4,272,256]{2,1,0:T(8,128)(2,1)S(1)}, u32[]{:S(2)}) copy-start(bf16[4,272,256]{2,1,0:T(8,128)(2,1)S(1)} %bitcast_dynamic-update-slice_fusion) | copy-start | bytes 1671172
  122.1 12.0 %collective-permute-start.7 = (bf16[4,4,272,256]{3,2,1,0:T(8,128)(2,1)}, bf16[4,4,272,256]{3,2,1,0:T(8,128)(2,1)S(1)}, u32[]{:S(2)}, u32[]{:S(2)}) collective-permute-start(bf16[4,4,272,256]{3,2,1,0:T(8,128)(2,1)} %bitcast.21), channel_id=1, source_target_pairs={{0,1},{1,0},{2,3},{3,2},{4,5},{5,4},{6,7},{7,6},{8,9},{9,8},{10,11... | collective-permute-start | bytes 6684680 | tf_op jit(solution)/shard_map/gather_posteriors/ppermute | solution.py:420
  124.1 15.1 %collective-permute-start.4 = (bf16[4,128,256]{2,1,0:T(8,128)(2,1)S(1)}, bf16[4,128,256]{2,1,0:T(8,128)(2,1)S(1)}, u32[]{:S(2)}, u32[]{:S(2)}) collective-permute-start(bf16[4,128,256]{2,1,0:T(8,128)(2,1)S(1)} %bitcast.24), channel_id=1, source_target_pairs={{0,128},{32,160},{64,192},{96,224},{128,256},{160,288},{192,320},{... | collective-permute-start | bytes 786440 | tf_op jit(solution)/shard_map/gather_posteriors/ppermute | solution.py:418
  128.5 17.2 %collective-permute-start.5 = (bf16[4,128,256]{2,1,0:T(8,128)(2,1)S(1)}, bf16[4,128,256]{2,1,0:T(8,128)(2,1)S(1)}, u32[]{:S(2)}, u32[]{:S(2)}) collective-permute-start(bf16[4,128,256]{2,1,0:T(8,128)(2,1)S(1)} %bitcast.25), channel_id=1, source_target_pairs={{0,384},{32,416},{64,448},{96,480},{128,0},{160,32},{192,64},{224,... | collective-permute-start | bytes 786440 | tf_op jit(solution)/shard_map/gather_posteriors/ppermute | solution.py:418
  130.4 15.2 %collective-permute-start.6 = (bf16[4,128,256]{2,1,0:T(8,128)(2,1)S(1)}, bf16[4,128,256]{2,1,0:T(8,128)(2,1)S(1)}, u32[]{:S(2)}, u32[]{:S(2)}) collective-permute-start(bf16[4,128,256]{2,1,0:T(8,128)(2,1)S(1)} %bitcast.26), channel_id=1, source_target_pairs={{0,256},{32,288},{64,320},{96,352},{128,384},{160,416},{192,448},{... | collective-permute-start | bytes 786440 | tf_op jit(solution)/shard_map/gather_posteriors/ppermute | solution.py:418
  134.1 1.6 %copy-start = (bf16[16,272,256]{2,1,0:T(8,128)(2,1)S(1)}, bf16[16,272,256]{2,1,0:T(8,128)(2,1)}, u32[]{:S(2)}) copy-start(bf16[16,272,256]{2,1,0:T(8,128)(2,1)} %all-gather.9.cloned.1.call-done) | copy-start | bytes 6684676
  135.8 9.9 %copy-start.1 = (bf16[16,272,256]{2,1,0:T(8,128)(2,1)S(1)}, bf16[16,272,256]{2,1,0:T(8,128)(2,1)}, u32[]{:S(2)}) copy-start(bf16[16,272,256]{2,1,0:T(8,128)(2,1)} %all-gather.9.cloned.1.call-done) | copy-start | bytes 6684676
Sparse Core Ops, SparseCore 0:
  42.6 33.2 all-gather.6
  78.0 41.5 all-gather.8

commit v5 on v4

--- a/solution.py
+++ b/solution.py
@@ -14,7 +14,7 @@
 LANES = 128
 TERM_ROWS = 16
 MOST_VMEM = 63 << 20
-BACK_VMEM = 20 << 20
+SMALL_VMEM = 20 << 20
 WEIGHT_VMEM = 60 << 20
 SMALL_COST = pl.CostEstimate(flops=1, bytes_accessed=1, transcendentals=0)
 INTERPRET = False
@@ -44,10 +44,9 @@
             for y in range(NY):
                 for zl in range(NZL):
                     for c in range(NC):
-                        pose = (y * NZL + zl) * NC + c
-                        src = x * NZH + zh
-                        dst = ((x + y) % NX) * NZH + (zh + zl) % NZH
-                        pairs.append((src * n_pose + pose, dst * n_pose + pose))
+                        src = (x * NZH + zh) * n_pose + (y * NZL + zl) * NC + c
+                        dst = (((x + y) % NX) * NZH + zl) * n_pose + (y * NZL + zh) * NC + c
+                        pairs.append((src, dst))
     return pairs
 
 
@@ -229,13 +228,10 @@
     )(x[None], proj, weighted, noise, part, bias)
 
 
-def posterior_kernel(core_ref, scores_hbm, log_sums_ref, post_ref, post_bf_ref, scores_ref, sem):
-    copy = pltpu.make_async_copy(scores_hbm, scores_ref, sem)
-    copy.start()
+def posterior_kernel(core_ref, scores_ref, log_sums_ref, post_ref, post_bf_ref):
     parts = log_sums_ref[...]
     peak = jnp.max(parts, axis=0)
     log_sum = peak + jnp.log(jnp.sum(jnp.exp(parts - peak[None]), axis=0))
-    copy.wait()
     posteriors = jnp.exp(scores_ref[...] - log_sum)
     half = posteriors.shape[1] // NC
     swapped = jnp.concatenate([posteriors[:, half:], posteriors[:, :half]], axis=1)
@@ -250,16 +246,15 @@
         posterior_kernel,
         in_specs=[
             pl.BlockSpec(memory_space=pltpu.SMEM),
-            pl.BlockSpec(memory_space=pl.ANY),
+            pl.BlockSpec(memory_space=pltpu.VMEM),
             pl.BlockSpec(memory_space=pltpu.VMEM),
         ],
         out_shape=[
             jax.ShapeDtypeStruct((n, rows), jnp.float32),
             jax.ShapeDtypeStruct((rows, n), jnp.bfloat16),
         ],
-        scratch_shapes=[pltpu.VMEM(scores.shape, jnp.float32), pltpu.SemaphoreType.DMA],
         cost_estimate=SMALL_COST,
-        compiler_params=pltpu.CompilerParams(vmem_limit_bytes=MOST_VMEM),
+        compiler_params=pltpu.CompilerParams(vmem_limit_bytes=SMALL_VMEM),
         interpret=INTERPRET,
         name="posterior",
     )(core[None], scores, log_sums)
@@ -339,7 +334,7 @@
         out_specs=[in_vmem] * len(out_shape),
         out_shape=out_shape,
         cost_estimate=SMALL_COST,
-        compiler_params=pltpu.CompilerParams(vmem_limit_bytes=BACK_VMEM),
+        compiler_params=pltpu.CompilerParams(vmem_limit_bytes=SMALL_VMEM),
         interpret=INTERPRET,
         name="back_project",
     )(start[None], *posts, *images, *before)
@@ -360,7 +355,7 @@
     _, rows, slab = projections.shape
     half = n // NC
     group, pose = lax.axis_index("grp"), lax.axis_index("pose")
-    x, zh = group >> 2, group & 3
+    x = group >> 2
     y, zl, core = pose >> 3, (pose >> 1) & 3, pose & 1
 
     z_groups = [[a * NZH + b for b in range(NZH)] for a in range(NX)]
@@ -374,7 +369,7 @@
         proj = lax.all_gather(proj_z, "grp", axis=0, axis_index_groups=x_groups)
 
     with jax.named_scope("exchange_images"):
-        target = (((x + y) & 3) << 2) + ((zh + zl) & 3)
+        target = (((x + y) & 3) << 2) + zl
         cut = lax.dynamic_slice(images, (0, core * half, target * slab), (2, half, slab))
         part_defocus = lax.dynamic_slice(defocus, (core * half,), (half,))
         pixel = (target * slab + jnp.arange(slab)).astype(jnp.float32)
@@ -402,7 +397,7 @@
         turned = copies_of(share, NZL)
         for d in (1, 2, 3):
             block = lax.ppermute(share, "pose", pose_shift(0, d, 0))
-            turned = lax.dynamic_update_slice_in_dim(turned, block[None], (zh - zl + d) & 3, 0)
+            turned = lax.dynamic_update_slice_in_dim(turned, block[None], (zl - d) & 3, 0)
         turned, proj = lax.optimization_barrier((turned, proj))
         own = lax.all_gather(turned, "pose", axis=0, axis_index_groups=y_groups)
 

time: 155 us -> 154 us (level)
  Pallas kernels: 20.2 us -> 18.6 us
    pallas_call x1, Pallas kernels: 2.46 us -> 0.84 us  [posterior(): pl.pallas_call(posterior_kernel, in_specs=[pl.BlockSpec(memory_space=pltp...]
  transfers between devices with their start and end apart: 10 -> 10, of which waited for: 4 -> 3; matrix products, arithmetic and copies ran while one was open for 4% -> 4% of each run, Pallas kernels for 12% -> 11%
where the time goes in v5:
time: 154 us; the launch traced here: 153 us
  blocking collectives  73 us (47%)
  starting transfers between devices  29.3 us (19%)
  Pallas kernels  18.6 us (12%)
  between operations  14.3 us (9%)
  waiting for transfers between devices  9.34 us (6%)
  other arithmetic  4.8 us (3%)
  local copies, waits for them, and re-layouts  2.87 us (2%)
    all_gather x1, blocking collectives, on_device(): lax.all_gather(projections, 'grp', axis=0, axis_index_groups=z_groups)  35.2 us
    all_gather x1, blocking collectives, on_device(): lax.all_gather(post_bf, 'grp', axis=0, axis_index_groups=z_groups)  20.5 us
    all_to_all x1, blocking collectives, exchange(): return lax.all_to_all(copies, axis, 0, 0, axis_index_groups=groups)  17.3 us
    ppermute x3, starting transfers between devices, on_device(): block = lax.ppermute(share, 'pose', pose_shift(0, d, 0))  16.5 us
    ppermute x3, starting transfers between devices, on_device(): post[d] = lax.ppermute(post[0], 'grp', grp_shift(d))  10.1 us
    pallas_call x1, Pallas kernels, weight_images(): pl.pallas_call(weight_kernel, in_specs=[pl.BlockSpec(memory_space=pltpu.S...  7.24 us
    ppermute x3, waiting for transfers between devices, on_device(): post[d] = lax.ppermute(post[0], 'grp', grp_shift(d))  6.27 us
    pallas_call x1, Pallas kernels, score(): pl.pallas_call(score_kernel, in_specs=[pl.BlockSpec(memory_space=pltpu.SM...  5.32 us
  transfers between devices with their start and end apart: 10, of which 3 were waited for; matrix products, arithmetic and copies ran while one was open for 4% of the time, Pallas kernels for 11%

profile of v5, /device:TPU:6, one launch (start us, length us, event | category | flops | bytes accessed | tf_op | source)
XLA Modules:
  0.0 153.1 jit_solution(3254369977501579956)
XLA Ops:
  7.2 35.2 %all-gather = bf16[8,128,256]{2,1,0:T(8,128)(2,1)} all-gather(bf16[2,128,256]{2,1,0:T(8,128)(2,1)} %param.9), channel_id=2, replica_groups={{0,32,64,96},{128,160,192,224},{256,288,320,352},{384,416,448,480},{1,3..., dimensions={0}, use_global_device_ids=true | all-gather | bytes 655360 | tf_op jit(solution)/shard_map/gather_projections/all_gather | solution.py:367
  42.5 0.8 fusion.14
  43.8 0.9 multiply_convert_fusion
  45.5 0.8 broadcast_multiply_fusion
  46.3 1.7 %fusion.1 = (f32[256,256]{1,0:T(8,128)}, f32[256,256]{1,0:T(8,128)}) fusion(f32[256,128]{1,0:T(8,128)S(1)} %get-tuple-element.43, f32[256,128]{1,0:T(8,128)S(1)} %get-tuple-element.42), kind=kLoop, calls=%fused_computation.4 | loop fusion | flops 65536 | bytes 786432 | tf_op jit(solution)/shard_map/weights/cos | solution.py:171
  47.9 7.2 %weight_images.1 = (bf16[2,256,4096]{2,1,0:T(8,128)(2,1)}, bf16[256,4096]{1,0:T(8,128)(2,1)}, f32[128,256]{1,0:T(8,128)}) custom-call(s32[1]{0:T(128)} %bitcast.1.x_ref, bf16[2,256,4096]{2,1,0:T(8,128)(2,1)} %images_hbm.1, f32[256,256]{1,0:T(8,128)} %get-tuple-element.41.sin_ref, f32[256,256]{1,0:T(8,128)} %get-tuple-element.40.cos_ref, f32[1,4096]{1,0:T(1,128)} %bitcast.32, ...), custom_call_target="tpu_custom_call" | custom-call | flops 1 | bytes 1 | tf_op jit(solution)/shard_map/weights/weight_images/pallas_call | solution.py:152
  55.3 0.9 fusion.bias_ref
  56.2 6.8 %collective-permute-start.1 = (bf16[272,256]{1,0:T(8,128)(2,1)S(1)}, bf16[272,256]{1,0:T(8,128)(2,1)S(1)}, u32[]{:S(2)}, u32[]{:S(2)}) collective-permute-start(bf16[272,256]{1,0:T(8,128)(2,1)S(1)} %collective-permute-done), channel_id=1, source_target_pairs={{0,2},{1,3},{2,4},{3,5},{4,6},{5,7},{6,0},{7,1},{8,10},{9,11},{10,... | collective-permute-start | bytes 417800 | tf_op jit(solution)/shard_map/gather_images/ppermute | solution.py:399
  63.1 5.2 %collective-permute-start.2 = (bf16[272,256]{1,0:T(8,128)(2,1)S(1)}, bf16[272,256]{1,0:T(8,128)(2,1)S(1)}, u32[]{:S(2)}, u32[]{:S(2)}) collective-permute-start(bf16[272,256]{1,0:T(8,128)(2,1)S(1)} %collective-permute-done), channel_id=1, source_target_pairs={{0,4},{1,5},{2,6},{3,7},{4,0},{5,1},{6,2},{7,3},{8,12},{9,13},{10,... | collective-permute-start | bytes 417800 | tf_op jit(solution)/shard_map/gather_images/ppermute | solution.py:399
  68.2 4.5 %collective-permute-start.3 = (bf16[272,256]{1,0:T(8,128)(2,1)S(1)}, bf16[272,256]{1,0:T(8,128)(2,1)S(1)}, u32[]{:S(2)}, u32[]{:S(2)}) collective-permute-start(bf16[272,256]{1,0:T(8,128)(2,1)S(1)} %collective-permute-done), channel_id=1, source_target_pairs={{0,6},{1,7},{2,0},{3,1},{4,2},{5,3},{6,4},{7,5},{8,14},{9,15},{10,... | collective-permute-start | bytes 417800 | tf_op jit(solution)/shard_map/gather_images/ppermute | solution.py:399
  72.9 2.5 %collective-permute-done.3 = bf16[272,256]{1,0:T(8,128)(2,1)S(1)} collective-permute-done((bf16[272,256]{1,0:T(8,128)(2,1)S(1)}, bf16[272,256]{1,0:T(8,128)(2,1)S(1)}, u32[]{:S(2)}, u32[]{:S(2)}) %collective-permute-start.3) | collective-permute-done | bytes 139296 | tf_op jit(solution)/shard_map/gather_images/ppermute | solution.py:399
  76.2 5.3 %score.1 = (f32[128,256]{1,0:T(8,128)}, f32[32,1,256]{2,1,0:T(1,128)}) custom-call(s32[1]{0:T(128)} %bitcast.1.x_ref, bf16[4,4,2,128,256]{4,3,2,1,0:T(8,128)(2,1)} %bitcast.30, bf16[2,256,4096]{2,1,0:T(8,128)(2,1)} %get-tuple-element.25.weighted_hbm, bf16[256,4096]{1,0:T(8,128)(2,1)} %get-tuple-element.26.noise_hbm, f32[128,256]{1,0:T(8,128)} %get-tuple-element.27.part_ref, ...), custom_call_target="tpu_custom_call" | custom-call | flops 1 | bytes 1 | tf_op jit(solution)/shard_map/scores/score/pallas_call | solution.py:210
  81.5 17.3 %all_to_all.5.log_sums_ref = f32[32,1,256]{2,1,0:T(1,128)S(1)} all-to-all(f32[32,1,256]{2,1,0:T(1,128)} %get-tuple-element.30), channel_id=1, replica_groups=mesh['grp'=16,'pose'=32] {'pose'}, dimensions={0} | all-to-all | bytes 65536 | tf_op jit(solution)/shard_map/softmax/all_to_all | solution.py:344
  98.8 0.9 copy-done.2
  99.7 0.8 posterior.1
  100.5 20.5 %all-gather.2 = bf16[512,256]{1,0:T(8,128)(2,1)S(1)} all-gather(bf16[128,256]{1,0:T(8,128)(2,1)S(1)} %get-tuple-element.32), channel_id=4, replica_groups={{0,32,64,96},{128,160,192,224},{256,288,320,352},{384,416,448,480},{1,3..., dimensions={0}, use_global_device_ids=true | all-gather | bytes 327680 | tf_op jit(solution)/shard_map/gather_posteriors/all_gather | solution.py:411
  121.1 1.9 %collective-permute-start.7 = (bf16[4,4,272,256]{3,2,1,0:T(8,128)(2,1)}, bf16[4,4,272,256]{3,2,1,0:T(8,128)(2,1)S(1)}, u32[]{:S(2)}, u32[]{:S(2)}) collective-permute-start(bf16[4,4,272,256]{3,2,1,0:T(8,128)(2,1)} %bitcast.21), channel_id=1, source_target_pairs={{0,1},{1,0},{2,3},{3,2},{4,5},{5,4},{6,7},{7,6},{8,9},{9,8},{10,11... | collective-permute-start | bytes 6684680 | tf_op jit(solution)/shard_map/gather_posteriors/ppermute | solution.py:415
  123.0 4.3 %collective-permute-start.4 = (bf16[4,128,256]{2,1,0:T(8,128)(2,1)S(1)}, bf16[4,128,256]{2,1,0:T(8,128)(2,1)S(1)}, u32[]{:S(2)}, u32[]{:S(2)}) collective-permute-start(bf16[4,128,256]{2,1,0:T(8,128)(2,1)S(1)} %bitcast.24), channel_id=1, source_target_pairs={{0,128},{32,160},{64,192},{96,224},{128,256},{160,288},{192,320},{... | collective-permute-start | bytes 786440 | tf_op jit(solution)/shard_map/gather_posteriors/ppermute | solution.py:413
  127.3 1.9 %collective-permute-start.5 = (bf16[4,128,256]{2,1,0:T(8,128)(2,1)S(1)}, bf16[4,128,256]{2,1,0:T(8,128)(2,1)S(1)}, u32[]{:S(2)}, u32[]{:S(2)}) collective-permute-start(bf16[4,128,256]{2,1,0:T(8,128)(2,1)S(1)} %bitcast.25), channel_id=1, source_target_pairs={{0,384},{32,416},{64,448},{96,480},{128,0},{160,32},{192,64},{224,... | collective-permute-start | bytes 786440 | tf_op jit(solution)/shard_map/gather_posteriors/ppermute | solution.py:413
  129.2 3.9 %collective-permute-start.6 = (bf16[4,128,256]{2,1,0:T(8,128)(2,1)S(1)}, bf16[4,128,256]{2,1,0:T(8,128)(2,1)S(1)}, u32[]{:S(2)}, u32[]{:S(2)}) collective-permute-start(bf16[4,128,256]{2,1,0:T(8,128)(2,1)S(1)} %bitcast.26), channel_id=1, source_target_pairs={{0,256},{32,288},{64,320},{96,352},{128,384},{160,416},{192,448},{... | collective-permute-start | bytes 786440 | tf_op jit(solution)/shard_map/gather_posteriors/ppermute | solution.py:413
  133.1 1.6 %copy-done = bf16[16,272,256]{2,1,0:T(8,128)(2,1)S(1)} copy-done((bf16[16,272,256]{2,1,0:T(8,128)(2,1)S(1)}, bf16[16,272,256]{2,1,0:T(8,128)(2,1)}, u32[]{:S(2)}) %copy-start) | copy-done | bytes 2228248
  134.7 3.4 %back_project.2 = (f32[3,128,256]{2,1,0:T(8,128)S(1)}, bf16[3,256,1024]{2,1,0:T(8,128)(2,1)S(1)}) custom-call(s32[1]{0:T(128)} %bitcast.12.start_ref, bf16[4,128,256]{2,1,0:T(8,128)(2,1)S(1)} %bitcast.27, bf16[4,4,272,256]{3,2,1,0:T(8,128)(2,1)S(1)} %bitcast.22, bf16[4,4,272,256]{3,2,1,0:T(8,128)(2,1)S(1)} %collective-permute-done.7.refs_2_.refs_4_), custom_call_target="tpu_custom_call" | custom-call | flops 1 | bytes 1 | tf_op jit(solution)/shard_map/back_project/back_project/pallas_call | solution.py:330
  138.2 6.3 %collective-permute-done.5.refs_1_ = bf16[4,128,256]{2,1,0:T(8,128)(2,1)S(1)} collective-permute-done((bf16[4,128,256]{2,1,0:T(8,128)(2,1)S(1)}, bf16[4,128,256]{2,1,0:T(8,128)(2,1)S(1)}, u32[]{:S(2)}, u32[]{:S(2)}) %collective-permute-start.5) | collective-permute-done | bytes 262176 | tf_op jit(solution)/shard_map/gather_posteriors/ppermute | solution.py:413
  144.4 1.8 %back_project.3 = f32[3,128,256]{2,1,0:T(8,128)} custom-call(s32[1]{0:T(128)} %bitcast.12.start_ref, bf16[4,128,256]{2,1,0:T(8,128)(2,1)S(1)} %collective-permute-done.4.refs_0_, bf16[4,128,256]{2,1,0:T(8,128)(2,1)S(1)} %collective-permute-done.5.refs_1_, bf16[4,128,256]{2,1,0:T(8,128)(2,1)S(1)} %collective-permute-done.6.refs_2_, ...), custom_call_target="tpu_custom_call" | custom-call | flops 1 | bytes 1 | tf_op jit(solution)/shard_map/back_project/back_project/pallas_call | solution.py:330
  (38 shorter events, 2.4 us)
Async XLA Ops:
  7.2 68.7 %all-gather.7.cloned.1.call-start = ((), (), s32[]{:S(2)}) async-start(), calls=%async_computation.1 | async-start | bytes 2621440 | tf_op jit(solution)/shard_map/gather_projections/all_gather | solution.py:369
  42.4 78.6 %all-gather.9.cloned.1.call-start = ((), (), s32[]{:S(2)}) async-start(), calls=%async_computation.2 | async-start | bytes 2785280 | tf_op jit(solution)/shard_map/gather_images/all_gather | solution.py:402
  44.8 11.4 %collective-permute-start = (bf16[272,256]{1,0:T(8,128)(2,1)S(1)}, bf16[272,256]{1,0:T(8,128)(2,1)S(1)}, u32[]{:S(2)}, u32[]{:S(2)}) collective-permute-start(bf16[272,256]{1,0:T(8,128)(2,1)S(1)} %pad_maximum_fusion.1), channel_id=1, source_target_pairs={{0,0},{1,1},{2,32},{3,33},{4,64},{5,65},{6,96},{7,97},{8,136},{9,1... | collective-permute-start | bytes 417800 | tf_op jit(solution)/shard_map/exchange_images/ppermute | solution.py:380
  47.9 7.3 %copy-start.6 = (f32[64]{0:T(128)S(1)}, f32[64]{0:T(128)}, u32[]{:S(2)}) copy-start(f32[64]{0:T(128)} %param.12) | copy-start | bytes 772
  47.9 7.3 %copy-start.7 = (s32[128]{0:T(128)S(1)}, s32[128]{0:T(128)}, u32[]{:S(2)}) copy-start(s32[128]{0:T(128)} %param.13) | copy-start | bytes 1540
  47.9 7.4 %copy-start.4 = (s32[256,256]{1,0:T(8,128)S(1)}, s32[256,256]{1,0:T(8,128)}, u32[]{:S(2)}) copy-start(s32[256,256]{1,0:T(8,128)} %param.15) | copy-start | bytes 786436
  47.9 7.4 %copy-start.5 = (s32[128]{0:T(128)S(1)}, s32[128]{0:T(128)}, u32[]{:S(2)}) copy-start(s32[128]{0:T(128)} %param.14) | copy-start | bytes 1540
  56.2 16.6 %collective-permute-start.1 = (bf16[272,256]{1,0:T(8,128)(2,1)S(1)}, bf16[272,256]{1,0:T(8,128)(2,1)S(1)}, u32[]{:S(2)}, u32[]{:S(2)}) collective-permute-start(bf16[272,256]{1,0:T(8,128)(2,1)S(1)} %collective-permute-done), channel_id=1, source_target_pairs={{0,2},{1,3},{2,4},{3,5},{4,6},{5,7},{6,0},{7,1},{8,10},{9,11},{10,... | collective-permute-start | bytes 417800 | tf_op jit(solution)/shard_map/gather_images/ppermute | solution.py:399
  63.1 9.8 %collective-permute-start.2 = (bf16[272,256]{1,0:T(8,128)(2,1)S(1)}, bf16[272,256]{1,0:T(8,128)(2,1)S(1)}, u32[]{:S(2)}, u32[]{:S(2)}) collective-permute-start(bf16[272,256]{1,0:T(8,128)(2,1)S(1)} %collective-permute-done), channel_id=1, source_target_pairs={{0,4},{1,5},{2,6},{3,7},{4,0},{5,1},{6,2},{7,3},{8,12},{9,13},{10,... | collective-permute-start | bytes 417800 | tf_op jit(solution)/shard_map/gather_images/ppermute | solution.py:399
  68.2 7.1 %collective-permute-start.3 = (bf16[272,256]{1,0:T(8,128)(2,1)S(1)}, bf16[272,256]{1,0:T(8,128)(2,1)S(1)}, u32[]{:S(2)}, u32[]{:S(2)}) collective-permute-start(bf16[272,256]{1,0:T(8,128)(2,1)S(1)} %collective-permute-done), channel_id=1, source_target_pairs={{0,6},{1,7},{2,0},{3,1},{4,2},{5,3},{6,4},{7,5},{8,14},{9,15},{10,... | collective-permute-start | bytes 417800 | tf_op jit(solution)/shard_map/gather_images/ppermute | solution.py:399
  75.3 0.8 copy-start.3
  98.8 0.9 copy-start.2
  121.1 12.1 %collective-permute-start.7 = (bf16[4,4,272,256]{3,2,1,0:T(8,128)(2,1)}, bf16[4,4,272,256]{3,2,1,0:T(8,128)(2,1)S(1)}, u32[]{:S(2)}, u32[]{:S(2)}) collective-permute-start(bf16[4,4,272,256]{3,2,1,0:T(8,128)(2,1)} %bitcast.21), channel_id=1, source_target_pairs={{0,1},{1,0},{2,3},{3,2},{4,5},{5,4},{6,7},{7,6},{8,9},{9,8},{10,11... | collective-permute-start | bytes 6684680 | tf_op jit(solution)/shard_map/gather_posteriors/ppermute | solution.py:415
  123.0 15.2 %collective-permute-start.4 = (bf16[4,128,256]{2,1,0:T(8,128)(2,1)S(1)}, bf16[4,128,256]{2,1,0:T(8,128)(2,1)S(1)}, u32[]{:S(2)}, u32[]{:S(2)}) collective-permute-start(bf16[4,128,256]{2,1,0:T(8,128)(2,1)S(1)} %bitcast.24), channel_id=1, source_target_pairs={{0,128},{32,160},{64,192},{96,224},{128,256},{160,288},{192,320},{... | collective-permute-start | bytes 786440 | tf_op jit(solution)/shard_map/gather_posteriors/ppermute | solution.py:413
  127.3 17.2 %collective-permute-start.5 = (bf16[4,128,256]{2,1,0:T(8,128)(2,1)S(1)}, bf16[4,128,256]{2,1,0:T(8,128)(2,1)S(1)}, u32[]{:S(2)}, u32[]{:S(2)}) collective-permute-start(bf16[4,128,256]{2,1,0:T(8,128)(2,1)S(1)} %bitcast.25), channel_id=1, source_target_pairs={{0,384},{32,416},{64,448},{96,480},{128,0},{160,32},{192,64},{224,... | collective-permute-start | bytes 786440 | tf_op jit(solution)/shard_map/gather_posteriors/ppermute | solution.py:413
  129.2 15.2 %collective-permute-start.6 = (bf16[4,128,256]{2,1,0:T(8,128)(2,1)S(1)}, bf16[4,128,256]{2,1,0:T(8,128)(2,1)S(1)}, u32[]{:S(2)}, u32[]{:S(2)}) collective-permute-start(bf16[4,128,256]{2,1,0:T(8,128)(2,1)S(1)} %bitcast.26), channel_id=1, source_target_pairs={{0,256},{32,288},{64,320},{96,352},{128,384},{160,416},{192,448},{... | collective-permute-start | bytes 786440 | tf_op jit(solution)/shard_map/gather_posteriors/ppermute | solution.py:413
  133.1 1.6 %copy-start = (bf16[16,272,256]{2,1,0:T(8,128)(2,1)S(1)}, bf16[16,272,256]{2,1,0:T(8,128)(2,1)}, u32[]{:S(2)}) copy-start(bf16[16,272,256]{2,1,0:T(8,128)(2,1)} %all-gather.9.cloned.1.call-done) | copy-start | bytes 6684676
  134.7 9.7 %copy-start.1 = (bf16[16,272,256]{2,1,0:T(8,128)(2,1)S(1)}, bf16[16,272,256]{2,1,0:T(8,128)(2,1)}, u32[]{:S(2)}) copy-start(bf16[16,272,256]{2,1,0:T(8,128)(2,1)} %all-gather.9.cloned.1.call-done) | copy-start | bytes 6684676
Sparse Core Ops, SparseCore 0:
  42.6 33.2 all-gather.6
  78.0 41.5 all-gather.8

commit v6 on v5

--- a/solution.py
+++ b/solution.py
@@ -13,7 +13,7 @@
 NY, NZL, NC = 4, 4, 2
 LANES = 128
 TERM_ROWS = 16
-MOST_VMEM = 63 << 20
+SCORE_VMEM = 53 << 20
 SMALL_VMEM = 20 << 20
 WEIGHT_VMEM = 60 << 20
 SMALL_COST = pl.CostEstimate(flops=1, bytes_accessed=1, transcendentals=0)
@@ -172,8 +172,8 @@
 
 
 def score_kernel(
-    x_ref, proj_hbm, weighted_hbm, noise_hbm, part_ref, bias_ref, scores_ref, log_sum_ref,
-    proj_ref, weighted_ref, noise_ref, sems,
+    x_ref, proj_hbm, weighted_hbm, noise_hbm, part_hbm, bias_ref, scores_ref, log_sum_ref,
+    proj_ref, weighted_ref, noise_ref, part_ref, sems, part_sem,
 ):
     n_s, n_z, _, _, slab = proj_ref.shape
     block = n_z * slab
@@ -190,11 +190,16 @@
     for i in range(n_s):
         for copy in copies(i):
             copy.start()
-    total = part_ref[...]
+    part_copy = pltpu.make_async_copy(part_hbm, part_ref, part_sem)
+    part_copy.start()
+    total = None
     for i in range(n_s):
         for copy in copies(i):
             copy.wait()
-        total += score_terms(proj_ref.at[i], weighted_ref[i, 0], weighted_ref[i, 1], noise_ref[i])
+        terms = score_terms(proj_ref.at[i], weighted_ref[i, 0], weighted_ref[i, 1], noise_ref[i])
+        total = terms if total is None else total + terms
+    part_copy.wait()
+    total += part_ref[...]
     bias = bias_ref[...]
     scores = jnp.where(bias == NEG_FILL, bias, total + bias)
     scores_ref[...] = scores
@@ -209,7 +214,7 @@
     in_hbm, in_vmem = pl.BlockSpec(memory_space=pl.ANY), pl.BlockSpec(memory_space=pltpu.VMEM)
     return pl.pallas_call(
         score_kernel,
-        in_specs=[pl.BlockSpec(memory_space=pltpu.SMEM)] + [in_hbm] * 3 + [in_vmem] * 2,
+        in_specs=[pl.BlockSpec(memory_space=pltpu.SMEM)] + [in_hbm] * 4 + [in_vmem],
         out_specs=[in_vmem] * 2,
         out_shape=[
             jax.ShapeDtypeStruct((rows, n), jnp.float32),
@@ -219,10 +224,12 @@
             pltpu.VMEM((n_x - 1,) + proj.shape[1:], jnp.bfloat16),
             pltpu.VMEM((n_x - 1, 2, n, n_z * slab), jnp.bfloat16),
             pltpu.VMEM((n_x - 1, n, n_z * slab), jnp.bfloat16),
+            pltpu.VMEM((rows, n), jnp.float32),
             pltpu.SemaphoreType.DMA((3, n_x - 1)),
+            pltpu.SemaphoreType.DMA,
         ],
         cost_estimate=SMALL_COST,
-        compiler_params=pltpu.CompilerParams(vmem_limit_bytes=MOST_VMEM),
+        compiler_params=pltpu.CompilerParams(vmem_limit_bytes=SCORE_VMEM),
         interpret=INTERPRET,
         name="score",
     )(x[None], proj, weighted, noise, part, bias)
@@ -409,14 +416,14 @@
 
     with jax.named_scope("gather_posteriors"):
         post = [lax.all_gather(post_bf, "grp", axis=0, axis_index_groups=z_groups)] + [None] * 3
-        for d in (1, 3, 2):
+        for d in (2, 1, 3):
             post[d] = lax.ppermute(post[0], "grp", grp_shift(d))
         post[0], own = lax.optimization_barrier((post[0], own))
         other = lax.ppermute(own, "pose", pose_shift(0, 0, 1))
 
     with jax.named_scope("back_project"):
         start = group * slab
-        near, far, stacks = (0,), (1, 3, 2), (own, other)
+        near, far, stacks = (0,), (1, 2, 3), (own, other)
         before = back_project(start, width, near, [post[d] for d in near], stacks, ahead=far)
         (back_proj,) = back_project(start, width, far, [post[d] for d in far], stacks, before=before)
     return (posteriors, back_proj)

time: 154 us -> 152 us (0.987)
  waiting for transfers between devices: 9.34 us -> 11.7 us
    pallas_call x1, Pallas kernels: 5.32 us -> 3.77 us  [score(): pl.pallas_call(score_kernel, in_specs=[pl.BlockSpec(memory_space=pltpu.SM...]
  transfers between devices with their start and end apart: 10 -> 10, of which waited for: 3 -> 5; matrix products, arithmetic and copies ran while one was open for 4% -> 3% of each run, Pallas kernels for 11% -> 10%
where the time goes in v6:
time: 152 us; the launch traced here: 151 us
  blocking collectives  73 us (48%)
  starting transfers between devices  27.8 us (18%)
  Pallas kernels  17.1 us (11%)
  between operations  14.3 us (9%)
  waiting for transfers between devices  11.7 us (8%)
  other arithmetic  4.8 us (3%)
  local copies, waits for them, and re-layouts  1.73 us (1%)
    all_gather x1, blocking collectives, on_device(): lax.all_gather(projections, 'grp', axis=0, axis_index_groups=z_groups)  35.2 us
    all_gather x1, blocking collectives, on_device(): lax.all_gather(post_bf, 'grp', axis=0, axis_index_groups=z_groups)  21.2 us
    all_to_all x1, blocking collectives, exchange(): return lax.all_to_all(copies, axis, 0, 0, axis_index_groups=groups)  16.7 us
    ppermute x3, starting transfers between devices, on_device(): block = lax.ppermute(share, 'pose', pose_shift(0, d, 0))  16.5 us
    ppermute x3, starting transfers between devices, on_device(): post[d] = lax.ppermute(post[0], 'grp', grp_shift(d))  8.66 us
    pallas_call x1, Pallas kernels, weight_images(): pl.pallas_call(weight_kernel, in_specs=[pl.BlockSpec(memory_space=pltpu.S...  7.24 us
    ppermute x3, waiting for transfers between devices, on_device(): post[d] = lax.ppermute(post[0], 'grp', grp_shift(d))  6.72 us
    pallas_call x2, Pallas kernels, back_project(): pl.pallas_call(functools.partial(back_kernel, sources, ahead, width), in_...  5.24 us
  transfers between devices with their start and end apart: 10, of which 5 were waited for; matrix products, arithmetic and copies ran while one was open for 3% of the time, Pallas kernels for 10%

profile of v6, /device:TPU:6, one launch (start us, length us, event | category | flops | bytes accessed | tf_op | source)
XLA Modules:
  0.0 150.7 jit_solution(6920799093850675799)
XLA Ops:
  7.2 35.2 %all-gather = bf16[8,128,256]{2,1,0:T(8,128)(2,1)} all-gather(bf16[2,128,256]{2,1,0:T(8,128)(2,1)} %param.9), channel_id=2, replica_groups={{0,32,64,96},{128,160,192,224},{256,288,320,352},{384,416,448,480},{1,3..., dimensions={0}, use_global_device_ids=true | all-gather | bytes 655360 | tf_op jit(solution)/shard_map/gather_projections/all_gather | solution.py:374
  43.8 0.9 multiply_convert_fusion
  45.5 0.8 broadcast_multiply_fusion
  46.3 1.7 %fusion.1 = (f32[256,256]{1,0:T(8,128)}, f32[256,256]{1,0:T(8,128)}) fusion(f32[256,128]{1,0:T(8,128)S(1)} %get-tuple-element.43, f32[256,128]{1,0:T(8,128)S(1)} %get-tuple-element.42), kind=kLoop, calls=%fused_computation.4 | loop fusion | flops 65536 | bytes 786432 | tf_op jit(solution)/shard_map/weights/cos | solution.py:171
  47.9 7.2 %weight_images.1 = (bf16[2,256,4096]{2,1,0:T(8,128)(2,1)}, bf16[256,4096]{1,0:T(8,128)(2,1)}, f32[128,256]{1,0:T(8,128)}) custom-call(s32[1]{0:T(128)} %bitcast.1.x_ref, bf16[2,256,4096]{2,1,0:T(8,128)(2,1)} %images_hbm.1, f32[256,256]{1,0:T(8,128)} %get-tuple-element.41.sin_ref, f32[256,256]{1,0:T(8,128)} %get-tuple-element.40.cos_ref, f32[1,4096]{1,0:T(1,128)} %bitcast.32, ...), custom_call_target="tpu_custom_call" | custom-call | flops 1 | bytes 1 | tf_op jit(solution)/shard_map/weights/weight_images/pallas_call | solution.py:152
  55.6 6.9 %collective-permute-start.1 = (bf16[272,256]{1,0:T(8,128)(2,1)S(1)}, bf16[272,256]{1,0:T(8,128)(2,1)S(1)}, u32[]{:S(2)}, u32[]{:S(2)}) collective-permute-start(bf16[272,256]{1,0:T(8,128)(2,1)S(1)} %collective-permute-done), channel_id=1, source_target_pairs={{0,2},{1,3},{2,4},{3,5},{4,6},{5,7},{6,0},{7,1},{8,10},{9,11},{10,... | collective-permute-start | bytes 417800 | tf_op jit(solution)/shard_map/gather_images/ppermute | solution.py:406
  62.4 5.2 %collective-permute-start.2 = (bf16[272,256]{1,0:T(8,128)(2,1)S(1)}, bf16[272,256]{1,0:T(8,128)(2,1)S(1)}, u32[]{:S(2)}, u32[]{:S(2)}) collective-permute-start(bf16[272,256]{1,0:T(8,128)(2,1)S(1)} %collective-permute-done), channel_id=1, source_target_pairs={{0,4},{1,5},{2,6},{3,7},{4,0},{5,1},{6,2},{7,3},{8,12},{9,13},{10,... | collective-permute-start | bytes 417800 | tf_op jit(solution)/shard_map/gather_images/ppermute | solution.py:406
  67.6 4.5 %collective-permute-start.3 = (bf16[272,256]{1,0:T(8,128)(2,1)S(1)}, bf16[272,256]{1,0:T(8,128)(2,1)S(1)}, u32[]{:S(2)}, u32[]{:S(2)}) collective-permute-start(bf16[272,256]{1,0:T(8,128)(2,1)S(1)} %collective-permute-done), channel_id=1, source_target_pairs={{0,6},{1,7},{2,0},{3,1},{4,2},{5,3},{6,4},{7,5},{8,14},{9,15},{10,... | collective-permute-start | bytes 417800 | tf_op jit(solution)/shard_map/gather_images/ppermute | solution.py:406
  72.2 2.5 %collective-permute-done.3 = bf16[272,256]{1,0:T(8,128)(2,1)S(1)} collective-permute-done((bf16[272,256]{1,0:T(8,128)(2,1)S(1)}, bf16[272,256]{1,0:T(8,128)(2,1)S(1)}, u32[]{:S(2)}, u32[]{:S(2)}) %collective-permute-start.3) | collective-permute-done | bytes 139296 | tf_op jit(solution)/shard_map/gather_images/ppermute | solution.py:406
  74.7 1.2 all-gather.7.cloned.1.call-done
  75.9 3.8 %score.1 = (f32[128,256]{1,0:T(8,128)S(1)}, f32[32,1,256]{2,1,0:T(1,128)S(1)}) custom-call(s32[1]{0:T(128)} %bitcast.1.x_ref, bf16[4,4,2,128,256]{4,3,2,1,0:T(8,128)(2,1)} %bitcast.30, bf16[2,256,4096]{2,1,0:T(8,128)(2,1)} %get-tuple-element.25.weighted_hbm, bf16[256,4096]{1,0:T(8,128)(2,1)} %get-tuple-element.26.noise_hbm, f32[128,256]{1,0:T(8,128)S(1)} %copy-done.2, ...), custom_call_target="tpu_custom_call" | custom-call | flops 1 | bytes 1 | tf_op jit(solution)/shard_map/scores/score/pallas_call | solution.py:215
  79.7 16.7 %all_to_all.5.log_sums_ref = f32[32,1,256]{2,1,0:T(1,128)S(1)} all-to-all(f32[32,1,256]{2,1,0:T(1,128)S(1)} %get-tuple-element.30), channel_id=1, replica_groups=mesh['grp'=16,'pose'=32] {'pose'}, dimensions={0} | all-to-all | bytes 65536 | tf_op jit(solution)/shard_map/softmax/all_to_all | solution.py:351
  96.4 0.8 posterior.1
  97.2 21.2 %all-gather.2 = bf16[512,256]{1,0:T(8,128)(2,1)S(1)} all-gather(bf16[128,256]{1,0:T(8,128)(2,1)S(1)} %get-tuple-element.32), channel_id=4, replica_groups={{0,32,64,96},{128,160,192,224},{256,288,320,352},{384,416,448,480},{1,3..., dimensions={0}, use_global_device_ids=true | all-gather | bytes 327680 | tf_op jit(solution)/shard_map/gather_posteriors/all_gather | solution.py:418
  118.4 1.3 all-gather.9.cloned.1.call-done
  119.7 1.9 %collective-permute-start.7 = (bf16[4,4,272,256]{3,2,1,0:T(8,128)(2,1)}, bf16[4,4,272,256]{3,2,1,0:T(8,128)(2,1)S(1)}, u32[]{:S(2)}, u32[]{:S(2)}) collective-permute-start(bf16[4,4,272,256]{3,2,1,0:T(8,128)(2,1)} %bitcast.21), channel_id=1, source_target_pairs={{0,1},{1,0},{2,3},{3,2},{4,5},{5,4},{6,7},{7,6},{8,9},{9,8},{10,11... | collective-permute-start | bytes 6684680 | tf_op jit(solution)/shard_map/gather_posteriors/ppermute | solution.py:422
  121.6 3.0 %collective-permute-start.4 = (bf16[4,128,256]{2,1,0:T(8,128)(2,1)S(1)}, bf16[4,128,256]{2,1,0:T(8,128)(2,1)S(1)}, u32[]{:S(2)}, u32[]{:S(2)}) collective-permute-start(bf16[4,128,256]{2,1,0:T(8,128)(2,1)S(1)} %bitcast.24), channel_id=1, source_target_pairs={{0,128},{32,160},{64,192},{96,224},{128,256},{160,288},{192,320},{... | collective-permute-start | bytes 786440 | tf_op jit(solution)/shard_map/gather_posteriors/ppermute | solution.py:420
  124.6 3.7 %collective-permute-start.5 = (bf16[4,128,256]{2,1,0:T(8,128)(2,1)S(1)}, bf16[4,128,256]{2,1,0:T(8,128)(2,1)S(1)}, u32[]{:S(2)}, u32[]{:S(2)}) collective-permute-start(bf16[4,128,256]{2,1,0:T(8,128)(2,1)S(1)} %bitcast.25), channel_id=1, source_target_pairs={{0,256},{32,288},{64,320},{96,352},{128,384},{160,416},{192,448},{... | collective-permute-start | bytes 786440 | tf_op jit(solution)/shard_map/gather_posteriors/ppermute | solution.py:420
  128.3 1.9 %collective-permute-start.6 = (bf16[4,128,256]{2,1,0:T(8,128)(2,1)S(1)}, bf16[4,128,256]{2,1,0:T(8,128)(2,1)S(1)}, u32[]{:S(2)}, u32[]{:S(2)}) collective-permute-start(bf16[4,128,256]{2,1,0:T(8,128)(2,1)S(1)} %bitcast.26), channel_id=1, source_target_pairs={{0,384},{32,416},{64,448},{96,480},{128,0},{160,32},{192,64},{224,... | collective-permute-start | bytes 786440 | tf_op jit(solution)/shard_map/gather_posteriors/ppermute | solution.py:420
  130.3 1.6 %copy-done = bf16[16,272,256]{2,1,0:T(8,128)(2,1)S(1)} copy-done((bf16[16,272,256]{2,1,0:T(8,128)(2,1)S(1)}, bf16[16,272,256]{2,1,0:T(8,128)(2,1)}, u32[]{:S(2)}) %copy-start) | copy-done | bytes 2228248
  131.9 3.4 %back_project.2 = (f32[3,128,256]{2,1,0:T(8,128)S(1)}, bf16[3,256,1024]{2,1,0:T(8,128)(2,1)S(1)}) custom-call(s32[1]{0:T(128)} %bitcast.12.start_ref, bf16[4,128,256]{2,1,0:T(8,128)(2,1)S(1)} %bitcast.27, bf16[4,4,272,256]{3,2,1,0:T(8,128)(2,1)S(1)} %bitcast.22, bf16[4,4,272,256]{3,2,1,0:T(8,128)(2,1)S(1)} %collective-permute-done.7.refs_2_.refs_4_), custom_call_target="tpu_custom_call" | custom-call | flops 1 | bytes 1 | tf_op jit(solution)/shard_map/back_project/back_project/pallas_call | solution.py:337
  135.3 1.8 %collective-permute-done.5.refs_1_ = bf16[4,128,256]{2,1,0:T(8,128)(2,1)S(1)} collective-permute-done((bf16[4,128,256]{2,1,0:T(8,128)(2,1)S(1)}, bf16[4,128,256]{2,1,0:T(8,128)(2,1)S(1)}, u32[]{:S(2)}, u32[]{:S(2)}) %collective-permute-start.5) | collective-permute-done | bytes 262176 | tf_op jit(solution)/shard_map/gather_posteriors/ppermute | solution.py:420
  137.2 4.9 %collective-permute-done.6.refs_2_ = bf16[4,128,256]{2,1,0:T(8,128)(2,1)S(1)} collective-permute-done((bf16[4,128,256]{2,1,0:T(8,128)(2,1)S(1)}, bf16[4,128,256]{2,1,0:T(8,128)(2,1)S(1)}, u32[]{:S(2)}, u32[]{:S(2)}) %collective-permute-start.6) | collective-permute-done | bytes 262176 | tf_op jit(solution)/shard_map/gather_posteriors/ppermute | solution.py:420
  142.0 1.8 %back_project.3 = f32[3,128,256]{2,1,0:T(8,128)} custom-call(s32[1]{0:T(128)} %bitcast.12.start_ref, bf16[4,128,256]{2,1,0:T(8,128)(2,1)S(1)} %collective-permute-done.4.refs_0_, bf16[4,128,256]{2,1,0:T(8,128)(2,1)S(1)} %collective-permute-done.5.refs_1_, bf16[4,128,256]{2,1,0:T(8,128)(2,1)S(1)} %collective-permute-done.6.refs_2_, ...), custom_call_target="tpu_custom_call" | custom-call | flops 1 | bytes 1 | tf_op jit(solution)/shard_map/back_project/back_project/pallas_call | solution.py:337
  (38 shorter events, 2.5 us)
Async XLA Ops:
  7.2 68.7 %all-gather.7.cloned.1.call-start = ((), (), s32[]{:S(2)}) async-start(), calls=%async_computation.1 | async-start | bytes 2621440 | tf_op jit(solution)/shard_map/gather_projections/all_gather | solution.py:376
  42.4 77.2 %all-gather.9.cloned.1.call-start = ((), (), s32[]{:S(2)}) async-start(), calls=%async_computation.2 | async-start | bytes 2785280 | tf_op jit(solution)/shard_map/gather_images/all_gather | solution.py:409
  44.8 10.8 %collective-permute-start = (bf16[272,256]{1,0:T(8,128)(2,1)S(1)}, bf16[272,256]{1,0:T(8,128)(2,1)S(1)}, u32[]{:S(2)}, u32[]{:S(2)}) collective-permute-start(bf16[272,256]{1,0:T(8,128)(2,1)S(1)} %pad_maximum_fusion.1), channel_id=1, source_target_pairs={{0,0},{1,1},{2,32},{3,33},{4,64},{5,65},{6,96},{7,97},{8,136},{9,1... | collective-permute-start | bytes 417800 | tf_op jit(solution)/shard_map/exchange_images/ppermute | solution.py:387
  47.9 7.3 %copy-start.6 = (f32[64]{0:T(128)S(1)}, f32[64]{0:T(128)}, u32[]{:S(2)}) copy-start(f32[64]{0:T(128)} %param.12) | copy-start | bytes 772
  47.9 7.3 %copy-start.7 = (s32[128]{0:T(128)S(1)}, s32[128]{0:T(128)}, u32[]{:S(2)}) copy-start(s32[128]{0:T(128)} %param.13) | copy-start | bytes 1540
  47.9 7.4 %copy-start.4 = (s32[256,256]{1,0:T(8,128)S(1)}, s32[256,256]{1,0:T(8,128)}, u32[]{:S(2)}) copy-start(s32[256,256]{1,0:T(8,128)} %param.15) | copy-start | bytes 786436
  47.9 7.4 %copy-start.5 = (s32[128]{0:T(128)S(1)}, s32[128]{0:T(128)}, u32[]{:S(2)}) copy-start(s32[128]{0:T(128)} %param.14) | copy-start | bytes 1540
  55.2 20.7 %copy-start.2 = (f32[128,256]{1,0:T(8,128)S(1)}, f32[128,256]{1,0:T(8,128)}, u32[]{:S(2)}) copy-start(f32[128,256]{1,0:T(8,128)} %get-tuple-element.27.part_hbm) | copy-start | bytes 393220
  55.6 16.6 %collective-permute-start.1 = (bf16[272,256]{1,0:T(8,128)(2,1)S(1)}, bf16[272,256]{1,0:T(8,128)(2,1)S(1)}, u32[]{:S(2)}, u32[]{:S(2)}) collective-permute-start(bf16[272,256]{1,0:T(8,128)(2,1)S(1)} %collective-permute-done), channel_id=1, source_target_pairs={{0,2},{1,3},{2,4},{3,5},{4,6},{5,7},{6,0},{7,1},{8,10},{9,11},{10,... | collective-permute-start | bytes 417800 | tf_op jit(solution)/shard_map/gather_images/ppermute | solution.py:406
  62.4 9.8 %collective-permute-start.2 = (bf16[272,256]{1,0:T(8,128)(2,1)S(1)}, bf16[272,256]{1,0:T(8,128)(2,1)S(1)}, u32[]{:S(2)}, u32[]{:S(2)}) collective-permute-start(bf16[272,256]{1,0:T(8,128)(2,1)S(1)} %collective-permute-done), channel_id=1, source_target_pairs={{0,4},{1,5},{2,6},{3,7},{4,0},{5,1},{6,2},{7,3},{8,12},{9,13},{10,... | collective-permute-start | bytes 417800 | tf_op jit(solution)/shard_map/gather_images/ppermute | solution.py:406
  67.6 7.1 %collective-permute-start.3 = (bf16[272,256]{1,0:T(8,128)(2,1)S(1)}, bf16[272,256]{1,0:T(8,128)(2,1)S(1)}, u32[]{:S(2)}, u32[]{:S(2)}) collective-permute-start(bf16[272,256]{1,0:T(8,128)(2,1)S(1)} %collective-permute-done), channel_id=1, source_target_pairs={{0,6},{1,7},{2,0},{3,1},{4,2},{5,3},{6,4},{7,5},{8,14},{9,15},{10,... | collective-permute-start | bytes 417800 | tf_op jit(solution)/shard_map/gather_images/ppermute | solution.py:406
  74.7 1.2 copy-start.3
  119.7 10.6 %collective-permute-start.7 = (bf16[4,4,272,256]{3,2,1,0:T(8,128)(2,1)}, bf16[4,4,272,256]{3,2,1,0:T(8,128)(2,1)S(1)}, u32[]{:S(2)}, u32[]{:S(2)}) collective-permute-start(bf16[4,4,272,256]{3,2,1,0:T(8,128)(2,1)} %bitcast.21), channel_id=1, source_target_pairs={{0,1},{1,0},{2,3},{3,2},{4,5},{5,4},{6,7},{7,6},{8,9},{9,8},{10,11... | collective-permute-start | bytes 6684680 | tf_op jit(solution)/shard_map/gather_posteriors/ppermute | solution.py:422
  121.6 13.7 %collective-permute-start.4 = (bf16[4,128,256]{2,1,0:T(8,128)(2,1)S(1)}, bf16[4,128,256]{2,1,0:T(8,128)(2,1)S(1)}, u32[]{:S(2)}, u32[]{:S(2)}) collective-permute-start(bf16[4,128,256]{2,1,0:T(8,128)(2,1)S(1)} %bitcast.24), channel_id=1, source_target_pairs={{0,128},{32,160},{64,192},{96,224},{128,256},{160,288},{192,320},{... | collective-permute-start | bytes 786440 | tf_op jit(solution)/shard_map/gather_posteriors/ppermute | solution.py:420
  124.6 12.6 %collective-permute-start.5 = (bf16[4,128,256]{2,1,0:T(8,128)(2,1)S(1)}, bf16[4,128,256]{2,1,0:T(8,128)(2,1)S(1)}, u32[]{:S(2)}, u32[]{:S(2)}) collective-permute-start(bf16[4,128,256]{2,1,0:T(8,128)(2,1)S(1)} %bitcast.25), channel_id=1, source_target_pairs={{0,256},{32,288},{64,320},{96,352},{128,384},{160,416},{192,448},{... | collective-permute-start | bytes 786440 | tf_op jit(solution)/shard_map/gather_posteriors/ppermute | solution.py:420
  128.3 13.7 %collective-permute-start.6 = (bf16[4,128,256]{2,1,0:T(8,128)(2,1)S(1)}, bf16[4,128,256]{2,1,0:T(8,128)(2,1)S(1)}, u32[]{:S(2)}, u32[]{:S(2)}) collective-permute-start(bf16[4,128,256]{2,1,0:T(8,128)(2,1)S(1)} %bitcast.26), channel_id=1, source_target_pairs={{0,384},{32,416},{64,448},{96,480},{128,0},{160,32},{192,64},{224,... | collective-permute-start | bytes 786440 | tf_op jit(solution)/shard_map/gather_posteriors/ppermute | solution.py:420
  130.3 1.6 %copy-start = (bf16[16,272,256]{2,1,0:T(8,128)(2,1)S(1)}, bf16[16,272,256]{2,1,0:T(8,128)(2,1)}, u32[]{:S(2)}) copy-start(bf16[16,272,256]{2,1,0:T(8,128)(2,1)} %all-gather.9.cloned.1.call-done) | copy-start | bytes 6684676
  131.9 10.1 %copy-start.1 = (bf16[16,272,256]{2,1,0:T(8,128)(2,1)S(1)}, bf16[16,272,256]{2,1,0:T(8,128)(2,1)}, u32[]{:S(2)}) copy-start(bf16[16,272,256]{2,1,0:T(8,128)(2,1)} %all-gather.9.cloned.1.call-done) | copy-start | bytes 6684676
Sparse Core Ops, SparseCore 0:
  42.6 33.2 all-gather.6
  78.0 41.6 all-gather.8

commit v7 on v6

--- a/solution.py
+++ b/solution.py
@@ -416,14 +416,14 @@
 
     with jax.named_scope("gather_posteriors"):
         post = [lax.all_gather(post_bf, "grp", axis=0, axis_index_groups=z_groups)] + [None] * 3
-        for d in (2, 1, 3):
+        for d in (1, 3, 2):
             post[d] = lax.ppermute(post[0], "grp", grp_shift(d))
         post[0], own = lax.optimization_barrier((post[0], own))
         other = lax.ppermute(own, "pose", pose_shift(0, 0, 1))
 
     with jax.named_scope("back_project"):
         start = group * slab
-        near, far, stacks = (0,), (1, 2, 3), (own, other)
+        near, far, stacks = (0,), (1, 3, 2), (own, other)
         before = back_project(start, width, near, [post[d] for d in near], stacks, ahead=far)
         (back_proj,) = back_project(start, width, far, [post[d] for d in far], stacks, before=before)
     return (posteriors, back_proj)

time: 152 us -> 151 us (level)
  transfers between devices with their start and end apart: 10 -> 10, of which waited for: 5 -> 4; matrix products, arithmetic and copies ran while one was open for 3% -> 3% of each run, Pallas kernels for 10% -> 10%
where the time goes in v7:
time: 151 us; the launch traced here: 150 us
  blocking collectives  73 us (48%)
  starting transfers between devices  28.4 us (19%)
  Pallas kernels  17.1 us (11%)
  between operations  14.3 us (9%)
  waiting for transfers between devices  10.9 us (7%)
  other arithmetic  4.8 us (3%)
  local copies, waits for them, and re-layouts  1.73 us (1%)
    all_gather x1, blocking collectives, on_device(): lax.all_gather(projections, 'grp', axis=0, axis_index_groups=z_groups)  35.2 us
    all_gather x1, blocking collectives, on_device(): lax.all_gather(post_bf, 'grp', axis=0, axis_index_groups=z_groups)  21.2 us
    all_to_all x1, blocking collectives, exchange(): return lax.all_to_all(copies, axis, 0, 0, axis_index_groups=groups)  16.7 us
    ppermute x3, starting transfers between devices, on_device(): block = lax.ppermute(share, 'pose', pose_shift(0, d, 0))  16.5 us
    ppermute x3, starting transfers between devices, on_device(): post[d] = lax.ppermute(post[0], 'grp', grp_shift(d))  9.2 us
    pallas_call x1, Pallas kernels, weight_images(): pl.pallas_call(weight_kernel, in_specs=[pl.BlockSpec(memory_space=pltpu.S...  7.24 us
    ppermute x3, waiting for transfers between devices, on_device(): post[d] = lax.ppermute(post[0], 'grp', grp_shift(d))  5.88 us
    pallas_call x2, Pallas kernels, back_project(): pl.pallas_call(functools.partial(back_kernel, sources, ahead, width), in_...  5.23 us
  transfers between devices with their start and end apart: 10, of which 4 were waited for; matrix products, arithmetic and copies ran while one was open for 3% of the time, Pallas kernels for 10%

profile of v7, /device:TPU:6, one launch (start us, length us, event | category | flops | bytes accessed | tf_op | source)
XLA Modules:
  0.0 150.4 jit_solution(17290176556978919741)
XLA Ops:
  7.2 35.2 %all-gather = bf16[8,128,256]{2,1,0:T(8,128)(2,1)} all-gather(bf16[2,128,256]{2,1,0:T(8,128)(2,1)} %param.9), channel_id=2, replica_groups={{0,32,64,96},{128,160,192,224},{256,288,320,352},{384,416,448,480},{1,3..., dimensions={0}, use_global_device_ids=true | all-gather | bytes 655360 | tf_op jit(solution)/shard_map/gather_projections/all_gather | solution.py:374
  42.5 0.8 fusion.14
  43.8 0.9 multiply_convert_fusion
  45.5 0.8 broadcast_multiply_fusion
  46.3 1.7 %fusion.1 = (f32[256,256]{1,0:T(8,128)}, f32[256,256]{1,0:T(8,128)}) fusion(f32[256,128]{1,0:T(8,128)S(1)} %get-tuple-element.43, f32[256,128]{1,0:T(8,128)S(1)} %get-tuple-element.42), kind=kLoop, calls=%fused_computation.4 | loop fusion | flops 65536 | bytes 786432 | tf_op jit(solution)/shard_map/weights/cos | solution.py:171
  47.9 7.2 %weight_images.1 = (bf16[2,256,4096]{2,1,0:T(8,128)(2,1)}, bf16[256,4096]{1,0:T(8,128)(2,1)}, f32[128,256]{1,0:T(8,128)}) custom-call(s32[1]{0:T(128)} %bitcast.1.x_ref, bf16[2,256,4096]{2,1,0:T(8,128)(2,1)} %images_hbm.1, f32[256,256]{1,0:T(8,128)} %get-tuple-element.41.sin_ref, f32[256,256]{1,0:T(8,128)} %get-tuple-element.40.cos_ref, f32[1,4096]{1,0:T(1,128)} %bitcast.32, ...), custom_call_target="tpu_custom_call" | custom-call | flops 1 | bytes 1 | tf_op jit(solution)/shard_map/weights/weight_images/pallas_call | solution.py:152
  55.6 6.9 %collective-permute-start.1 = (bf16[272,256]{1,0:T(8,128)(2,1)S(1)}, bf16[272,256]{1,0:T(8,128)(2,1)S(1)}, u32[]{:S(2)}, u32[]{:S(2)}) collective-permute-start(bf16[272,256]{1,0:T(8,128)(2,1)S(1)} %collective-permute-done), channel_id=1, source_target_pairs={{0,2},{1,3},{2,4},{3,5},{4,6},{5,7},{6,0},{7,1},{8,10},{9,11},{10,... | collective-permute-start | bytes 417800 | tf_op jit(solution)/shard_map/gather_images/ppermute | solution.py:406
  62.4 5.2 %collective-permute-start.2 = (bf16[272,256]{1,0:T(8,128)(2,1)S(1)}, bf16[272,256]{1,0:T(8,128)(2,1)S(1)}, u32[]{:S(2)}, u32[]{:S(2)}) collective-permute-start(bf16[272,256]{1,0:T(8,128)(2,1)S(1)} %collective-permute-done), channel_id=1, source_target_pairs={{0,4},{1,5},{2,6},{3,7},{4,0},{5,1},{6,2},{7,3},{8,12},{9,13},{10,... | collective-permute-start | bytes 417800 | tf_op jit(solution)/shard_map/gather_images/ppermute | solution.py:406
  67.6 4.5 %collective-permute-start.3 = (bf16[272,256]{1,0:T(8,128)(2,1)S(1)}, bf16[272,256]{1,0:T(8,128)(2,1)S(1)}, u32[]{:S(2)}, u32[]{:S(2)}) collective-permute-start(bf16[272,256]{1,0:T(8,128)(2,1)S(1)} %collective-permute-done), channel_id=1, source_target_pairs={{0,6},{1,7},{2,0},{3,1},{4,2},{5,3},{6,4},{7,5},{8,14},{9,15},{10,... | collective-permute-start | bytes 417800 | tf_op jit(solution)/shard_map/gather_images/ppermute | solution.py:406
  72.2 2.5 %collective-permute-done.3 = bf16[272,256]{1,0:T(8,128)(2,1)S(1)} collective-permute-done((bf16[272,256]{1,0:T(8,128)(2,1)S(1)}, bf16[272,256]{1,0:T(8,128)(2,1)S(1)}, u32[]{:S(2)}, u32[]{:S(2)}) %collective-permute-start.3) | collective-permute-done | bytes 139296 | tf_op jit(solution)/shard_map/gather_images/ppermute | solution.py:406
  74.7 1.2 all-gather.7.cloned.1.call-done
  75.9 3.8 %score.1 = (f32[128,256]{1,0:T(8,128)S(1)}, f32[32,1,256]{2,1,0:T(1,128)S(1)}) custom-call(s32[1]{0:T(128)} %bitcast.1.x_ref, bf16[4,4,2,128,256]{4,3,2,1,0:T(8,128)(2,1)} %bitcast.30, bf16[2,256,4096]{2,1,0:T(8,128)(2,1)} %get-tuple-element.25.weighted_hbm, bf16[256,4096]{1,0:T(8,128)(2,1)} %get-tuple-element.26.noise_hbm, f32[128,256]{1,0:T(8,128)S(1)} %copy-done.2, ...), custom_call_target="tpu_custom_call" | custom-call | flops 1 | bytes 1 | tf_op jit(solution)/shard_map/scores/score/pallas_call | solution.py:215
  79.7 16.7 %all_to_all.5.log_sums_ref = f32[32,1,256]{2,1,0:T(1,128)S(1)} all-to-all(f32[32,1,256]{2,1,0:T(1,128)S(1)} %get-tuple-element.30), channel_id=1, replica_groups=mesh['grp'=16,'pose'=32] {'pose'}, dimensions={0} | all-to-all | bytes 65536 | tf_op jit(solution)/shard_map/softmax/all_to_all | solution.py:351
  96.4 0.8 posterior.1
  97.2 21.2 %all-gather.2 = bf16[512,256]{1,0:T(8,128)(2,1)S(1)} all-gather(bf16[128,256]{1,0:T(8,128)(2,1)S(1)} %get-tuple-element.32), channel_id=4, replica_groups={{0,32,64,96},{128,160,192,224},{256,288,320,352},{384,416,448,480},{1,3..., dimensions={0}, use_global_device_ids=true | all-gather | bytes 327680 | tf_op jit(solution)/shard_map/gather_posteriors/all_gather | solution.py:418
  118.4 1.3 all-gather.9.cloned.1.call-done
  119.7 1.9 %collective-permute-start.7 = (bf16[4,4,272,256]{3,2,1,0:T(8,128)(2,1)}, bf16[4,4,272,256]{3,2,1,0:T(8,128)(2,1)S(1)}, u32[]{:S(2)}, u32[]{:S(2)}) collective-permute-start(bf16[4,4,272,256]{3,2,1,0:T(8,128)(2,1)} %bitcast.21), channel_id=1, source_target_pairs={{0,1},{1,0},{2,3},{3,2},{4,5},{5,4},{6,7},{7,6},{8,9},{9,8},{10,11... | collective-permute-start | bytes 6684680 | tf_op jit(solution)/shard_map/gather_posteriors/ppermute | solution.py:422
  121.6 3.0 %collective-permute-start.4 = (bf16[4,128,256]{2,1,0:T(8,128)(2,1)S(1)}, bf16[4,128,256]{2,1,0:T(8,128)(2,1)S(1)}, u32[]{:S(2)}, u32[]{:S(2)}) collective-permute-start(bf16[4,128,256]{2,1,0:T(8,128)(2,1)S(1)} %bitcast.24), channel_id=1, source_target_pairs={{0,128},{32,160},{64,192},{96,224},{128,256},{160,288},{192,320},{... | collective-permute-start | bytes 786440 | tf_op jit(solution)/shard_map/gather_posteriors/ppermute | solution.py:420
  124.6 2.8 %collective-permute-start.5 = (bf16[4,128,256]{2,1,0:T(8,128)(2,1)S(1)}, bf16[4,128,256]{2,1,0:T(8,128)(2,1)S(1)}, u32[]{:S(2)}, u32[]{:S(2)}) collective-permute-start(bf16[4,128,256]{2,1,0:T(8,128)(2,1)S(1)} %bitcast.25), channel_id=1, source_target_pairs={{0,384},{32,416},{64,448},{96,480},{128,0},{160,32},{192,64},{224,... | collective-permute-start | bytes 786440 | tf_op jit(solution)/shard_map/gather_posteriors/ppermute | solution.py:420
  127.4 3.4 %collective-permute-start.6 = (bf16[4,128,256]{2,1,0:T(8,128)(2,1)S(1)}, bf16[4,128,256]{2,1,0:T(8,128)(2,1)S(1)}, u32[]{:S(2)}, u32[]{:S(2)}) collective-permute-start(bf16[4,128,256]{2,1,0:T(8,128)(2,1)S(1)} %bitcast.26), channel_id=1, source_target_pairs={{0,256},{32,288},{64,320},{96,352},{128,384},{160,416},{192,448},{... | collective-permute-start | bytes 786440 | tf_op jit(solution)/shard_map/gather_posteriors/ppermute | solution.py:420
  130.8 1.6 %copy-done = bf16[16,272,256]{2,1,0:T(8,128)(2,1)S(1)} copy-done((bf16[16,272,256]{2,1,0:T(8,128)(2,1)S(1)}, bf16[16,272,256]{2,1,0:T(8,128)(2,1)}, u32[]{:S(2)}) %copy-start) | copy-done | bytes 2228248
  132.4 3.4 %back_project.2 = (f32[3,128,256]{2,1,0:T(8,128)S(1)}, bf16[3,256,1024]{2,1,0:T(8,128)(2,1)S(1)}) custom-call(s32[1]{0:T(128)} %bitcast.12.start_ref, bf16[4,128,256]{2,1,0:T(8,128)(2,1)S(1)} %bitcast.27, bf16[4,4,272,256]{3,2,1,0:T(8,128)(2,1)S(1)} %bitcast.22, bf16[4,4,272,256]{3,2,1,0:T(8,128)(2,1)S(1)} %collective-permute-done.7.refs_2_.refs_4_), custom_call_target="tpu_custom_call" | custom-call | flops 1 | bytes 1 | tf_op jit(solution)/shard_map/back_project/back_project/pallas_call | solution.py:337
  135.9 5.9 %collective-permute-done.5.refs_1_ = bf16[4,128,256]{2,1,0:T(8,128)(2,1)S(1)} collective-permute-done((bf16[4,128,256]{2,1,0:T(8,128)(2,1)S(1)}, bf16[4,128,256]{2,1,0:T(8,128)(2,1)S(1)}, u32[]{:S(2)}, u32[]{:S(2)}) %collective-permute-start.5) | collective-permute-done | bytes 262176 | tf_op jit(solution)/shard_map/gather_posteriors/ppermute | solution.py:420
  141.8 1.8 %back_project.3 = f32[3,128,256]{2,1,0:T(8,128)} custom-call(s32[1]{0:T(128)} %bitcast.12.start_ref, bf16[4,128,256]{2,1,0:T(8,128)(2,1)S(1)} %collective-permute-done.4.refs_0_, bf16[4,128,256]{2,1,0:T(8,128)(2,1)S(1)} %collective-permute-done.5.refs_1_, bf16[4,128,256]{2,1,0:T(8,128)(2,1)S(1)} %collective-permute-done.6.refs_2_, ...), custom_call_target="tpu_custom_call" | custom-call | flops 1 | bytes 1 | tf_op jit(solution)/shard_map/back_project/back_project/pallas_call | solution.py:337
  (38 shorter events, 1.8 us)
Async XLA Ops:
  7.2 68.7 %all-gather.7.cloned.1.call-start = ((), (), s32[]{:S(2)}) async-start(), calls=%async_computation.1 | async-start | bytes 2621440 | tf_op jit(solution)/shard_map/gather_projections/all_gather | solution.py:376
  42.4 77.2 %all-gather.9.cloned.1.call-start = ((), (), s32[]{:S(2)}) async-start(), calls=%async_computation.2 | async-start | bytes 2785280 | tf_op jit(solution)/shard_map/gather_images/all_gather | solution.py:409
  44.8 10.8 %collective-permute-start = (bf16[272,256]{1,0:T(8,128)(2,1)S(1)}, bf16[272,256]{1,0:T(8,128)(2,1)S(1)}, u32[]{:S(2)}, u32[]{:S(2)}) collective-permute-start(bf16[272,256]{1,0:T(8,128)(2,1)S(1)} %pad_maximum_fusion.1), channel_id=1, source_target_pairs={{0,0},{1,1},{2,32},{3,33},{4,64},{5,65},{6,96},{7,97},{8,136},{9,1... | collective-permute-start | bytes 417800 | tf_op jit(solution)/shard_map/exchange_images/ppermute | solution.py:387
  47.9 7.3 %copy-start.6 = (f32[64]{0:T(128)S(1)}, f32[64]{0:T(128)}, u32[]{:S(2)}) copy-start(f32[64]{0:T(128)} %param.12) | copy-start | bytes 772
  47.9 7.3 %copy-start.7 = (s32[128]{0:T(128)S(1)}, s32[128]{0:T(128)}, u32[]{:S(2)}) copy-start(s32[128]{0:T(128)} %param.13) | copy-start | bytes 1540
  47.9 7.4 %copy-start.4 = (s32[256,256]{1,0:T(8,128)S(1)}, s32[256,256]{1,0:T(8,128)}, u32[]{:S(2)}) copy-start(s32[256,256]{1,0:T(8,128)} %param.15) | copy-start | bytes 786436
  47.9 7.4 %copy-start.5 = (s32[128]{0:T(128)S(1)}, s32[128]{0:T(128)}, u32[]{:S(2)}) copy-start(s32[128]{0:T(128)} %param.14) | copy-start | bytes 1540
  55.2 20.7 %copy-start.2 = (f32[128,256]{1,0:T(8,128)S(1)}, f32[128,256]{1,0:T(8,128)}, u32[]{:S(2)}) copy-start(f32[128,256]{1,0:T(8,128)} %get-tuple-element.27.part_hbm) | copy-start | bytes 393220
  55.6 16.6 %collective-permute-start.1 = (bf16[272,256]{1,0:T(8,128)(2,1)S(1)}, bf16[272,256]{1,0:T(8,128)(2,1)S(1)}, u32[]{:S(2)}, u32[]{:S(2)}) collective-permute-start(bf16[272,256]{1,0:T(8,128)(2,1)S(1)} %collective-permute-done), channel_id=1, source_target_pairs={{0,2},{1,3},{2,4},{3,5},{4,6},{5,7},{6,0},{7,1},{8,10},{9,11},{10,... | collective-permute-start | bytes 417800 | tf_op jit(solution)/shard_map/gather_images/ppermute | solution.py:406
  62.4 9.8 %collective-permute-start.2 = (bf16[272,256]{1,0:T(8,128)(2,1)S(1)}, bf16[272,256]{1,0:T(8,128)(2,1)S(1)}, u32[]{:S(2)}, u32[]{:S(2)}) collective-permute-start(bf16[272,256]{1,0:T(8,128)(2,1)S(1)} %collective-permute-done), channel_id=1, source_target_pairs={{0,4},{1,5},{2,6},{3,7},{4,0},{5,1},{6,2},{7,3},{8,12},{9,13},{10,... | collective-permute-start | bytes 417800 | tf_op jit(solution)/shard_map/gather_images/ppermute | solution.py:406
  67.6 7.1 %collective-permute-start.3 = (bf16[272,256]{1,0:T(8,128)(2,1)S(1)}, bf16[272,256]{1,0:T(8,128)(2,1)S(1)}, u32[]{:S(2)}, u32[]{:S(2)}) collective-permute-start(bf16[272,256]{1,0:T(8,128)(2,1)S(1)} %collective-permute-done), channel_id=1, source_target_pairs={{0,6},{1,7},{2,0},{3,1},{4,2},{5,3},{6,4},{7,5},{8,14},{9,15},{10,... | collective-permute-start | bytes 417800 | tf_op jit(solution)/shard_map/gather_images/ppermute | solution.py:406
  74.7 1.2 copy-start.3
  119.7 11.1 %collective-permute-start.7 = (bf16[4,4,272,256]{3,2,1,0:T(8,128)(2,1)}, bf16[4,4,272,256]{3,2,1,0:T(8,128)(2,1)S(1)}, u32[]{:S(2)}, u32[]{:S(2)}) collective-permute-start(bf16[4,4,272,256]{3,2,1,0:T(8,128)(2,1)} %bitcast.21), channel_id=1, source_target_pairs={{0,1},{1,0},{2,3},{3,2},{4,5},{5,4},{6,7},{7,6},{8,9},{9,8},{10,11... | collective-permute-start | bytes 6684680 | tf_op jit(solution)/shard_map/gather_posteriors/ppermute | solution.py:422
  121.6 14.3 %collective-permute-start.4 = (bf16[4,128,256]{2,1,0:T(8,128)(2,1)S(1)}, bf16[4,128,256]{2,1,0:T(8,128)(2,1)S(1)}, u32[]{:S(2)}, u32[]{:S(2)}) collective-permute-start(bf16[4,128,256]{2,1,0:T(8,128)(2,1)S(1)} %bitcast.24), channel_id=1, source_target_pairs={{0,128},{32,160},{64,192},{96,224},{128,256},{160,288},{192,320},{... | collective-permute-start | bytes 786440 | tf_op jit(solution)/shard_map/gather_posteriors/ppermute | solution.py:420
  124.6 17.2 %collective-permute-start.5 = (bf16[4,128,256]{2,1,0:T(8,128)(2,1)S(1)}, bf16[4,128,256]{2,1,0:T(8,128)(2,1)S(1)}, u32[]{:S(2)}, u32[]{:S(2)}) collective-permute-start(bf16[4,128,256]{2,1,0:T(8,128)(2,1)S(1)} %bitcast.25), channel_id=1, source_target_pairs={{0,384},{32,416},{64,448},{96,480},{128,0},{160,32},{192,64},{224,... | collective-permute-start | bytes 786440 | tf_op jit(solution)/shard_map/gather_posteriors/ppermute | solution.py:420
  127.4 14.3 %collective-permute-start.6 = (bf16[4,128,256]{2,1,0:T(8,128)(2,1)S(1)}, bf16[4,128,256]{2,1,0:T(8,128)(2,1)S(1)}, u32[]{:S(2)}, u32[]{:S(2)}) collective-permute-start(bf16[4,128,256]{2,1,0:T(8,128)(2,1)S(1)} %bitcast.26), channel_id=1, source_target_pairs={{0,256},{32,288},{64,320},{96,352},{128,384},{160,416},{192,448},{... | collective-permute-start | bytes 786440 | tf_op jit(solution)/shard_map/gather_posteriors/ppermute | solution.py:420
  130.8 1.6 %copy-start = (bf16[16,272,256]{2,1,0:T(8,128)(2,1)S(1)}, bf16[16,272,256]{2,1,0:T(8,128)(2,1)}, u32[]{:S(2)}) copy-start(bf16[16,272,256]{2,1,0:T(8,128)(2,1)} %all-gather.9.cloned.1.call-done) | copy-start | bytes 6684676
  132.4 9.3 %copy-start.1 = (bf16[16,272,256]{2,1,0:T(8,128)(2,1)S(1)}, bf16[16,272,256]{2,1,0:T(8,128)(2,1)}, u32[]{:S(2)}) copy-start(bf16[16,272,256]{2,1,0:T(8,128)(2,1)} %all-gather.9.cloned.1.call-done) | copy-start | bytes 6684676
Sparse Core Ops, SparseCore 0:
  42.6 33.2 all-gather.6
  78.0 41.6 all-gather.8

commit v8 on v6

--- a/solution.py
+++ b/solution.py
@@ -416,7 +416,7 @@
 
     with jax.named_scope("gather_posteriors"):
         post = [lax.all_gather(post_bf, "grp", axis=0, axis_index_groups=z_groups)] + [None] * 3
-        for d in (2, 1, 3):
+        for d in (1, 2, 3):
             post[d] = lax.ppermute(post[0], "grp", grp_shift(d))
         post[0], own = lax.optimization_barrier((post[0], own))
         other = lax.ppermute(own, "pose", pose_shift(0, 0, 1))

time: 152 us -> 152 us (level)
  no operation moved by 1% of the time
where the time goes in v8:
time: 152 us; the launch traced here: 151 us
  blocking collectives  73 us (48%)
  starting transfers between devices  27.8 us (18%)
  Pallas kernels  17.1 us (11%)
  between operations  14.3 us (9%)
  waiting for transfers between devices  11.7 us (8%)
  other arithmetic  4.8 us (3%)
  local copies, waits for them, and re-layouts  1.73 us (1%)
    all_gather x1, blocking collectives, on_device(): lax.all_gather(projections, 'grp', axis=0, axis_index_groups=z_groups)  35.2 us
    all_gather x1, blocking collectives, on_device(): lax.all_gather(post_bf, 'grp', axis=0, axis_index_groups=z_groups)  21.2 us
    all_to_all x1, blocking collectives, exchange(): return lax.all_to_all(copies, axis, 0, 0, axis_index_groups=groups)  16.7 us
    ppermute x3, starting transfers between devices, on_device(): block = lax.ppermute(share, 'pose', pose_shift(0, d, 0))  16.5 us
    ppermute x3, starting transfers between devices, on_device(): post[d] = lax.ppermute(post[0], 'grp', grp_shift(d))  8.66 us
    pallas_call x1, Pallas kernels, weight_images(): pl.pallas_call(weight_kernel, in_specs=[pl.BlockSpec(memory_space=pltpu.S...  7.24 us
    ppermute x3, waiting for transfers between devices, on_device(): post[d] = lax.ppermute(post[0], 'grp', grp_shift(d))  6.72 us
    pallas_call x2, Pallas kernels, back_project(): pl.pallas_call(functools.partial(back_kernel, sources, ahead, width), in_...  5.24 us
  transfers between devices with their start and end apart: 10, of which 5 were waited for; matrix products, arithmetic and copies ran while one was open for 3% of the time, Pallas kernels for 10%

profile of v8, /device:TPU:6, one launch (start us, length us, event | category | flops | bytes accessed | tf_op | source)
XLA Modules:
  0.0 150.7 jit_solution(6920799093850675799)
XLA Ops:
  7.2 35.2 %all-gather = bf16[8,128,256]{2,1,0:T(8,128)(2,1)} all-gather(bf16[2,128,256]{2,1,0:T(8,128)(2,1)} %param.9), channel_id=2, replica_groups={{0,32,64,96},{128,160,192,224},{256,288,320,352},{384,416,448,480},{1,3..., dimensions={0}, use_global_device_ids=true | all-gather | bytes 655360 | tf_op jit(solution)/shard_map/gather_projections/all_gather | solution.py:374
  43.8 0.9 multiply_convert_fusion
  45.5 0.8 broadcast_multiply_fusion
  46.3 1.7 %fusion.1 = (f32[256,256]{1,0:T(8,128)}, f32[256,256]{1,0:T(8,128)}) fusion(f32[256,128]{1,0:T(8,128)S(1)} %get-tuple-element.43, f32[256,128]{1,0:T(8,128)S(1)} %get-tuple-element.42), kind=kLoop, calls=%fused_computation.4 | loop fusion | flops 65536 | bytes 786432 | tf_op jit(solution)/shard_map/weights/cos | solution.py:171
  47.9 7.2 %weight_images.1 = (bf16[2,256,4096]{2,1,0:T(8,128)(2,1)}, bf16[256,4096]{1,0:T(8,128)(2,1)}, f32[128,256]{1,0:T(8,128)}) custom-call(s32[1]{0:T(128)} %bitcast.1.x_ref, bf16[2,256,4096]{2,1,0:T(8,128)(2,1)} %images_hbm.1, f32[256,256]{1,0:T(8,128)} %get-tuple-element.41.sin_ref, f32[256,256]{1,0:T(8,128)} %get-tuple-element.40.cos_ref, f32[1,4096]{1,0:T(1,128)} %bitcast.32, ...), custom_call_target="tpu_custom_call" | custom-call | flops 1 | bytes 1 | tf_op jit(solution)/shard_map/weights/weight_images/pallas_call | solution.py:152
  55.6 6.9 %collective-permute-start.1 = (bf16[272,256]{1,0:T(8,128)(2,1)S(1)}, bf16[272,256]{1,0:T(8,128)(2,1)S(1)}, u32[]{:S(2)}, u32[]{:S(2)}) collective-permute-start(bf16[272,256]{1,0:T(8,128)(2,1)S(1)} %collective-permute-done), channel_id=1, source_target_pairs={{0,2},{1,3},{2,4},{3,5},{4,6},{5,7},{6,0},{7,1},{8,10},{9,11},{10,... | collective-permute-start | bytes 417800 | tf_op jit(solution)/shard_map/gather_images/ppermute | solution.py:406
  62.4 5.2 %collective-permute-start.2 = (bf16[272,256]{1,0:T(8,128)(2,1)S(1)}, bf16[272,256]{1,0:T(8,128)(2,1)S(1)}, u32[]{:S(2)}, u32[]{:S(2)}) collective-permute-start(bf16[272,256]{1,0:T(8,128)(2,1)S(1)} %collective-permute-done), channel_id=1, source_target_pairs={{0,4},{1,5},{2,6},{3,7},{4,0},{5,1},{6,2},{7,3},{8,12},{9,13},{10,... | collective-permute-start | bytes 417800 | tf_op jit(solution)/shard_map/gather_images/ppermute | solution.py:406
  67.6 4.5 %collective-permute-start.3 = (bf16[272,256]{1,0:T(8,128)(2,1)S(1)}, bf16[272,256]{1,0:T(8,128)(2,1)S(1)}, u32[]{:S(2)}, u32[]{:S(2)}) collective-permute-start(bf16[272,256]{1,0:T(8,128)(2,1)S(1)} %collective-permute-done), channel_id=1, source_target_pairs={{0,6},{1,7},{2,0},{3,1},{4,2},{5,3},{6,4},{7,5},{8,14},{9,15},{10,... | collective-permute-start | bytes 417800 | tf_op jit(solution)/shard_map/gather_images/ppermute | solution.py:406
  72.2 2.5 %collective-permute-done.3 = bf16[272,256]{1,0:T(8,128)(2,1)S(1)} collective-permute-done((bf16[272,256]{1,0:T(8,128)(2,1)S(1)}, bf16[272,256]{1,0:T(8,128)(2,1)S(1)}, u32[]{:S(2)}, u32[]{:S(2)}) %collective-permute-start.3) | collective-permute-done | bytes 139296 | tf_op jit(solution)/shard_map/gather_images/ppermute | solution.py:406
  74.7 1.2 all-gather.7.cloned.1.call-done
  75.9 3.8 %score.1 = (f32[128,256]{1,0:T(8,128)S(1)}, f32[32,1,256]{2,1,0:T(1,128)S(1)}) custom-call(s32[1]{0:T(128)} %bitcast.1.x_ref, bf16[4,4,2,128,256]{4,3,2,1,0:T(8,128)(2,1)} %bitcast.30, bf16[2,256,4096]{2,1,0:T(8,128)(2,1)} %get-tuple-element.25.weighted_hbm, bf16[256,4096]{1,0:T(8,128)(2,1)} %get-tuple-element.26.noise_hbm, f32[128,256]{1,0:T(8,128)S(1)} %copy-done.2, ...), custom_call_target="tpu_custom_call" | custom-call | flops 1 | bytes 1 | tf_op jit(solution)/shard_map/scores/score/pallas_call | solution.py:215
  79.7 16.7 %all_to_all.5.log_sums_ref = f32[32,1,256]{2,1,0:T(1,128)S(1)} all-to-all(f32[32,1,256]{2,1,0:T(1,128)S(1)} %get-tuple-element.30), channel_id=1, replica_groups=mesh['grp'=16,'pose'=32] {'pose'}, dimensions={0} | all-to-all | bytes 65536 | tf_op jit(solution)/shard_map/softmax/all_to_all | solution.py:351
  96.4 0.8 posterior.1
  97.2 21.2 %all-gather.2 = bf16[512,256]{1,0:T(8,128)(2,1)S(1)} all-gather(bf16[128,256]{1,0:T(8,128)(2,1)S(1)} %get-tuple-element.32), channel_id=4, replica_groups={{0,32,64,96},{128,160,192,224},{256,288,320,352},{384,416,448,480},{1,3..., dimensions={0}, use_global_device_ids=true | all-gather | bytes 327680 | tf_op jit(solution)/shard_map/gather_posteriors/all_gather | solution.py:418
  118.4 1.3 all-gather.9.cloned.1.call-done
  119.7 1.9 %collective-permute-start.7 = (bf16[4,4,272,256]{3,2,1,0:T(8,128)(2,1)}, bf16[4,4,272,256]{3,2,1,0:T(8,128)(2,1)S(1)}, u32[]{:S(2)}, u32[]{:S(2)}) collective-permute-start(bf16[4,4,272,256]{3,2,1,0:T(8,128)(2,1)} %bitcast.21), channel_id=1, source_target_pairs={{0,1},{1,0},{2,3},{3,2},{4,5},{5,4},{6,7},{7,6},{8,9},{9,8},{10,11... | collective-permute-start | bytes 6684680 | tf_op jit(solution)/shard_map/gather_posteriors/ppermute | solution.py:422
  121.6 3.0 %collective-permute-start.4 = (bf16[4,128,256]{2,1,0:T(8,128)(2,1)S(1)}, bf16[4,128,256]{2,1,0:T(8,128)(2,1)S(1)}, u32[]{:S(2)}, u32[]{:S(2)}) collective-permute-start(bf16[4,128,256]{2,1,0:T(8,128)(2,1)S(1)} %bitcast.24), channel_id=1, source_target_pairs={{0,128},{32,160},{64,192},{96,224},{128,256},{160,288},{192,320},{... | collective-permute-start | bytes 786440 | tf_op jit(solution)/shard_map/gather_posteriors/ppermute | solution.py:420
  124.6 3.7 %collective-permute-start.5 = (bf16[4,128,256]{2,1,0:T(8,128)(2,1)S(1)}, bf16[4,128,256]{2,1,0:T(8,128)(2,1)S(1)}, u32[]{:S(2)}, u32[]{:S(2)}) collective-permute-start(bf16[4,128,256]{2,1,0:T(8,128)(2,1)S(1)} %bitcast.25), channel_id=1, source_target_pairs={{0,256},{32,288},{64,320},{96,352},{128,384},{160,416},{192,448},{... | collective-permute-start | bytes 786440 | tf_op jit(solution)/shard_map/gather_posteriors/ppermute | solution.py:420
  128.3 1.9 %collective-permute-start.6 = (bf16[4,128,256]{2,1,0:T(8,128)(2,1)S(1)}, bf16[4,128,256]{2,1,0:T(8,128)(2,1)S(1)}, u32[]{:S(2)}, u32[]{:S(2)}) collective-permute-start(bf16[4,128,256]{2,1,0:T(8,128)(2,1)S(1)} %bitcast.26), channel_id=1, source_target_pairs={{0,384},{32,416},{64,448},{96,480},{128,0},{160,32},{192,64},{224,... | collective-permute-start | bytes 786440 | tf_op jit(solution)/shard_map/gather_posteriors/ppermute | solution.py:420
  130.3 1.6 %copy-done = bf16[16,272,256]{2,1,0:T(8,128)(2,1)S(1)} copy-done((bf16[16,272,256]{2,1,0:T(8,128)(2,1)S(1)}, bf16[16,272,256]{2,1,0:T(8,128)(2,1)}, u32[]{:S(2)}) %copy-start) | copy-done | bytes 2228248
  131.9 3.4 %back_project.2 = (f32[3,128,256]{2,1,0:T(8,128)S(1)}, bf16[3,256,1024]{2,1,0:T(8,128)(2,1)S(1)}) custom-call(s32[1]{0:T(128)} %bitcast.12.start_ref, bf16[4,128,256]{2,1,0:T(8,128)(2,1)S(1)} %bitcast.27, bf16[4,4,272,256]{3,2,1,0:T(8,128)(2,1)S(1)} %bitcast.22, bf16[4,4,272,256]{3,2,1,0:T(8,128)(2,1)S(1)} %collective-permute-done.7.refs_2_.refs_4_), custom_call_target="tpu_custom_call" | custom-call | flops 1 | bytes 1 | tf_op jit(solution)/shard_map/back_project/back_project/pallas_call | solution.py:337
  135.3 1.8 %collective-permute-done.5.refs_1_ = bf16[4,128,256]{2,1,0:T(8,128)(2,1)S(1)} collective-permute-done((bf16[4,128,256]{2,1,0:T(8,128)(2,1)S(1)}, bf16[4,128,256]{2,1,0:T(8,128)(2,1)S(1)}, u32[]{:S(2)}, u32[]{:S(2)}) %collective-permute-start.5) | collective-permute-done | bytes 262176 | tf_op jit(solution)/shard_map/gather_posteriors/ppermute | solution.py:420
  137.2 4.9 %collective-permute-done.6.refs_2_ = bf16[4,128,256]{2,1,0:T(8,128)(2,1)S(1)} collective-permute-done((bf16[4,128,256]{2,1,0:T(8,128)(2,1)S(1)}, bf16[4,128,256]{2,1,0:T(8,128)(2,1)S(1)}, u32[]{:S(2)}, u32[]{:S(2)}) %collective-permute-start.6) | collective-permute-done | bytes 262176 | tf_op jit(solution)/shard_map/gather_posteriors/ppermute | solution.py:420
  142.0 1.8 %back_project.3 = f32[3,128,256]{2,1,0:T(8,128)} custom-call(s32[1]{0:T(128)} %bitcast.12.start_ref, bf16[4,128,256]{2,1,0:T(8,128)(2,1)S(1)} %collective-permute-done.4.refs_0_, bf16[4,128,256]{2,1,0:T(8,128)(2,1)S(1)} %collective-permute-done.5.refs_1_, bf16[4,128,256]{2,1,0:T(8,128)(2,1)S(1)} %collective-permute-done.6.refs_2_, ...), custom_call_target="tpu_custom_call" | custom-call | flops 1 | bytes 1 | tf_op jit(solution)/shard_map/back_project/back_project/pallas_call | solution.py:337
  (38 shorter events, 2.5 us)
Async XLA Ops:
  7.2 68.7 %all-gather.7.cloned.1.call-start = ((), (), s32[]{:S(2)}) async-start(), calls=%async_computation.1 | async-start | bytes 2621440 | tf_op jit(solution)/shard_map/gather_projections/all_gather | solution.py:376
  42.4 77.2 %all-gather.9.cloned.1.call-start = ((), (), s32[]{:S(2)}) async-start(), calls=%async_computation.2 | async-start | bytes 2785280 | tf_op jit(solution)/shard_map/gather_images/all_gather | solution.py:409
  44.8 10.8 %collective-permute-start = (bf16[272,256]{1,0:T(8,128)(2,1)S(1)}, bf16[272,256]{1,0:T(8,128)(2,1)S(1)}, u32[]{:S(2)}, u32[]{:S(2)}) collective-permute-start(bf16[272,256]{1,0:T(8,128)(2,1)S(1)} %pad_maximum_fusion.1), channel_id=1, source_target_pairs={{0,0},{1,1},{2,32},{3,33},{4,64},{5,65},{6,96},{7,97},{8,136},{9,1... | collective-permute-start | bytes 417800 | tf_op jit(solution)/shard_map/exchange_images/ppermute | solution.py:387
  47.9 7.3 %copy-start.6 = (f32[64]{0:T(128)S(1)}, f32[64]{0:T(128)}, u32[]{:S(2)}) copy-start(f32[64]{0:T(128)} %param.12) | copy-start | bytes 772
  47.9 7.3 %copy-start.7 = (s32[128]{0:T(128)S(1)}, s32[128]{0:T(128)}, u32[]{:S(2)}) copy-start(s32[128]{0:T(128)} %param.13) | copy-start | bytes 1540
  47.9 7.4 %copy-start.4 = (s32[256,256]{1,0:T(8,128)S(1)}, s32[256,256]{1,0:T(8,128)}, u32[]{:S(2)}) copy-start(s32[256,256]{1,0:T(8,128)} %param.15) | copy-start | bytes 786436
  47.9 7.4 %copy-start.5 = (s32[128]{0:T(128)S(1)}, s32[128]{0:T(128)}, u32[]{:S(2)}) copy-start(s32[128]{0:T(128)} %param.14) | copy-start | bytes 1540
  55.2 20.7 %copy-start.2 = (f32[128,256]{1,0:T(8,128)S(1)}, f32[128,256]{1,0:T(8,128)}, u32[]{:S(2)}) copy-start(f32[128,256]{1,0:T(8,128)} %get-tuple-element.27.part_hbm) | copy-start | bytes 393220
  55.6 16.6 %collective-permute-start.1 = (bf16[272,256]{1,0:T(8,128)(2,1)S(1)}, bf16[272,256]{1,0:T(8,128)(2,1)S(1)}, u32[]{:S(2)}, u32[]{:S(2)}) collective-permute-start(bf16[272,256]{1,0:T(8,128)(2,1)S(1)} %collective-permute-done), channel_id=1, source_target_pairs={{0,2},{1,3},{2,4},{3,5},{4,6},{5,7},{6,0},{7,1},{8,10},{9,11},{10,... | collective-permute-start | bytes 417800 | tf_op jit(solution)/shard_map/gather_images/ppermute | solution.py:406
  62.4 9.8 %collective-permute-start.2 = (bf16[272,256]{1,0:T(8,128)(2,1)S(1)}, bf16[272,256]{1,0:T(8,128)(2,1)S(1)}, u32[]{:S(2)}, u32[]{:S(2)}) collective-permute-start(bf16[272,256]{1,0:T(8,128)(2,1)S(1)} %collective-permute-done), channel_id=1, source_target_pairs={{0,4},{1,5},{2,6},{3,7},{4,0},{5,1},{6,2},{7,3},{8,12},{9,13},{10,... | collective-permute-start | bytes 417800 | tf_op jit(solution)/shard_map/gather_images/ppermute | solution.py:406
  67.6 7.1 %collective-permute-start.3 = (bf16[272,256]{1,0:T(8,128)(2,1)S(1)}, bf16[272,256]{1,0:T(8,128)(2,1)S(1)}, u32[]{:S(2)}, u32[]{:S(2)}) collective-permute-start(bf16[272,256]{1,0:T(8,128)(2,1)S(1)} %collective-permute-done), channel_id=1, source_target_pairs={{0,6},{1,7},{2,0},{3,1},{4,2},{5,3},{6,4},{7,5},{8,14},{9,15},{10,... | collective-permute-start | bytes 417800 | tf_op jit(solution)/shard_map/gather_images/ppermute | solution.py:406
  74.7 1.2 copy-start.3
  119.7 10.6 %collective-permute-start.7 = (bf16[4,4,272,256]{3,2,1,0:T(8,128)(2,1)}, bf16[4,4,272,256]{3,2,1,0:T(8,128)(2,1)S(1)}, u32[]{:S(2)}, u32[]{:S(2)}) collective-permute-start(bf16[4,4,272,256]{3,2,1,0:T(8,128)(2,1)} %bitcast.21), channel_id=1, source_target_pairs={{0,1},{1,0},{2,3},{3,2},{4,5},{5,4},{6,7},{7,6},{8,9},{9,8},{10,11... | collective-permute-start | bytes 6684680 | tf_op jit(solution)/shard_map/gather_posteriors/ppermute | solution.py:422
  121.6 13.7 %collective-permute-start.4 = (bf16[4,128,256]{2,1,0:T(8,128)(2,1)S(1)}, bf16[4,128,256]{2,1,0:T(8,128)(2,1)S(1)}, u32[]{:S(2)}, u32[]{:S(2)}) collective-permute-start(bf16[4,128,256]{2,1,0:T(8,128)(2,1)S(1)} %bitcast.24), channel_id=1, source_target_pairs={{0,128},{32,160},{64,192},{96,224},{128,256},{160,288},{192,320},{... | collective-permute-start | bytes 786440 | tf_op jit(solution)/shard_map/gather_posteriors/ppermute | solution.py:420
  124.6 12.6 %collective-permute-start.5 = (bf16[4,128,256]{2,1,0:T(8,128)(2,1)S(1)}, bf16[4,128,256]{2,1,0:T(8,128)(2,1)S(1)}, u32[]{:S(2)}, u32[]{:S(2)}) collective-permute-start(bf16[4,128,256]{2,1,0:T(8,128)(2,1)S(1)} %bitcast.25), channel_id=1, source_target_pairs={{0,256},{32,288},{64,320},{96,352},{128,384},{160,416},{192,448},{... | collective-permute-start | bytes 786440 | tf_op jit(solution)/shard_map/gather_posteriors/ppermute | solution.py:420
  128.3 13.7 %collective-permute-start.6 = (bf16[4,128,256]{2,1,0:T(8,128)(2,1)S(1)}, bf16[4,128,256]{2,1,0:T(8,128)(2,1)S(1)}, u32[]{:S(2)}, u32[]{:S(2)}) collective-permute-start(bf16[4,128,256]{2,1,0:T(8,128)(2,1)S(1)} %bitcast.26), channel_id=1, source_target_pairs={{0,384},{32,416},{64,448},{96,480},{128,0},{160,32},{192,64},{224,... | collective-permute-start | bytes 786440 | tf_op jit(solution)/shard_map/gather_posteriors/ppermute | solution.py:420
  130.3 1.6 %copy-start = (bf16[16,272,256]{2,1,0:T(8,128)(2,1)S(1)}, bf16[16,272,256]{2,1,0:T(8,128)(2,1)}, u32[]{:S(2)}) copy-start(bf16[16,272,256]{2,1,0:T(8,128)(2,1)} %all-gather.9.cloned.1.call-done) | copy-start | bytes 6684676
  131.9 10.1 %copy-start.1 = (bf16[16,272,256]{2,1,0:T(8,128)(2,1)S(1)}, bf16[16,272,256]{2,1,0:T(8,128)(2,1)}, u32[]{:S(2)}) copy-start(bf16[16,272,256]{2,1,0:T(8,128)(2,1)} %all-gather.9.cloned.1.call-done) | copy-start | bytes 6684676
Sparse Core Ops, SparseCore 0:
  42.6 33.2 all-gather.6
  78.0 41.6 all-gather.8
